TPU v7x, 32 devices: a whole 2x2x4 slice. The times are simulated.
32 devices in a mesh: row: 8 (over z, y), col: 4 (over x, core).
Axes of the slice: x: 2, y: 2, z: 4, core: 2. Of those that a mesh axis runs over, the one named last changes fastest.
Arguments:
- image: bfloat16 [256, 128, 192], P('row', 'col'), may hold values from -6 to 6
- conv_weight: bfloat16 [3, 3, 192, 384], replicated, may hold values from -0.15625 to 0.15625
- conv_bias: float32 [384], replicated, may hold values from -3 to 3
- merge_gain: float32 [384], replicated, may hold values from 0.25 to 1.75
- merge_shift: float32 [384], replicated, may hold values from -3 to 3
- norm_gain: float32 [384], replicated, may hold values from 0.25 to 1.75
- norm_shift: float32 [384], replicated, may hold values from -3 to 3
- qkv_weight: bfloat16 [384, 1152], replicated, may hold values from -4 to 4
- proj_weight: bfloat16 [384, 384], replicated, may hold values from -0.3125 to 0.3125
- proj_bias: float32 [384], replicated, may hold values from -3 to 3
Outputs:
- block_out: bfloat16 [128, 64, 384], P('row', 'col')
All inputs are finite; a program needn't handle non-finite values.
Results may differ from a plain program's by a relative error of at most 0.02.
The roundings to bfloat16 on the way count: a program that leaves them out, or rounds other values in their place, can miss the bound.
Values may be sent and summed in bfloat16 or wider, within the bound.
No kernel may reach another device: no remote copies, remote signals or barrier semaphores. Data moves between devices by JAX's collectives and lax.ppermute only.
A program may use at most 128 MiB of HBM per device.

v0:
```python
import math

import jax
import jax.numpy as jnp
from jax import lax
from jax.experimental import pallas as pl
from jax.experimental.pallas import tpu as pltpu
from jax.sharding import PartitionSpec as P

HEADS = 16
SPLIT = 8
HALF = HEADS // 2
F32 = jnp.float32
BF16 = jnp.bfloat16
LANES = 128


def params():
    return pltpu.CompilerParams(vmem_limit_bytes=48 * 1024 * 1024)


def vmem(count):
    return [pl.BlockSpec(memory_space=pltpu.VMEM)] * count


def dot(left, right):
    return jnp.dot(left, right, preferred_element_type=F32)


def layer_norm(values, gain, shift):
    center = values - jnp.mean(values, -1, keepdims=True)
    spread = jnp.mean(center * center, -1, keepdims=True)
    return center * lax.rsqrt(spread + 1e-05) * gain + shift


def quadrants(rows, cols):
    return [(a, b) for a in range(rows // SPLIT) for b in range(cols // SPLIT)]


def merge_kernel(
    image, upper, left, corner, weight, bias, gain, shift, gain2, shift2, qkv, tokens, normed, chunks, pixels
):
    in_rows, in_cols, channels = image.shape
    rows, cols = in_rows // 2, in_cols // 2
    width = weight.shape[3]
    depth = width // HEADS
    first = SPLIT
    parts = [(k, k * LANES, min(LANES, channels - k * LANES)) for k in range(pixels.shape[0])]
    for part, start, size in parts:
        lanes = pl.ds(0, size)
        here = pl.ds(start, size)
        pixels[part, pl.ds(1, in_rows), pl.ds(first, in_cols), lanes] = image[:, :, here].astype(F32)
        pixels[part, 0, pl.ds(first, in_cols), lanes] = upper[0, :, here].astype(F32)
        pixels[part, 0, pl.ds(first - 1, 1), lanes] = corner[0, :, here].astype(F32)[in_cols - 1 :]
        beside = left[:, here].astype(F32)
        for i in range(in_rows):
            pixels[part, 1 + i, pl.ds(first - 1, 1), lanes] = beside[i : i + 1]
    merged = jnp.zeros((rows * cols, width), F32)
    for tap in range(3):
        pieces = []
        for part, start, size in parts:
            stack = [
                pixels[part, i, pl.ds(first - 1 + tap, cols, stride=2), :] for i in range(in_rows + 1)
            ]
            pieces.append((stack, size))
        for tap_row in range(3):
            window = jnp.concatenate(
                [
                    jnp.concatenate(stack[tap_row : tap_row + 2 * rows - 1 : 2], 0)[:, :size]
                    for stack, size in pieces
                ],
                1,
            ).astype(BF16)
            merged = merged + dot(window, weight[tap_row, tap])
    merged = (merged + bias[...]).reshape(rows, cols, width)
    merged = jnp.concatenate(
        [
            merged[a * SPLIT : (a + 1) * SPLIT, b * SPLIT : (b + 1) * SPLIT].reshape(SPLIT * SPLIT, width)
            for a, b in quadrants(rows, cols)
        ],
        0,
    )
    held = layer_norm(merged, gain[...], shift[...]).astype(BF16)
    tokens[...] = held
    again = layer_norm(held.astype(F32), gain2[...], shift2[...]).astype(BF16)
    normed[...] = again
    across = cols // SPLIT
    count = chunks.shape[0]
    per = across * HALF // count
    for b in range(across):
        mine = [
            again[(a * across + b) * SPLIT * SPLIT : (a * across + b + 1) * SPLIT * SPLIT]
            for a in range(rows // SPLIT)
        ]
        mine = jnp.concatenate(mine, 0)
        lines = []
        for kind in range(3):
            begin = kind * width + width // 2
            base = begin // LANES * LANES
            wide = dot(mine, qkv[:, base : (kind + 1) * width])
            lines.append(wide.T[begin - base :])
        for item in range(b * HALF, (b + 1) * HALF, per):
            low = (item - b * HALF) * depth
            chunks[item // per] = jnp.concatenate(
                [kind[low : low + per * depth] for kind in lines], 0
            ).astype(BF16)


def row_qkv_kernel(normed, qkv, queries, pairs):
    width = normed.shape[1]
    half = width // 2
    step = normed.shape[0] // queries.shape[0]
    for a in range(queries.shape[0]):
        mine = normed[a * step : (a + 1) * step]
        for kind in range(3):
            begin = kind * width
            end = begin + -(-half // LANES) * LANES
            lines = dot(mine, qkv[:, begin:end]).T[:half].astype(BF16)
            if kind == 0:
                queries[a] = lines
            else:
                pairs[a, (kind - 1) * half : kind * half] = lines


def padded_rows(values, start, total):
    size, lanes = values.shape
    pieces = []
    if start:
        pieces.append(jnp.zeros((start, lanes), F32))
    pieces.append(values)
    if total - start - size:
        pieces.append(jnp.zeros((total - start - size, lanes), F32))
    return jnp.concatenate(pieces, 0)


def with_sum_row(values):
    lanes = values.shape[1]
    return jnp.concatenate(
        [values, jnp.ones((1, lanes), F32), jnp.zeros((7, lanes), F32)], 0
    ).astype(BF16)


def weights_of(scores, depth):
    highest = jnp.max(scores, 0, keepdims=True)
    return jnp.exp2((scores - highest) * (math.log2(math.e) / math.sqrt(depth))).astype(BF16)


def col_attention_kernel(depth, arrived, result):
    count, lines, length = arrived.shape
    per = lines // (3 * depth)
    total = per * depth
    lanes = jnp.concatenate([arrived[s].astype(F32) for s in range(count)], 1)
    key_rows = lanes[total : 2 * total].T.astype(BF16)
    block = 2 * length
    outs = []
    for begin in range(0, count * length, block):
        heads = []
        for h in range(per):
            queries = padded_rows(lanes[h * depth : (h + 1) * depth, begin : begin + block], h * depth, total)
            scores = dot(key_rows, queries.astype(BF16))
            probs = weights_of(scores, depth)
            values = with_sum_row(lanes[2 * total + h * depth : 2 * total + (h + 1) * depth])
            mixed = dot(values, probs)
            heads.append(mixed[:depth] / mixed[depth : depth + 1])
        heads = jnp.concatenate(heads, 0).astype(BF16)
        for k in range(block // length):
            result[begin // length + k] = heads[:, k * length : (k + 1) * length]


def row_attention_kernel(count, queries, *refs):
    pairs = refs[:count]
    tokens, weight, bias, partial = refs[count:]
    stripes, half, length = queries.shape
    depth = half // HALF
    for a in range(stripes):
        both = jnp.concatenate([ref[a].astype(F32) for ref in pairs], 1)
        key_rows = both[:half].T.astype(BF16)
        lines = queries[a].astype(F32)
        heads = []
        for h in range(0, HALF, 2):
            wide = jnp.concatenate(
                [
                    padded_rows(lines[g * depth : (g + 1) * depth], g * depth, half)
                    for g in (h, h + 1)
                ],
                1,
            ).astype(BF16)
            probs = weights_of(dot(key_rows, wide), depth)
            for k, g in enumerate((h, h + 1)):
                values = with_sum_row(both[half + g * depth : half + (g + 1) * depth])
                mixed = dot(values, probs[:, k * length : (k + 1) * length])
                heads.append(mixed[:depth] / mixed[depth : depth + 1])
        attention = jnp.concatenate(heads, 0).T.astype(BF16)
        here = pl.ds(a * length, length)
        partial[here] = tokens[here].astype(F32) + dot(attention, weight[:half]) + bias[...]


def output_kernel(arrived, partial, weight, output):
    rows, cols, width = output.shape
    half = width // 2
    count = arrived.shape[0]
    across = cols // SPLIT
    down = rows // SPLIT
    square = SPLIT * SPLIT
    each = count // across
    blocks = {}
    for b in range(across):
        lines = jnp.concatenate([arrived[b * each + k].astype(F32) for k in range(each)], 0)
        mixed = dot(lines.T.astype(BF16), weight[half:])
        for a in range(down):
            here = pl.ds((a * across + b) * square, square)
            blocks[a, b] = (partial[here] + mixed[a * square : (a + 1) * square]).reshape(
                SPLIT, SPLIT, width
            )
    for a in range(down):
        output[a * SPLIT : (a + 1) * SPLIT] = jnp.concatenate(
            [blocks[a, b] for b in range(across)], 1
        ).astype(BF16)


def call(kernel, name, out_shape, args, flops, scratch=()):
    moved = sum(x.size * x.dtype.itemsize for x in args)
    return pl.pallas_call(
        kernel,
        out_shape=out_shape,
        in_specs=vmem(len(args)),
        out_specs=jax.tree.map(lambda _: pl.BlockSpec(memory_space=pltpu.VMEM), out_shape),
        scratch_shapes=scratch,
        compiler_params=params(),
        cost_estimate=pl.CostEstimate(flops=flops, bytes_accessed=moved, transcendentals=0),
        name=name,
    )(*args)


def shape(dims, dtype=BF16):
    return jax.ShapeDtypeStruct(dims, dtype)


def gathered(value, axis):
    held = [value]
    bit = lax.axis_size(axis) // 2
    while bit:
        pairs = [(k, k ^ bit) for k in range(lax.axis_size(axis))]
        held = held + [lax.ppermute(block, axis, pairs) for block in held]
        bit //= 2
    return held


def on_device(
    image,
    conv_weight,
    conv_bias,
    merge_gain,
    merge_shift,
    norm_gain,
    norm_shift,
    qkv_weight,
    proj_weight,
    proj_bias,
):
    in_rows, in_cols, channels = image.shape
    rows, cols = in_rows // 2, in_cols // 2
    width = conv_weight.shape[3]
    half = width // 2
    depth = width // HEADS
    row_count = lax.axis_size("row")
    col_count = lax.axis_size("col")
    down = [(k, k + 1) for k in range(row_count - 1)]
    right = [(k, k + 1) for k in range(col_count - 1)]
    upper = lax.ppermute(image[-1:], "row", down)
    left = lax.ppermute(image[:, -1], "col", right)
    corner = lax.ppermute(upper, "col", right)
    row = lambda value: value.reshape(1, width)
    stripes, across = rows // SPLIT, cols // SPLIT
    per = across * HALF // row_count
    lanes = rows * SPLIT
    tokens, normed, chunks = call(
        merge_kernel,
        "merge",
        (
            shape((rows * cols, width)),
            shape((rows * cols, width)),
            shape((row_count, 3 * per * depth, lanes)),
        ),
        (
            image,
            upper,
            left,
            corner,
            conv_weight,
            row(conv_bias),
            row(merge_gain),
            row(merge_shift),
            row(norm_gain),
            row(norm_shift),
            qkv_weight,
        ),
        10**9,
        [pltpu.VMEM((-(-channels // LANES), in_rows + 1, in_cols + SPLIT, LANES), F32)],
    )
    arrived = lax.all_to_all(chunks, "row", 0, 0, tiled=True)
    queries, pairs = call(
        row_qkv_kernel,
        "row_qkv",
        (shape((stripes, half, cols * SPLIT)), shape((stripes, width, cols * SPLIT))),
        (normed, qkv_weight),
        3 * 10**8,
    )
    held = gathered(pairs, "col")
    result = call(
        lambda *refs: col_attention_kernel(depth, *refs),
        "col_attention",
        shape((row_count, per * depth, lanes)),
        (arrived,),
        2 * 10**9,
    )
    back = lax.all_to_all(result, "row", 0, 0, tiled=True)
    partial = call(
        lambda *refs: row_attention_kernel(len(held), *refs),
        "row_attention",
        shape((rows * cols, width), F32),
        (queries, *held, tokens, proj_weight, row(proj_bias)),
        2 * 10**9,
    )
    return call(
        output_kernel,
        "output",
        shape((rows, cols, width)),
        (back, partial, proj_weight),
        10**8,
    )


def solution(mesh):
    return jax.shard_map(
        on_device,
        mesh=mesh,
        in_specs=(P("row", "col", None), P(), P(), P(), P(), P(), P(), P(), P(), P()),
        out_specs=P("row", "col", None),
        check_vma=False,
    )
```

profile of v0, /device:TPU:0, one launch (start us, length us, event | category | flops | bytes accessed | tf_op | source)
XLA Modules:
  0.0 54.2 jit_solution(15921917691639061880)
XLA Ops:
  0.0 0.7 %slice.6 = bf16[1,32,192]{2,1,0:T(8,128)(2,1)S(1)} slice(bf16[32,32,192]{2,1,0:T(8,128)(2,1)} %image.1), slice={[31:32], [0:32], [0:192]} | slice | bytes 24576 | tf_op jit(solution)/shard_map/slice | solution.py:270
  0.7 4.9 %collective-permute-start = (bf16[1,32,192]{2,1,0:T(8,128)(2,1)S(1)}, bf16[1,32,192]{2,1,0:T(8,128)(2,1)S(1)}, u32[]{:S(2)}, u32[]{:S(2)}) collective-permute-start(bf16[1,32,192]{2,1,0:T(8,128)(2,1)S(1)} %slice.6), channel_id=1, source_target_pairs={{0,4},{4,8},{8,12},{12,16},{16,20},{20,24},{24,28},{1,5},{5,9},{9,... | collective-permute-start | bytes 36872 | tf_op jit(solution)/shard_map/ppermute | solution.py:270
  5.6 0.9 %slice.7 = bf16[32,1,192]{2,1,0:T(2,128)(2,1)S(1)} slice(bf16[32,32,192]{2,1,0:T(8,128)(2,1)} %image.1), slice={[0:32], [31:32], [0:192]} | slice | bytes 24576 | tf_op jit(solution)/shard_map/slice | solution.py:271
  6.5 1.5 %collective-permute-start.1 = (bf16[32,192]{1,0:T(8,128)(2,1)S(1)}, bf16[32,192]{1,0:T(8,128)(2,1)S(1)}, u32[]{:S(2)}, u32[]{:S(2)}) collective-permute-start(bf16[32,192]{1,0:T(8,128)(2,1)S(1)} %bitcast.3), channel_id=1, source_target_pairs={{0,1},{1,2},{2,3},{4,5},{5,6},{6,7},{8,9},{9,10},{10,11},{12,13},{... | collective-permute-start | bytes 36872 | tf_op jit(solution)/shard_map/ppermute | solution.py:271
  8.0 0.0 collective-permute-done.upper
  8.0 4.0 %collective-permute-start.2 = (bf16[1,32,192]{2,1,0:T(8,128)(2,1)S(1)}, bf16[1,32,192]{2,1,0:T(8,128)(2,1)S(1)}, u32[]{:S(2)}, u32[]{:S(2)}) collective-permute-start(bf16[1,32,192]{2,1,0:T(8,128)(2,1)S(1)} %collective-permute-done.upper), channel_id=1, source_target_pairs={{0,1},{1,2},{2,3},{4,5},{5,6},{6,7},{8,9},{9,10},{10,11},{12,13},{... | collective-permute-start | bytes 36872 | tf_op jit(solution)/shard_map/ppermute | solution.py:272
  12.0 0.7 %reshape.18.bias = f32[1,384]{1,0:T(1,128)S(1)} reshape(f32[384]{0:T(512)} %param.12) | data formatting | bytes 3072 | tf_op jit(solution)/shard_map/reshape | solution.py:273
  12.7 0.7 %reshape.19.gain = f32[1,384]{1,0:T(1,128)S(1)} reshape(f32[384]{0:T(512)} %param.13) | data formatting | bytes 3072 | tf_op jit(solution)/shard_map/reshape | solution.py:273
  13.4 0.7 %reshape.20.shift = f32[1,384]{1,0:T(1,128)S(1)} reshape(f32[384]{0:T(512)} %param.14) | data formatting | bytes 3072 | tf_op jit(solution)/shard_map/reshape | solution.py:273
  14.0 0.7 %reshape.21.gain2 = f32[1,384]{1,0:T(1,128)S(1)} reshape(f32[384]{0:T(512)} %param.15) | data formatting | bytes 3072 | tf_op jit(solution)/shard_map/reshape | solution.py:273
  14.7 0.7 %reshape.22.shift2 = f32[1,384]{1,0:T(1,128)S(1)} reshape(f32[384]{0:T(512)} %param.16) | data formatting | bytes 3072 | tf_op jit(solution)/shard_map/reshape | solution.py:273
  15.4 0.0 collective-permute-done.1.left
  15.4 0.0 collective-permute-done.2.corner
  15.4 1.0 %copy-done.1 = bf16[32,32,192]{2,1,0:T(8,128)(2,1)S(1)} copy-done((bf16[32,32,192]{2,1,0:T(8,128)(2,1)S(1)}, bf16[32,32,192]{2,1,0:T(8,128)(2,1)}, u32[]{:S(2)}) %copy-start.1) | copy-done | bytes 393240
  16.5 1.3 %copy-done.2 = bf16[3,3,192,384]{3,2,1,0:T(8,128)(2,1)S(1)} copy-done((bf16[3,3,192,384]{3,2,1,0:T(8,128)(2,1)S(1)}, bf16[3,3,192,384]{3,2,1,0:T(8,128)(2,1)}, u32[]{:S(2)}) %copy-start.2) | copy-done | bytes 1327128
  17.8 1.2 %copy-done.3 = bf16[384,1152]{1,0:T(8,128)(2,1)S(1)} copy-done((bf16[384,1152]{1,0:T(8,128)(2,1)S(1)}, bf16[384,1152]{1,0:T(8,128)(2,1)}, u32[]{:S(2)}) %copy-start.3) | copy-done | bytes 884760
  19.0 2.2 %merge.1 = (bf16[256,384]{1,0:T(8,128)(2,1)S(1)}, bf16[256,384]{1,0:T(8,128)(2,1)S(1)}, bf16[8,144,128]{2,1,0:T(8,128)(2,1)}) custom-call(bf16[32,32,192]{2,1,0:T(8,128)(2,1)S(1)} %copy-done.1, bf16[1,32,192]{2,1,0:T(8,128)(2,1)S(1)} %collective-permute-done.upper, bf16[32,192]{1,0:T(8,128)(2,1)S(1)} %collective-permute-done.1.left, ...), custom_call_target="tpu_custom_call" | custom-call | flops 1000000000 | bytes 2649600 | tf_op jit(solution)/shard_map/merge/pallas_call | solution.py:223
  21.2 5.0 %all-to-all-start = ((bf16[8,144,128]{2,1,0:T(8,128)(2,1)}), bf16[8,144,128]{2,1,0:T(8,128)(2,1)S(1)}, u32[]{:S(2)}, u32[]{:S(2)}) async-start(bf16[8,144,128]{2,1,0:T(8,128)(2,1)} %get-tuple-element.10), calls=%async_computation | async-start | bytes 589824 | tf_op jit(solution)/shard_map/all_to_all | solution.py:301
  26.2 0.4 row_qkv.1
  26.7 0.2 collective-permute-start.3
  26.9 0.0 collective-permute-start.4
  26.9 6.6 %collective-permute-done.3.refs_2_ = bf16[2,384,128]{2,1,0:T(8,128)(2,1)S(1)} collective-permute-done((bf16[2,384,128]{2,1,0:T(8,128)(2,1)S(1)}, bf16[2,384,128]{2,1,0:T(8,128)(2,1)S(1)}, u32[]{:S(2)}, u32[]{:S(2)}) %collective-permute-start.3) | collective-permute-done | bytes 196640 | tf_op jit(solution)/shard_map/ppermute | solution.py:244
  33.5 0.0 collective-permute-start.5
  33.5 0.0 copy-start
  33.5 2.7 %all-to-all-done.refs_0_ = bf16[8,144,128]{2,1,0:T(8,128)(2,1)S(1)} async-done(((bf16[8,144,128]{2,1,0:T(8,128)(2,1)}), bf16[8,144,128]{2,1,0:T(8,128)(2,1)S(1)}, u32[]{:S(2)}, u32[]{:S(2)}) %all-to-all-start) | async-done | bytes 294944 | tf_op jit(solution)/shard_map/all_to_all | solution.py:301
  36.2 6.3 %col_attention.1 = bf16[8,48,128]{2,1,0:T(8,128)(2,1)} custom-call(bf16[8,144,128]{2,1,0:T(8,128)(2,1)S(1)} %all-to-all-done.refs_0_), custom_call_target="tpu_custom_call" | custom-call | flops 2000000000 | bytes 294912 | tf_op jit(solution)/shard_map/col_attention/pallas_call | solution.py:223
  42.5 3.6 %all-to-all-start.1 = ((bf16[8,48,128]{2,1,0:T(8,128)(2,1)}), bf16[8,48,128]{2,1,0:T(8,128)(2,1)S(1)}, u32[]{:S(2)}, u32[]{:S(2)}) async-start(bf16[8,48,128]{2,1,0:T(8,128)(2,1)} %col_attention.1), calls=%async_computation.1 | async-start | bytes 196608 | tf_op jit(solution)/shard_map/all_to_all | solution.py:317
  46.1 0.0 collective-permute-done.4.refs_3_
  46.1 0.0 collective-permute-done.5.refs_4_
  46.1 3.5 %row_attention.1.partial = f32[256,384]{1,0:T(8,128)S(1)} custom-call(bf16[2,192,128]{2,1,0:T(8,128)(2,1)S(1)} %get-tuple-element.12.refs_0_, bf16[2,384,128]{2,1,0:T(8,128)(2,1)S(1)} %get-tuple-element.13.refs_1_, bf16[2,384,128]{2,1,0:T(8,128)(2,1)S(1)} %collective-permute-done.3.refs_2_, bf16[2,384,128]{2,1,0:T(8,128)(2,1)S(1)} %collective-permute-done.4.refs_3_, ...), custom_call_target="tpu_custom_call" | custom-call | flops 2000000000 | bytes 1377792 | tf_op jit(solution)/shard_map/row_attention/pallas_call | solution.py:223
  49.7 3.6 %all-to-all-done.1.arrived = bf16[8,48,128]{2,1,0:T(8,128)(2,1)S(1)} async-done(((bf16[8,48,128]{2,1,0:T(8,128)(2,1)}), bf16[8,48,128]{2,1,0:T(8,128)(2,1)S(1)}, u32[]{:S(2)}, u32[]{:S(2)}) %all-to-all-start.1) | async-done | bytes 98336 | tf_op jit(solution)/shard_map/all_to_all | solution.py:317
  53.2 1.0 %output.1 = bf16[16,16,384]{2,1,0:T(8,128)(2,1)} custom-call(bf16[8,48,128]{2,1,0:T(8,128)(2,1)S(1)} %all-to-all-done.1.arrived, f32[256,384]{1,0:T(8,128)S(1)} %row_attention.1.partial, bf16[384,384]{1,0:T(8,128)(2,1)S(1)} %copy-done), custom_call_target="tpu_custom_call" | custom-call | flops 100000000 | bytes 786432 | tf_op jit(solution)/shard_map/output/pallas_call | solution.py:223
  (10 shorter events, 0.0 us)
Async XLA Ops:
  0.7 7.3 %collective-permute-start = (bf16[1,32,192]{2,1,0:T(8,128)(2,1)S(1)}, bf16[1,32,192]{2,1,0:T(8,128)(2,1)S(1)}, u32[]{:S(2)}, u32[]{:S(2)}) collective-permute-start(bf16[1,32,192]{2,1,0:T(8,128)(2,1)S(1)} %slice.6), channel_id=1, source_target_pairs={{0,4},{4,8},{8,12},{12,16},{16,20},{20,24},{24,28},{1,5},{5,9},{9,... | collective-permute-start | bytes 36872 | tf_op jit(solution)/shard_map/ppermute | solution.py:270
  6.5 8.9 %collective-permute-start.1 = (bf16[32,192]{1,0:T(8,128)(2,1)S(1)}, bf16[32,192]{1,0:T(8,128)(2,1)S(1)}, u32[]{:S(2)}, u32[]{:S(2)}) collective-permute-start(bf16[32,192]{1,0:T(8,128)(2,1)S(1)} %bitcast.3), channel_id=1, source_target_pairs={{0,1},{1,2},{2,3},{4,5},{5,6},{6,7},{8,9},{9,10},{10,11},{12,13},{... | collective-permute-start | bytes 36872 | tf_op jit(solution)/shard_map/ppermute | solution.py:271
  8.0 7.4 %collective-permute-start.2 = (bf16[1,32,192]{2,1,0:T(8,128)(2,1)S(1)}, bf16[1,32,192]{2,1,0:T(8,128)(2,1)S(1)}, u32[]{:S(2)}, u32[]{:S(2)}) collective-permute-start(bf16[1,32,192]{2,1,0:T(8,128)(2,1)S(1)} %collective-permute-done.upper), channel_id=1, source_target_pairs={{0,1},{1,2},{2,3},{4,5},{5,6},{6,7},{8,9},{9,10},{10,11},{12,13},{... | collective-permute-start | bytes 36872 | tf_op jit(solution)/shard_map/ppermute | solution.py:272
  15.4 1.0 %copy-start.1 = (bf16[32,32,192]{2,1,0:T(8,128)(2,1)S(1)}, bf16[32,32,192]{2,1,0:T(8,128)(2,1)}, u32[]{:S(2)}) copy-start(bf16[32,32,192]{2,1,0:T(8,128)(2,1)} %image.1) | copy-start | bytes 1179652
  16.5 1.3 %copy-start.2 = (bf16[3,3,192,384]{3,2,1,0:T(8,128)(2,1)S(1)}, bf16[3,3,192,384]{3,2,1,0:T(8,128)(2,1)}, u32[]{:S(2)}) copy-start(bf16[3,3,192,384]{3,2,1,0:T(8,128)(2,1)} %weight.2) | copy-start | bytes 3981316
  17.8 1.2 %copy-start.3 = (bf16[384,1152]{1,0:T(8,128)(2,1)S(1)}, bf16[384,1152]{1,0:T(8,128)(2,1)}, u32[]{:S(2)}) copy-start(bf16[384,1152]{1,0:T(8,128)(2,1)} %qkv.3) | copy-start | bytes 2654212
  19.0 7.3 %copy-start.4 = (bf16[384,1152]{1,0:T(8,128)(2,1)S(1)}, bf16[384,1152]{1,0:T(8,128)(2,1)}, u32[]{:S(2)}) copy-start(bf16[384,1152]{1,0:T(8,128)(2,1)} %qkv.3) | copy-start | bytes 2654212
  21.2 12.3 %copy-start.5 = (f32[384]{0:T(512)S(1)}, f32[384]{0:T(512)}, u32[]{:S(2)}) copy-start(f32[384]{0:T(512)} %param.19) | copy-start | bytes 4612
  21.2 15.0 %all-to-all-start = ((bf16[8,144,128]{2,1,0:T(8,128)(2,1)}), bf16[8,144,128]{2,1,0:T(8,128)(2,1)S(1)}, u32[]{:S(2)}, u32[]{:S(2)}) async-start(bf16[8,144,128]{2,1,0:T(8,128)(2,1)} %get-tuple-element.10), calls=%async_computation | async-start | bytes 589824 | tf_op jit(solution)/shard_map/all_to_all | solution.py:301
  26.7 6.8 %collective-permute-start.3 = (bf16[2,384,128]{2,1,0:T(8,128)(2,1)S(1)}, bf16[2,384,128]{2,1,0:T(8,128)(2,1)S(1)}, u32[]{:S(2)}, u32[]{:S(2)}) collective-permute-start(bf16[2,384,128]{2,1,0:T(8,128)(2,1)S(1)} %get-tuple-element.13.refs_1_), channel_id=1, source_target_pairs={{0,2},{1,3},{2,0},{3,1},{4,6},{5,7},{6,4},{7,5},{8,10},{9,11},{10,... | collective-permute-start | bytes 589832 | tf_op jit(solution)/shard_map/ppermute | solution.py:244
  26.9 19.2 %collective-permute-start.4 = (bf16[2,384,128]{2,1,0:T(8,128)(2,1)S(1)}, bf16[2,384,128]{2,1,0:T(8,128)(2,1)S(1)}, u32[]{:S(2)}, u32[]{:S(2)}) collective-permute-start(bf16[2,384,128]{2,1,0:T(8,128)(2,1)S(1)} %get-tuple-element.13.refs_1_), channel_id=1, source_target_pairs={{0,1},{1,0},{2,3},{3,2},{4,5},{5,4},{6,7},{7,6},{8,9},{9,8},{10,11... | collective-permute-start | bytes 589832 | tf_op jit(solution)/shard_map/ppermute | solution.py:244
  33.5 12.6 %collective-permute-start.5 = (bf16[2,384,128]{2,1,0:T(8,128)(2,1)S(1)}, bf16[2,384,128]{2,1,0:T(8,128)(2,1)S(1)}, u32[]{:S(2)}, u32[]{:S(2)}) collective-permute-start(bf16[2,384,128]{2,1,0:T(8,128)(2,1)S(1)} %collective-permute-done.3.refs_2_), channel_id=1, source_target_pairs={{0,1},{1,0},{2,3},{3,2},{4,5},{5,4},{6,7},{7,6},{8,9},{9,8},{10,11... | collective-permute-start | bytes 589832 | tf_op jit(solution)/shard_map/ppermute | solution.py:244
  33.5 12.6 %copy-start = (bf16[384,384]{1,0:T(8,128)(2,1)S(1)}, bf16[384,384]{1,0:T(8,128)(2,1)}, u32[]{:S(2)}) copy-start(bf16[384,384]{1,0:T(8,128)(2,1)} %weight.3) | copy-start | bytes 884740
  42.5 10.8 %all-to-all-start.1 = ((bf16[8,48,128]{2,1,0:T(8,128)(2,1)}), bf16[8,48,128]{2,1,0:T(8,128)(2,1)S(1)}, u32[]{:S(2)}, u32[]{:S(2)}) async-start(bf16[8,48,128]{2,1,0:T(8,128)(2,1)} %col_attention.1), calls=%async_computation.1 | async-start | bytes 196608 | tf_op jit(solution)/shard_map/all_to_all | solution.py:317
where the time goes:
time: 54.9 us; the launch traced here: 54.2 us
  starting transfers between devices  19.2 us (35%)
  Pallas kernels  13.4 us (24%)
  waiting for transfers between devices  12.9 us (23%)
  local copies, waits for them, and re-layouts  8.63 us (16%)
    pallas_call x5, Pallas kernels, call(): pl.pallas_call(kernel, out_shape=out_shape, in_specs=vmem(len(args)), out...  13.4 us
    ppermute x3, waiting for transfers between devices, gathered(): held = held + [lax.ppermute(block, axis, pairs) for block in held]  6.63 us
    all_to_all x1, starting transfers between devices, on_device(): arrived = lax.all_to_all(chunks, 'row', 0, 0, tiled=True)  5.01 us
    ppermute x1, starting transfers between devices, on_device(): upper = lax.ppermute(image[-1:], 'row', down)  4.86 us
    ppermute x1, starting transfers between devices, on_device(): corner = lax.ppermute(upper, 'col', right)  3.96 us
    all_to_all x1, starting transfers between devices, on_device(): back = lax.all_to_all(result, 'row', 0, 0, tiled=True)  3.64 us
    all_to_all x1, waiting for transfers between devices, on_device(): back = lax.all_to_all(result, 'row', 0, 0, tiled=True)  3.56 us
    unnamed x13, local copies, waits for them, and re-layouts  3.55 us
  transfers between devices with their start and end apart: 8, of which 3 were waited for; matrix products, arithmetic and copies ran while one was open for 8% of the time, Pallas kernels for 19%

commit v1 on v0

--- a/solution.py
+++ b/solution.py
@@ -37,60 +37,98 @@
     return [(a, b) for a in range(rows // SPLIT) for b in range(cols // SPLIT)]
 
 
+def lane_parts(channels):
+    return [(k, k * LANES, min(LANES, channels - k * LANES)) for k in range(-(-channels // LANES))]
+
+
+def every_second(ref, index, first, count, channels):
+    return jnp.concatenate(
+        [ref[(part, *index, pl.ds(first, count, stride=2))][:, :size] for part, _, size in lane_parts(channels)],
+        1,
+    )
+
+
+def edge_kernel(image, bottom, side):
+    rows, cols, _ = image.shape
+    bottom[...] = image[rows - 1 :]
+    side[...] = image[:, cols - 2 * SPLIT :].astype(F32)[:, 2 * SPLIT - 1].astype(BF16)
+
+
+def join_kernel(side, upper, joined):
+    size = side.shape[0]
+    extra = joined.shape[0] - size
+    joined[:size] = side[...]
+    joined[size:] = upper[0, upper.shape[1] - extra :]
+
+
+def own_kernel(image, weight, merged, pixels):
+    in_rows, in_cols, channels = image.shape
+    rows, cols = in_rows // 2, in_cols // 2
+    first = SPLIT
+    pixels[:, 0] = jnp.zeros(pixels.shape[:1] + pixels.shape[2:], F32)
+    pixels[:, :, :first] = jnp.zeros(pixels.shape[:2] + (first, LANES), F32)
+    for part, start, size in lane_parts(channels):
+        pixels[part, pl.ds(1, in_rows), pl.ds(first, in_cols), pl.ds(0, size)] = image[
+            :, :, pl.ds(start, size)
+        ].astype(F32)
+    total = jnp.zeros((rows * cols, merged.shape[1]), F32)
+    for tap in range(3):
+        lines = [
+            every_second(pixels, (i,), first - 1 + tap, cols, channels).astype(BF16)
+            for i in range(in_rows + 1)
+        ]
+        for tap_row in range(3):
+            window = jnp.concatenate(lines[tap_row : tap_row + 2 * rows - 1 : 2], 0)
+            total = total + dot(window, weight[tap_row, tap])
+    merged[...] = total
+
+
 def merge_kernel(
-    image, upper, left, corner, weight, bias, gain, shift, gain2, shift2, qkv, tokens, normed, chunks, pixels
+    merged, upper, joined, weight, qkv, bias, gain, shift, gain2, shift2, tokens, normed, chunks, edges
 ):
-    in_rows, in_cols, channels = image.shape
+    in_cols, channels = upper.shape[1:]
+    in_rows = 2 * merged.shape[0] // (in_cols // 2)
     rows, cols = in_rows // 2, in_cols // 2
     width = weight.shape[3]
     depth = width // HEADS
     first = SPLIT
-    parts = [(k, k * LANES, min(LANES, channels - k * LANES)) for k in range(pixels.shape[0])]
-    for part, start, size in parts:
-        lanes = pl.ds(0, size)
-        here = pl.ds(start, size)
-        pixels[part, pl.ds(1, in_rows), pl.ds(first, in_cols), lanes] = image[:, :, here].astype(F32)
-        pixels[part, 0, pl.ds(first, in_cols), lanes] = upper[0, :, here].astype(F32)
-        pixels[part, 0, pl.ds(first - 1, 1), lanes] = corner[0, :, here].astype(F32)[in_cols - 1 :]
-        beside = left[:, here].astype(F32)
-        for i in range(in_rows):
-            pixels[part, 1 + i, pl.ds(first - 1, 1), lanes] = beside[i : i + 1]
-    merged = jnp.zeros((rows * cols, width), F32)
-    for tap in range(3):
-        pieces = []
-        for part, start, size in parts:
-            stack = [
-                pixels[part, i, pl.ds(first - 1 + tap, cols, stride=2), :] for i in range(in_rows + 1)
-            ]
-            pieces.append((stack, size))
-        for tap_row in range(3):
-            window = jnp.concatenate(
-                [
-                    jnp.concatenate(stack[tap_row : tap_row + 2 * rows - 1 : 2], 0)[:, :size]
-                    for stack, size in pieces
-                ],
-                1,
-            ).astype(BF16)
-            merged = merged + dot(window, weight[tap_row, tap])
-    merged = (merged + bias[...]).reshape(rows, cols, width)
-    merged = jnp.concatenate(
+    row = lambda ref: ref[...].reshape(1, width)
+    for part, start, size in lane_parts(channels):
+        lanes, here = pl.ds(0, size), pl.ds(start, size)
+        beside = joined[:, here].astype(F32)
+        edges[part, 0, pl.ds(first, in_cols), lanes] = upper[0, :, here].astype(F32)
+        edges[part, 0, pl.ds(first - 1, 1), lanes] = beside[beside.shape[0] - 1 :]
+        edges[part, 1, pl.ds(first, in_rows), lanes] = beside[:in_rows]
+        edges[part, 1, pl.ds(first - 1, 1), lanes] = jnp.zeros((1, size), F32)
+    above = [every_second(edges, (0,), first - 1 + tap, cols, channels).astype(BF16) for tap in range(3)]
+    aside = [every_second(edges, (1,), first - 1 + tap, rows, channels).astype(BF16) for tap in range(3)]
+    corner = dot(jnp.concatenate([above[0], aside[0]], 0), weight[0, 0])
+    top = corner[:cols] + dot(above[1], weight[0, 1]) + dot(above[2], weight[0, 2])
+    near = corner[cols:] + dot(aside[1], weight[1, 0]) + dot(aside[2], weight[2, 0])
+    grid = merged[...].reshape(rows, cols, width)
+    grid = jnp.concatenate([grid[:1] + top.reshape(1, cols, width), grid[1:]], 0)
+    begin = lax.broadcasted_iota(jnp.int32, (rows, SPLIT, width), 1) == 0
+    grid = jnp.concatenate(
+        [grid[:, :SPLIT] + jnp.where(begin, near.reshape(rows, 1, width), 0.0), grid[:, SPLIT:]], 1
+    )
+    grid = jnp.concatenate(
         [
-            merged[a * SPLIT : (a + 1) * SPLIT, b * SPLIT : (b + 1) * SPLIT].reshape(SPLIT * SPLIT, width)
+            grid[a * SPLIT : (a + 1) * SPLIT, b * SPLIT : (b + 1) * SPLIT].reshape(SPLIT * SPLIT, width)
             for a, b in quadrants(rows, cols)
         ],
         0,
     )
-    held = layer_norm(merged, gain[...], shift[...]).astype(BF16)
+    held = layer_norm(grid + row(bias), row(gain), row(shift)).astype(BF16)
     tokens[...] = held
-    again = layer_norm(held.astype(F32), gain2[...], shift2[...]).astype(BF16)
+    again = layer_norm(held.astype(F32), row(gain2), row(shift2)).astype(BF16)
     normed[...] = again
     across = cols // SPLIT
     count = chunks.shape[0]
     per = across * HALF // count
+    square = SPLIT * SPLIT
     for b in range(across):
         mine = [
-            again[(a * across + b) * SPLIT * SPLIT : (a * across + b + 1) * SPLIT * SPLIT]
-            for a in range(rows // SPLIT)
+            again[(a * across + b) * square : (a * across + b + 1) * square] for a in range(rows // SPLIT)
         ]
         mine = jnp.concatenate(mine, 0)
         lines = []
@@ -140,9 +178,20 @@
     ).astype(BF16)
 
 
-def weights_of(scores, depth):
-    highest = jnp.max(scores, 0, keepdims=True)
+def weights_of(scores, highest, depth):
     return jnp.exp2((scores - highest) * (math.log2(math.e) / math.sqrt(depth))).astype(BF16)
+
+
+def ahead_of(items, score, finish, ahead):
+    waiting = [score(item) for item in items[:ahead]]
+    for k, item in enumerate(items):
+        if k + ahead < len(items):
+            waiting.append(score(items[k + ahead]))
+        finish(item, *waiting.pop(0))
+
+
+def attended(mixed, depth):
+    return mixed[:depth] / mixed[depth : depth + 1]
 
 
 def col_attention_kernel(depth, arrived, result):
@@ -151,18 +200,25 @@
     total = per * depth
     lanes = jnp.concatenate([arrived[s].astype(F32) for s in range(count)], 1)
     key_rows = lanes[total : 2 * total].T.astype(BF16)
-    block = 2 * length
-    outs = []
-    for begin in range(0, count * length, block):
-        heads = []
-        for h in range(per):
-            queries = padded_rows(lanes[h * depth : (h + 1) * depth, begin : begin + block], h * depth, total)
-            scores = dot(key_rows, queries.astype(BF16))
-            probs = weights_of(scores, depth)
-            values = with_sum_row(lanes[2 * total + h * depth : 2 * total + (h + 1) * depth])
-            mixed = dot(values, probs)
-            heads.append(mixed[:depth] / mixed[depth : depth + 1])
-        heads = jnp.concatenate(heads, 0).astype(BF16)
+    values = [
+        with_sum_row(lanes[2 * total + h * depth : 2 * total + (h + 1) * depth]) for h in range(per)
+    ]
+    block = 4 * length
+    done = {}
+
+    def score(item):
+        begin, h = item
+        queries = padded_rows(lanes[h * depth : (h + 1) * depth, begin : begin + block], h * depth, total)
+        scores = dot(key_rows, queries.astype(BF16))
+        return scores, jnp.max(scores, 0, keepdims=True)
+
+    def finish(item, scores, highest):
+        done[item] = attended(dot(values[item[1]], weights_of(scores, highest, depth)), depth)
+
+    starts = range(0, count * length, block)
+    ahead_of([(begin, h) for begin in starts for h in range(per)], score, finish, 1)
+    for begin in starts:
+        heads = jnp.concatenate([done[begin, h] for h in range(per)], 0).astype(BF16)
         for k in range(block // length):
             result[begin // length + k] = heads[:, k * length : (k + 1) * length]
 
@@ -172,27 +228,38 @@
     tokens, weight, bias, partial = refs[count:]
     stripes, half, length = queries.shape
     depth = half // HALF
+    together = 2
+    both, key_rows, lines, done = [], [], [], {}
     for a in range(stripes):
-        both = jnp.concatenate([ref[a].astype(F32) for ref in pairs], 1)
-        key_rows = both[:half].T.astype(BF16)
-        lines = queries[a].astype(F32)
-        heads = []
-        for h in range(0, HALF, 2):
-            wide = jnp.concatenate(
-                [
-                    padded_rows(lines[g * depth : (g + 1) * depth], g * depth, half)
-                    for g in (h, h + 1)
-                ],
-                1,
-            ).astype(BF16)
-            probs = weights_of(dot(key_rows, wide), depth)
-            for k, g in enumerate((h, h + 1)):
-                values = with_sum_row(both[half + g * depth : half + (g + 1) * depth])
-                mixed = dot(values, probs[:, k * length : (k + 1) * length])
-                heads.append(mixed[:depth] / mixed[depth : depth + 1])
-        attention = jnp.concatenate(heads, 0).T.astype(BF16)
+        both.append(jnp.concatenate([ref[a].astype(F32) for ref in pairs], 1))
+        key_rows.append(both[a][:half].T.astype(BF16))
+        lines.append(queries[a].astype(F32))
+
+    def score(item):
+        a, h = item
+        wide = [
+            padded_rows(lines[a][g * depth : (g + 1) * depth], g * depth, half)
+            for g in range(h, h + together)
+        ]
+        scores = dot(key_rows[a], jnp.concatenate(wide, 1).astype(BF16))
+        return scores, jnp.max(scores, 0, keepdims=True)
+
+    def finish(item, scores, highest):
+        a, h = item
+        probs = weights_of(scores, highest, depth)
+        for k in range(together):
+            g = h + k
+            values = with_sum_row(both[a][half + g * depth : half + (g + 1) * depth])
+            done[a, g] = attended(dot(values, probs[:, k * length : (k + 1) * length]), depth)
+
+    items = [(a, h) for a in range(stripes) for h in range(0, HALF, together)]
+    ahead_of(items, score, finish, 2)
+    for a in range(stripes):
+        attention = jnp.concatenate([done[a, g] for g in range(HALF)], 0).T.astype(BF16)
         here = pl.ds(a * length, length)
-        partial[here] = tokens[here].astype(F32) + dot(attention, weight[:half]) + bias[...]
+        partial[here] = (
+            tokens[here].astype(F32) + dot(attention, weight[:half]) + bias[...].reshape(1, 2 * half)
+        )
 
 
 def output_kernel(arrived, partial, weight, output):
@@ -267,10 +334,28 @@
     col_count = lax.axis_size("col")
     down = [(k, k + 1) for k in range(row_count - 1)]
     right = [(k, k + 1) for k in range(col_count - 1)]
-    upper = lax.ppermute(image[-1:], "row", down)
-    left = lax.ppermute(image[:, -1], "col", right)
-    corner = lax.ppermute(upper, "col", right)
-    row = lambda value: value.reshape(1, width)
+    near = 2 * SPLIT
+    bottom, side = call(
+        edge_kernel,
+        "edge",
+        (shape((1, in_cols, channels)), shape((in_rows, channels))),
+        (image,),
+        10**10,
+    )
+    upper = lax.ppermute(bottom, "row", down)
+    pixel_parts = -(-channels // LANES)
+    merged = call(
+        own_kernel,
+        "own_tile",
+        shape((rows * cols, width), F32),
+        (image, conv_weight),
+        10**9,
+        [pltpu.VMEM((pixel_parts, in_rows + 1, in_cols + SPLIT, LANES), F32)],
+    )
+    joined = call(
+        join_kernel, "join", shape((in_rows + near, channels)), (side, upper), 10**5
+    )
+    joined = lax.ppermute(joined, "col", right)
     stripes, across = rows // SPLIT, cols // SPLIT
     per = across * HALF // row_count
     lanes = rows * SPLIT
@@ -283,20 +368,19 @@
             shape((row_count, 3 * per * depth, lanes)),
         ),
         (
-            image,
+            merged,
             upper,
-            left,
-            corner,
+            joined,
             conv_weight,
-            row(conv_bias),
-            row(merge_gain),
-            row(merge_shift),
-            row(norm_gain),
-            row(norm_shift),
             qkv_weight,
+            conv_bias,
+            merge_gain,
+            merge_shift,
+            norm_gain,
+            norm_shift,
         ),
-        10**9,
-        [pltpu.VMEM((-(-channels // LANES), in_rows + 1, in_cols + SPLIT, LANES), F32)],
+        5 * 10**8,
+        [pltpu.VMEM((pixel_parts, 2, max(in_rows, in_cols) + SPLIT, LANES), F32)],
     )
     arrived = lax.all_to_all(chunks, "row", 0, 0, tiled=True)
     queries, pairs = call(
@@ -319,7 +403,7 @@
         lambda *refs: row_attention_kernel(len(held), *refs),
         "row_attention",
         shape((rows * cols, width), F32),
-        (queries, *held, tokens, proj_weight, row(proj_bias)),
+        (queries, *held, tokens, proj_weight, proj_bias),
         2 * 10**9,
     )
     return call(

time: 54.9 us -> 45.4 us (0.83)
  local copies, waits for them, and re-layouts: 8.63 us -> 1.19 us
  starting transfers between devices: 19.2 us -> 23.2 us
  Pallas kernels: 13.4 us -> 9.48 us
  waiting for transfers between devices: 12.9 us -> 11 us
    ppermute x3, starting transfers between devices: 0.22 us -> 4.58 us  [gathered(): held = held + [lax.ppermute(block, axis, pairs) for block in held]]
    ppermute x3 -> x2, starting transfers between devices: 10.3 us -> 6.29 us  [the longest x1 4.87 us: on_device(): upper = lax.ppermute(bottom, 'row', down)]
    pallas_call x5 -> x8, Pallas kernels: 13.4 us -> 9.48 us  [call(): pl.pallas_call(kernel, out_shape=out_shape, in_specs=vmem(len(args)), out...]
    reshape x6 -> x0, local copies, waits for them, and re-layouts: 3.42 us -> none  [on_device(): row = lambda value: value.reshape(1, width)]
    all_to_all x1, waiting for transfers between devices: 2.67 us -> 0.01 us  [on_device(): arrived = lax.all_to_all(chunks, 'row', 0, 0, tiled=True)]
    unnamed x13 -> x20, local copies, waits for them, and re-layouts: 3.55 us -> 1.19 us
    ppermute x3, waiting for transfers between devices: 6.63 us -> 4.33 us  [gathered(): held = held + [lax.ppermute(block, axis, pairs) for block in held]]
    all_to_all x1, starting transfers between devices: 3.64 us -> 5.72 us  [on_device(): back = lax.all_to_all(result, 'row', 0, 0, tiled=True)]
  transfers between devices with their start and end apart: 8 -> 7, of which waited for: 3 -> 3; matrix products, arithmetic and copies ran while one was open for 8% -> 0% of each run, Pallas kernels for 19% -> 15%
where the time goes in v1:
time: 45.4 us; the launch traced here: 45 us
  starting transfers between devices  23.2 us (51%)
  waiting for transfers between devices  11 us (24%)
  Pallas kernels  9.48 us (21%)
  local copies, waits for them, and re-layouts  1.19 us (3%)
    pallas_call x8, Pallas kernels, call(): pl.pallas_call(kernel, out_shape=out_shape, in_specs=vmem(len(args)), out...  9.48 us
    all_to_all x1, starting transfers between devices, on_device(): arrived = lax.all_to_all(chunks, 'row', 0, 0, tiled=True)  6.62 us
    all_to_all x1, starting transfers between devices, on_device(): back = lax.all_to_all(result, 'row', 0, 0, tiled=True)  5.72 us
    all_to_all x1, waiting for transfers between devices, on_device(): back = lax.all_to_all(result, 'row', 0, 0, tiled=True)  5.22 us
    ppermute x1, starting transfers between devices, on_device(): upper = lax.ppermute(bottom, 'row', down)  4.87 us
    ppermute x3, starting transfers between devices, gathered(): held = held + [lax.ppermute(block, axis, pairs) for block in held]  4.58 us
    ppermute x3, waiting for transfers between devices, gathered(): held = held + [lax.ppermute(block, axis, pairs) for block in held]  4.33 us
    ppermute x1, waiting for transfers between devices, on_device(): upper = lax.ppermute(bottom, 'row', down)  1.43 us
  transfers between devices with their start and end apart: 7, of which 3 were waited for; matrix products, arithmetic and copies ran while one was open for 0% of the time, Pallas kernels for 15%

profile of v1, /device:TPU:0, one launch (start us, length us, event | category | flops | bytes accessed | tf_op | source)
XLA Modules:
  0.0 45.0 jit_solution(1782538876235269036)
XLA Ops:
  0.0 1.1 %copy-done.8 = bf16[32,32,192]{2,1,0:T(8,128)(2,1)S(1)} copy-done((bf16[32,32,192]{2,1,0:T(8,128)(2,1)S(1)}, bf16[32,32,192]{2,1,0:T(8,128)(2,1)}, u32[]{:S(2)}) %copy-start.8) | copy-done | bytes 393240
  1.2 4.9 %collective-permute-start = (bf16[1,32,192]{2,1,0:T(8,128)(2,1)S(1)}, bf16[1,32,192]{2,1,0:T(8,128)(2,1)S(1)}, u32[]{:S(2)}, u32[]{:S(2)}) collective-permute-start(bf16[1,32,192]{2,1,0:T(8,128)(2,1)S(1)} %get-tuple-element.12), channel_id=1, source_target_pairs={{0,4},{4,8},{8,12},{12,16},{16,20},{20,24},{24,28},{1,5},{5,9},{9,... | collective-permute-start | bytes 36872 | tf_op jit(solution)/shard_map/ppermute | solution.py:345
  6.1 1.4 %collective-permute-done.upper = bf16[1,32,192]{2,1,0:T(8,128)(2,1)S(1)} collective-permute-done((bf16[1,32,192]{2,1,0:T(8,128)(2,1)S(1)}, bf16[1,32,192]{2,1,0:T(8,128)(2,1)S(1)}, u32[]{:S(2)}, u32[]{:S(2)}) %collective-permute-start) | collective-permute-done | bytes 12320 | tf_op jit(solution)/shard_map/ppermute | solution.py:345
  7.5 0.0 copy-start.5
  7.5 0.0 copy-start.6
  7.5 0.0 copy-start.7
  7.5 1.4 %collective-permute-start.1 = (bf16[48,192]{1,0:T(8,128)(2,1)S(1)}, bf16[48,192]{1,0:T(8,128)(2,1)S(1)}, u32[]{:S(2)}, u32[]{:S(2)}) collective-permute-start(bf16[48,192]{1,0:T(8,128)(2,1)S(1)} %join.1), channel_id=1, source_target_pairs={{0,1},{1,2},{2,3},{4,5},{5,6},{6,7},{8,9},{9,10},{10,11},{12,13},{... | collective-permute-start | bytes 55304 | tf_op jit(solution)/shard_map/ppermute | solution.py:358
  9.0 0.0 copy-done
  9.0 0.8 %own_tile.1.merged = f32[256,384]{1,0:T(8,128)S(1)} custom-call(bf16[32,32,192]{2,1,0:T(8,128)(2,1)S(1)} %copy-done.8, bf16[3,3,192,384]{3,2,1,0:T(8,128)(2,1)S(1)} %copy-done), custom_call_target="tpu_custom_call" | custom-call | flops 1000000000 | bytes 1720320 | tf_op jit(solution)/shard_map/own_tile/pallas_call | solution.py:290
  9.8 0.0 collective-permute-done.1.joined
  9.8 0.0 copy-done.1
  9.8 0.0 copy-done.3
  9.8 0.0 copy-done.4
  9.8 0.0 copy-done.5
  9.8 0.0 copy-done.6
  9.8 1.8 %merge.1 = (bf16[256,384]{1,0:T(8,128)(2,1)S(1)}, bf16[256,384]{1,0:T(8,128)(2,1)S(1)}, bf16[8,144,128]{2,1,0:T(8,128)(2,1)}) custom-call(f32[256,384]{1,0:T(8,128)S(1)} %own_tile.1.merged, bf16[1,32,192]{2,1,0:T(8,128)(2,1)S(1)} %collective-permute-done.upper, bf16[48,192]{1,0:T(8,128)(2,1)S(1)} %collective-permute-done.1.joined, ...), custom_call_target="tpu_custom_call" | custom-call | flops 500000000 | bytes 2643456 | tf_op jit(solution)/shard_map/merge/pallas_call | solution.py:290
  11.7 6.6 %all-to-all-start = ((bf16[8,144,128]{2,1,0:T(8,128)(2,1)}), bf16[8,144,128]{2,1,0:T(8,128)(2,1)S(1)}, u32[]{:S(2)}, u32[]{:S(2)}) async-start(bf16[8,144,128]{2,1,0:T(8,128)(2,1)} %get-tuple-element.14), calls=%async_computation | async-start | bytes 589824 | tf_op jit(solution)/shard_map/all_to_all | solution.py:385
  18.3 0.4 row_qkv.1
  18.7 0.0 copy-start.2
  18.7 0.0 copy-start.9
  18.7 4.6 %collective-permute-start.2 = (bf16[2,384,128]{2,1,0:T(8,128)(2,1)S(1)}, bf16[2,384,128]{2,1,0:T(8,128)(2,1)S(1)}, u32[]{:S(2)}, u32[]{:S(2)}) collective-permute-start(bf16[2,384,128]{2,1,0:T(8,128)(2,1)S(1)} %get-tuple-element.17.refs_1_), channel_id=1, source_target_pairs={{0,2},{1,3},{2,0},{3,1},{4,6},{5,7},{6,4},{7,5},{8,10},{9,11},{10,... | collective-permute-start | bytes 589832 | tf_op jit(solution)/shard_map/ppermute | solution.py:311
  23.3 0.0 collective-permute-start.3
  23.3 4.3 %collective-permute-done.2.refs_2_ = bf16[2,384,128]{2,1,0:T(8,128)(2,1)S(1)} collective-permute-done((bf16[2,384,128]{2,1,0:T(8,128)(2,1)S(1)}, bf16[2,384,128]{2,1,0:T(8,128)(2,1)S(1)}, u32[]{:S(2)}, u32[]{:S(2)}) %collective-permute-start.2) | collective-permute-done | bytes 196640 | tf_op jit(solution)/shard_map/ppermute | solution.py:311
  27.7 0.0 collective-permute-start.4
  27.7 0.0 all-to-all-done.refs_0_
  27.7 3.5 %col_attention.1 = bf16[8,48,128]{2,1,0:T(8,128)(2,1)} custom-call(bf16[8,144,128]{2,1,0:T(8,128)(2,1)S(1)} %all-to-all-done.refs_0_), custom_call_target="tpu_custom_call" | custom-call | flops 2000000000 | bytes 294912 | tf_op jit(solution)/shard_map/col_attention/pallas_call | solution.py:290
  31.2 5.7 %all-to-all-start.1 = ((bf16[8,48,128]{2,1,0:T(8,128)(2,1)}), bf16[8,48,128]{2,1,0:T(8,128)(2,1)S(1)}, u32[]{:S(2)}, u32[]{:S(2)}) async-start(bf16[8,48,128]{2,1,0:T(8,128)(2,1)} %col_attention.1), calls=%async_computation.1 | async-start | bytes 196608 | tf_op jit(solution)/shard_map/all_to_all | solution.py:401
  36.9 0.0 collective-permute-done.3.refs_3_
  36.9 0.0 collective-permute-done.4.refs_4_
  36.9 1.9 %row_attention.1.partial = f32[256,384]{1,0:T(8,128)S(1)} custom-call(bf16[2,192,128]{2,1,0:T(8,128)(2,1)S(1)} %get-tuple-element.16.refs_0_, bf16[2,384,128]{2,1,0:T(8,128)(2,1)S(1)} %get-tuple-element.17.refs_1_, bf16[2,384,128]{2,1,0:T(8,128)(2,1)S(1)} %collective-permute-done.2.refs_2_, bf16[2,384,128]{2,1,0:T(8,128)(2,1)S(1)} %collective-permute-done.3.refs_3_, ...), custom_call_target="tpu_custom_call" | custom-call | flops 2000000000 | bytes 1377792 | tf_op jit(solution)/shard_map/row_attention/pallas_call | solution.py:290
  38.9 5.2 %all-to-all-done.1.arrived = bf16[8,48,128]{2,1,0:T(8,128)(2,1)S(1)} async-done(((bf16[8,48,128]{2,1,0:T(8,128)(2,1)}), bf16[8,48,128]{2,1,0:T(8,128)(2,1)S(1)}, u32[]{:S(2)}, u32[]{:S(2)}) %all-to-all-start.1) | async-done | bytes 98336 | tf_op jit(solution)/shard_map/all_to_all | solution.py:401
  44.1 1.0 %output.1 = bf16[16,16,384]{2,1,0:T(8,128)(2,1)} custom-call(bf16[8,48,128]{2,1,0:T(8,128)(2,1)S(1)} %all-to-all-done.1.arrived, f32[256,384]{1,0:T(8,128)S(1)} %row_attention.1.partial, bf16[384,384]{1,0:T(8,128)(2,1)S(1)} %copy-done.2), custom_call_target="tpu_custom_call" | custom-call | flops 100000000 | bytes 786432 | tf_op jit(solution)/shard_map/output/pallas_call | solution.py:290
  (10 shorter events, 0.1 us)
Async XLA Ops:
  0.0 9.0 %copy-start = (bf16[3,3,192,384]{3,2,1,0:T(8,128)(2,1)S(1)}, bf16[3,3,192,384]{3,2,1,0:T(8,128)(2,1)}, u32[]{:S(2)}) copy-start(bf16[3,3,192,384]{3,2,1,0:T(8,128)(2,1)} %weight.4) | copy-start | bytes 3981316
  0.0 1.1 %copy-start.8 = (bf16[32,32,192]{2,1,0:T(8,128)(2,1)S(1)}, bf16[32,32,192]{2,1,0:T(8,128)(2,1)}, u32[]{:S(2)}) copy-start(bf16[32,32,192]{2,1,0:T(8,128)(2,1)} %image.3) | copy-start | bytes 1179652
  1.2 6.3 %collective-permute-start = (bf16[1,32,192]{2,1,0:T(8,128)(2,1)S(1)}, bf16[1,32,192]{2,1,0:T(8,128)(2,1)S(1)}, u32[]{:S(2)}, u32[]{:S(2)}) collective-permute-start(bf16[1,32,192]{2,1,0:T(8,128)(2,1)S(1)} %get-tuple-element.12), channel_id=1, source_target_pairs={{0,4},{4,8},{8,12},{12,16},{16,20},{20,24},{24,28},{1,5},{5,9},{9,... | collective-permute-start | bytes 36872 | tf_op jit(solution)/shard_map/ppermute | solution.py:345
  7.5 2.3 %copy-start.1 = (bf16[384,1152]{1,0:T(8,128)(2,1)S(1)}, bf16[384,1152]{1,0:T(8,128)(2,1)}, u32[]{:S(2)}) copy-start(bf16[384,1152]{1,0:T(8,128)(2,1)} %qkv.3) | copy-start | bytes 2654212
  7.5 2.3 %copy-start.3 = (f32[384]{0:T(512)S(1)}, f32[384]{0:T(512)}, u32[]{:S(2)}) copy-start(f32[384]{0:T(512)} %bias.1) | copy-start | bytes 4612
  7.5 2.3 %copy-start.4 = (f32[384]{0:T(512)S(1)}, f32[384]{0:T(512)}, u32[]{:S(2)}) copy-start(f32[384]{0:T(512)} %gain.1) | copy-start | bytes 4612
  7.5 2.3 %copy-start.5 = (f32[384]{0:T(512)S(1)}, f32[384]{0:T(512)}, u32[]{:S(2)}) copy-start(f32[384]{0:T(512)} %shift.1) | copy-start | bytes 4612
  7.5 2.3 %copy-start.6 = (f32[384]{0:T(512)S(1)}, f32[384]{0:T(512)}, u32[]{:S(2)}) copy-start(f32[384]{0:T(512)} %gain2.1) | copy-start | bytes 4612
  7.5 2.3 %copy-start.7 = (f32[384]{0:T(512)S(1)}, f32[384]{0:T(512)}, u32[]{:S(2)}) copy-start(f32[384]{0:T(512)} %shift2.1) | copy-start | bytes 4612
  7.5 2.3 %collective-permute-start.1 = (bf16[48,192]{1,0:T(8,128)(2,1)S(1)}, bf16[48,192]{1,0:T(8,128)(2,1)S(1)}, u32[]{:S(2)}, u32[]{:S(2)}) collective-permute-start(bf16[48,192]{1,0:T(8,128)(2,1)S(1)} %join.1), channel_id=1, source_target_pairs={{0,1},{1,2},{2,3},{4,5},{5,6},{6,7},{8,9},{9,10},{10,11},{12,13},{... | collective-permute-start | bytes 55304 | tf_op jit(solution)/shard_map/ppermute | solution.py:358
  11.7 16.0 %all-to-all-start = ((bf16[8,144,128]{2,1,0:T(8,128)(2,1)}), bf16[8,144,128]{2,1,0:T(8,128)(2,1)S(1)}, u32[]{:S(2)}, u32[]{:S(2)}) async-start(bf16[8,144,128]{2,1,0:T(8,128)(2,1)} %get-tuple-element.14), calls=%async_computation | async-start | bytes 589824 | tf_op jit(solution)/shard_map/all_to_all | solution.py:385
  18.7 18.2 %copy-start.2 = (bf16[384,384]{1,0:T(8,128)(2,1)S(1)}, bf16[384,384]{1,0:T(8,128)(2,1)}, u32[]{:S(2)}) copy-start(bf16[384,384]{1,0:T(8,128)(2,1)} %weight.5) | copy-start | bytes 884740
  18.7 18.2 %copy-start.9 = (f32[384]{0:T(512)S(1)}, f32[384]{0:T(512)}, u32[]{:S(2)}) copy-start(f32[384]{0:T(512)} %refs_7_.1) | copy-start | bytes 4612
  18.7 8.9 %collective-permute-start.2 = (bf16[2,384,128]{2,1,0:T(8,128)(2,1)S(1)}, bf16[2,384,128]{2,1,0:T(8,128)(2,1)S(1)}, u32[]{:S(2)}, u32[]{:S(2)}) collective-permute-start(bf16[2,384,128]{2,1,0:T(8,128)(2,1)S(1)} %get-tuple-element.17.refs_1_), channel_id=1, source_target_pairs={{0,2},{1,3},{2,0},{3,1},{4,6},{5,7},{6,4},{7,5},{8,10},{9,11},{10,... | collective-permute-start | bytes 589832 | tf_op jit(solution)/shard_map/ppermute | solution.py:311
  23.3 13.6 %collective-permute-start.3 = (bf16[2,384,128]{2,1,0:T(8,128)(2,1)S(1)}, bf16[2,384,128]{2,1,0:T(8,128)(2,1)S(1)}, u32[]{:S(2)}, u32[]{:S(2)}) collective-permute-start(bf16[2,384,128]{2,1,0:T(8,128)(2,1)S(1)} %get-tuple-element.17.refs_1_), channel_id=1, source_target_pairs={{0,1},{1,0},{2,3},{3,2},{4,5},{5,4},{6,7},{7,6},{8,9},{9,8},{10,11... | collective-permute-start | bytes 589832 | tf_op jit(solution)/shard_map/ppermute | solution.py:311
  27.7 9.3 %collective-permute-start.4 = (bf16[2,384,128]{2,1,0:T(8,128)(2,1)S(1)}, bf16[2,384,128]{2,1,0:T(8,128)(2,1)S(1)}, u32[]{:S(2)}, u32[]{:S(2)}) collective-permute-start(bf16[2,384,128]{2,1,0:T(8,128)(2,1)S(1)} %collective-permute-done.2.refs_2_), channel_id=1, source_target_pairs={{0,1},{1,0},{2,3},{3,2},{4,5},{5,4},{6,7},{7,6},{8,9},{9,8},{10,11... | collective-permute-start | bytes 589832 | tf_op jit(solution)/shard_map/ppermute | solution.py:311
  31.2 12.9 %all-to-all-start.1 = ((bf16[8,48,128]{2,1,0:T(8,128)(2,1)}), bf16[8,48,128]{2,1,0:T(8,128)(2,1)S(1)}, u32[]{:S(2)}, u32[]{:S(2)}) async-start(bf16[8,48,128]{2,1,0:T(8,128)(2,1)} %col_attention.1), calls=%async_computation.1 | async-start | bytes 196608 | tf_op jit(solution)/shard_map/all_to_all | solution.py:401

commit v2 on v1

--- a/solution.py
+++ b/solution.py
@@ -304,13 +304,19 @@
 
 
 def gathered(value, axis):
+    count = lax.axis_size(axis)
     held = [value]
-    bit = lax.axis_size(axis) // 2
-    while bit:
-        pairs = [(k, k ^ bit) for k in range(lax.axis_size(axis))]
-        held = held + [lax.ppermute(block, axis, pairs) for block in held]
-        bit //= 2
+    for step in range(count - 1, 0, -1):
+        pairs = [(k, k ^ step) for k in range(count)]
+        held.append(lax.ppermute(value, axis, pairs))
     return held
+
+
+def exchanged(value, axis):
+    count = lax.axis_size(axis)
+    lead = 5 * count // 8
+    order = [lead] + [k for k in range(count) if k != lead]
+    return lax.all_to_all(value, axis, 0, 0, axis_index_groups=[order], tiled=True)
 
 
 def on_device(
@@ -382,7 +388,7 @@
         5 * 10**8,
         [pltpu.VMEM((pixel_parts, 2, max(in_rows, in_cols) + SPLIT, LANES), F32)],
     )
-    arrived = lax.all_to_all(chunks, "row", 0, 0, tiled=True)
+    arrived = exchanged(chunks, "row")
     queries, pairs = call(
         row_qkv_kernel,
         "row_qkv",
@@ -398,7 +404,7 @@
         (arrived,),
         2 * 10**9,
     )
-    back = lax.all_to_all(result, "row", 0, 0, tiled=True)
+    back = exchanged(result, "row")
     partial = call(
         lambda *refs: row_attention_kernel(len(held), *refs),
         "row_attention",

time: 45.4 us -> 40.7 us (0.90)
  the two profiles are of different devices: /device:TPU:0 before, /device:TPU:6 now
where the time goes in v2:
time: 40.7 us; the launch traced here: 40.4 us
  starting transfers between devices  17.9 us (44%)
  waiting for transfers between devices  11.6 us (29%)
  Pallas kernels  9.47 us (23%)
  local copies, waits for them, and re-layouts  1.2 us (3%)
    all_to_all x2, starting transfers between devices, exchanged(): lax.all_to_all(value, axis, 0, 0, axis_index_groups=[order], tiled=True)  10.5 us
    pallas_call x8, Pallas kernels, call(): pl.pallas_call(kernel, out_shape=out_shape, in_specs=vmem(len(args)), out...  9.47 us
    all_to_all x2, waiting for transfers between devices, exchanged(): lax.all_to_all(value, axis, 0, 0, axis_index_groups=[order], tiled=True)  7.01 us
    ppermute x1, starting transfers between devices, on_device(): upper = lax.ppermute(bottom, 'row', down)  3.43 us
    ppermute x1, waiting for transfers between devices, on_device(): joined = lax.ppermute(joined, 'col', right)  2.43 us
    ppermute x1, waiting for transfers between devices, on_device(): upper = lax.ppermute(bottom, 'row', down)  2.2 us
    ppermute x1, starting transfers between devices, on_device(): joined = lax.ppermute(joined, 'col', right)  2.05 us
    ppermute x3, starting transfers between devices, gathered(): held.append(lax.ppermute(value, axis, pairs))  1.93 us
  transfers between devices with their start and end apart: 7, of which 4 were waited for; matrix products, arithmetic and copies ran while one was open for 0% of the time, Pallas kernels for 16%

profile of v2, /device:TPU:6, one launch (start us, length us, event | category | flops | bytes accessed | tf_op | source)
XLA Modules:
  0.0 40.4 jit_solution(84966807149688764)
XLA Ops:
  0.0 1.1 %copy-done.8 = bf16[32,32,192]{2,1,0:T(8,128)(2,1)S(1)} copy-done((bf16[32,32,192]{2,1,0:T(8,128)(2,1)S(1)}, bf16[32,32,192]{2,1,0:T(8,128)(2,1)}, u32[]{:S(2)}) %copy-start.8) | copy-done | bytes 393240
  1.2 3.4 %collective-permute-start = (bf16[1,32,192]{2,1,0:T(8,128)(2,1)S(1)}, bf16[1,32,192]{2,1,0:T(8,128)(2,1)S(1)}, u32[]{:S(2)}, u32[]{:S(2)}) collective-permute-start(bf16[1,32,192]{2,1,0:T(8,128)(2,1)S(1)} %get-tuple-element.12), channel_id=1, source_target_pairs={{0,4},{4,8},{8,12},{12,16},{16,20},{20,24},{24,28},{1,5},{5,9},{9,... | collective-permute-start | bytes 36872 | tf_op jit(solution)/shard_map/ppermute | solution.py:351
  4.6 2.2 %collective-permute-done.upper = bf16[1,32,192]{2,1,0:T(8,128)(2,1)S(1)} collective-permute-done((bf16[1,32,192]{2,1,0:T(8,128)(2,1)S(1)}, bf16[1,32,192]{2,1,0:T(8,128)(2,1)S(1)}, u32[]{:S(2)}, u32[]{:S(2)}) %collective-permute-start) | collective-permute-done | bytes 12320 | tf_op jit(solution)/shard_map/ppermute | solution.py:351
  6.8 0.0 copy-start.4
  6.8 0.0 copy-start.5
  6.9 0.0 copy-start.6
  6.9 0.0 copy-start.7
  6.9 2.1 %collective-permute-start.1 = (bf16[48,192]{1,0:T(8,128)(2,1)S(1)}, bf16[48,192]{1,0:T(8,128)(2,1)S(1)}, u32[]{:S(2)}, u32[]{:S(2)}) collective-permute-start(bf16[48,192]{1,0:T(8,128)(2,1)S(1)} %join.1), channel_id=1, source_target_pairs={{0,1},{1,2},{2,3},{4,5},{5,6},{6,7},{8,9},{9,10},{10,11},{12,13},{... | collective-permute-start | bytes 55304 | tf_op jit(solution)/shard_map/ppermute | solution.py:364
  8.9 0.0 copy-done
  9.0 0.8 %own_tile.1.merged = f32[256,384]{1,0:T(8,128)S(1)} custom-call(bf16[32,32,192]{2,1,0:T(8,128)(2,1)S(1)} %copy-done.8, bf16[3,3,192,384]{3,2,1,0:T(8,128)(2,1)S(1)} %copy-done), custom_call_target="tpu_custom_call" | custom-call | flops 1000000000 | bytes 1720320 | tf_op jit(solution)/shard_map/own_tile/pallas_call | solution.py:290
  9.7 2.4 %collective-permute-done.1.joined = bf16[48,192]{1,0:T(8,128)(2,1)S(1)} collective-permute-done((bf16[48,192]{1,0:T(8,128)(2,1)S(1)}, bf16[48,192]{1,0:T(8,128)(2,1)S(1)}, u32[]{:S(2)}, u32[]{:S(2)}) %collective-permute-start.1) | collective-permute-done | bytes 18464 | tf_op jit(solution)/shard_map/ppermute | solution.py:364
  12.2 0.0 copy-done.1
  12.2 0.0 copy-done.3
  12.2 0.0 copy-done.4
  12.2 0.0 copy-done.5
  12.2 1.8 %merge.1 = (bf16[256,384]{1,0:T(8,128)(2,1)S(1)}, bf16[256,384]{1,0:T(8,128)(2,1)S(1)}, bf16[8,144,128]{2,1,0:T(8,128)(2,1)}) custom-call(f32[256,384]{1,0:T(8,128)S(1)} %own_tile.1.merged, bf16[1,32,192]{2,1,0:T(8,128)(2,1)S(1)} %collective-permute-done.upper, bf16[48,192]{1,0:T(8,128)(2,1)S(1)} %collective-permute-done.1.joined, ...), custom_call_target="tpu_custom_call" | custom-call | flops 500000000 | bytes 2643456 | tf_op jit(solution)/shard_map/merge/pallas_call | solution.py:290
  14.0 6.3 %all-to-all-start = ((bf16[8,144,128]{2,1,0:T(8,128)(2,1)}), bf16[8,144,128]{2,1,0:T(8,128)(2,1)S(1)}, u32[]{:S(2)}, u32[]{:S(2)}) async-start(bf16[8,144,128]{2,1,0:T(8,128)(2,1)} %get-tuple-element.14), calls=%async_computation | async-start | bytes 589824 | tf_op jit(solution)/shard_map/all_to_all | solution.py:319
  20.3 0.4 %row_qkv.1 = (bf16[2,192,128]{2,1,0:T(8,128)(2,1)S(1)}, bf16[2,384,128]{2,1,0:T(8,128)(2,1)S(1)}) custom-call(bf16[256,384]{1,0:T(8,128)(2,1)S(1)} %get-tuple-element.15.normed, bf16[384,1152]{1,0:T(8,128)(2,1)S(1)} %copy-done.1), custom_call_target="tpu_custom_call" | custom-call | flops 300000000 | bytes 1081344 | tf_op jit(solution)/shard_map/row_qkv/pallas_call | solution.py:290
  20.7 0.0 copy-start.2
  20.8 0.0 copy-start.9
  20.8 0.1 collective-permute-start.4
  20.8 0.1 collective-permute-start.3
  20.9 1.8 %collective-permute-start.2 = (bf16[2,384,128]{2,1,0:T(8,128)(2,1)S(1)}, bf16[2,384,128]{2,1,0:T(8,128)(2,1)S(1)}, u32[]{:S(2)}, u32[]{:S(2)}) collective-permute-start(bf16[2,384,128]{2,1,0:T(8,128)(2,1)S(1)} %get-tuple-element.17.refs_1_), channel_id=1, source_target_pairs={{0,3},{1,2},{2,1},{3,0},{4,7},{5,6},{6,5},{7,4},{8,11},{9,10},{10,... | collective-permute-start | bytes 589832 | tf_op jit(solution)/shard_map/ppermute | solution.py:311
  22.7 4.1 %all-to-all-done.refs_0_ = bf16[8,144,128]{2,1,0:T(8,128)(2,1)S(1)} async-done(((bf16[8,144,128]{2,1,0:T(8,128)(2,1)}), bf16[8,144,128]{2,1,0:T(8,128)(2,1)S(1)}, u32[]{:S(2)}, u32[]{:S(2)}) %all-to-all-start) | async-done | bytes 294944 | tf_op jit(solution)/shard_map/all_to_all | solution.py:319
  26.8 3.5 %col_attention.1 = bf16[8,48,128]{2,1,0:T(8,128)(2,1)} custom-call(bf16[8,144,128]{2,1,0:T(8,128)(2,1)S(1)} %all-to-all-done.refs_0_), custom_call_target="tpu_custom_call" | custom-call | flops 2000000000 | bytes 294912 | tf_op jit(solution)/shard_map/col_attention/pallas_call | solution.py:290
  30.3 4.2 %all-to-all-start.1 = ((bf16[8,48,128]{2,1,0:T(8,128)(2,1)}), bf16[8,48,128]{2,1,0:T(8,128)(2,1)S(1)}, u32[]{:S(2)}, u32[]{:S(2)}) async-start(bf16[8,48,128]{2,1,0:T(8,128)(2,1)} %col_attention.1), calls=%async_computation.1 | async-start | bytes 196608 | tf_op jit(solution)/shard_map/all_to_all | solution.py:319
  34.5 0.0 collective-permute-done.4.refs_4_
  34.5 0.0 collective-permute-done.3.refs_3_
  34.5 0.0 collective-permute-done.2.refs_2_
  34.5 1.9 %row_attention.1.partial = f32[256,384]{1,0:T(8,128)S(1)} custom-call(bf16[2,192,128]{2,1,0:T(8,128)(2,1)S(1)} %get-tuple-element.16.refs_0_, bf16[2,384,128]{2,1,0:T(8,128)(2,1)S(1)} %get-tuple-element.17.refs_1_, bf16[2,384,128]{2,1,0:T(8,128)(2,1)S(1)} %collective-permute-done.2.refs_2_, bf16[2,384,128]{2,1,0:T(8,128)(2,1)S(1)} %collective-permute-done.3.refs_3_, ...), custom_call_target="tpu_custom_call" | custom-call | flops 2000000000 | bytes 1377792 | tf_op jit(solution)/shard_map/row_attention/pallas_call | solution.py:290
  36.5 2.9 %all-to-all-done.1.arrived = bf16[8,48,128]{2,1,0:T(8,128)(2,1)S(1)} async-done(((bf16[8,48,128]{2,1,0:T(8,128)(2,1)}), bf16[8,48,128]{2,1,0:T(8,128)(2,1)S(1)}, u32[]{:S(2)}, u32[]{:S(2)}) %all-to-all-start.1) | async-done | bytes 98336 | tf_op jit(solution)/shard_map/all_to_all | solution.py:319
  39.4 1.0 %output.1 = bf16[16,16,384]{2,1,0:T(8,128)(2,1)} custom-call(bf16[8,48,128]{2,1,0:T(8,128)(2,1)S(1)} %all-to-all-done.1.arrived, f32[256,384]{1,0:T(8,128)S(1)} %row_attention.1.partial, bf16[384,384]{1,0:T(8,128)(2,1)S(1)} %copy-done.2), custom_call_target="tpu_custom_call" | custom-call | flops 100000000 | bytes 786432 | tf_op jit(solution)/shard_map/output/pallas_call | solution.py:290
  (10 shorter events, 0.1 us)
Async XLA Ops:
  0.0 8.9 %copy-start = (bf16[3,3,192,384]{3,2,1,0:T(8,128)(2,1)S(1)}, bf16[3,3,192,384]{3,2,1,0:T(8,128)(2,1)}, u32[]{:S(2)}) copy-start(bf16[3,3,192,384]{3,2,1,0:T(8,128)(2,1)} %weight.4) | copy-start | bytes 3981316
  0.0 1.1 %copy-start.8 = (bf16[32,32,192]{2,1,0:T(8,128)(2,1)S(1)}, bf16[32,32,192]{2,1,0:T(8,128)(2,1)}, u32[]{:S(2)}) copy-start(bf16[32,32,192]{2,1,0:T(8,128)(2,1)} %image.3) | copy-start | bytes 1179652
  1.2 5.6 %collective-permute-start = (bf16[1,32,192]{2,1,0:T(8,128)(2,1)S(1)}, bf16[1,32,192]{2,1,0:T(8,128)(2,1)S(1)}, u32[]{:S(2)}, u32[]{:S(2)}) collective-permute-start(bf16[1,32,192]{2,1,0:T(8,128)(2,1)S(1)} %get-tuple-element.12), channel_id=1, source_target_pairs={{0,4},{4,8},{8,12},{12,16},{16,20},{20,24},{24,28},{1,5},{5,9},{9,... | collective-permute-start | bytes 36872 | tf_op jit(solution)/shard_map/ppermute | solution.py:351
  6.8 5.3 %copy-start.1 = (bf16[384,1152]{1,0:T(8,128)(2,1)S(1)}, bf16[384,1152]{1,0:T(8,128)(2,1)}, u32[]{:S(2)}) copy-start(bf16[384,1152]{1,0:T(8,128)(2,1)} %qkv.3) | copy-start | bytes 2654212
  6.8 5.3 %copy-start.3 = (f32[384]{0:T(512)S(1)}, f32[384]{0:T(512)}, u32[]{:S(2)}) copy-start(f32[384]{0:T(512)} %bias.1) | copy-start | bytes 4612
  6.8 5.3 %copy-start.4 = (f32[384]{0:T(512)S(1)}, f32[384]{0:T(512)}, u32[]{:S(2)}) copy-start(f32[384]{0:T(512)} %gain.1) | copy-start | bytes 4612
  6.8 5.3 %copy-start.5 = (f32[384]{0:T(512)S(1)}, f32[384]{0:T(512)}, u32[]{:S(2)}) copy-start(f32[384]{0:T(512)} %shift.1) | copy-start | bytes 4612
  6.9 5.3 %copy-start.6 = (f32[384]{0:T(512)S(1)}, f32[384]{0:T(512)}, u32[]{:S(2)}) copy-start(f32[384]{0:T(512)} %gain2.1) | copy-start | bytes 4612
  6.9 5.3 %copy-start.7 = (f32[384]{0:T(512)S(1)}, f32[384]{0:T(512)}, u32[]{:S(2)}) copy-start(f32[384]{0:T(512)} %shift2.1) | copy-start | bytes 4612
  6.9 5.3 %collective-permute-start.1 = (bf16[48,192]{1,0:T(8,128)(2,1)S(1)}, bf16[48,192]{1,0:T(8,128)(2,1)S(1)}, u32[]{:S(2)}, u32[]{:S(2)}) collective-permute-start(bf16[48,192]{1,0:T(8,128)(2,1)S(1)} %join.1), channel_id=1, source_target_pairs={{0,1},{1,2},{2,3},{4,5},{5,6},{6,7},{8,9},{9,10},{10,11},{12,13},{... | collective-permute-start | bytes 55304 | tf_op jit(solution)/shard_map/ppermute | solution.py:364
  14.0 12.8 %all-to-all-start = ((bf16[8,144,128]{2,1,0:T(8,128)(2,1)}), bf16[8,144,128]{2,1,0:T(8,128)(2,1)S(1)}, u32[]{:S(2)}, u32[]{:S(2)}) async-start(bf16[8,144,128]{2,1,0:T(8,128)(2,1)} %get-tuple-element.14), calls=%async_computation | async-start | bytes 589824 | tf_op jit(solution)/shard_map/all_to_all | solution.py:319
  20.7 13.8 %copy-start.2 = (bf16[384,384]{1,0:T(8,128)(2,1)S(1)}, bf16[384,384]{1,0:T(8,128)(2,1)}, u32[]{:S(2)}) copy-start(bf16[384,384]{1,0:T(8,128)(2,1)} %weight.5) | copy-start | bytes 884740
  20.8 13.8 %copy-start.9 = (f32[384]{0:T(512)S(1)}, f32[384]{0:T(512)}, u32[]{:S(2)}) copy-start(f32[384]{0:T(512)} %refs_7_.1) | copy-start | bytes 4612
  20.8 13.7 %collective-permute-start.4 = (bf16[2,384,128]{2,1,0:T(8,128)(2,1)S(1)}, bf16[2,384,128]{2,1,0:T(8,128)(2,1)S(1)}, u32[]{:S(2)}, u32[]{:S(2)}) collective-permute-start(bf16[2,384,128]{2,1,0:T(8,128)(2,1)S(1)} %get-tuple-element.17.refs_1_), channel_id=1, source_target_pairs={{0,1},{1,0},{2,3},{3,2},{4,5},{5,4},{6,7},{7,6},{8,9},{9,8},{10,11... | collective-permute-start | bytes 589832 | tf_op jit(solution)/shard_map/ppermute | solution.py:311
  20.8 13.7 %collective-permute-start.3 = (bf16[2,384,128]{2,1,0:T(8,128)(2,1)S(1)}, bf16[2,384,128]{2,1,0:T(8,128)(2,1)S(1)}, u32[]{:S(2)}, u32[]{:S(2)}) collective-permute-start(bf16[2,384,128]{2,1,0:T(8,128)(2,1)S(1)} %get-tuple-element.17.refs_1_), channel_id=1, source_target_pairs={{0,2},{1,3},{2,0},{3,1},{4,6},{5,7},{6,4},{7,5},{8,10},{9,11},{10,... | collective-permute-start | bytes 589832 | tf_op jit(solution)/shard_map/ppermute | solution.py:311
  20.9 13.6 %collective-permute-start.2 = (bf16[2,384,128]{2,1,0:T(8,128)(2,1)S(1)}, bf16[2,384,128]{2,1,0:T(8,128)(2,1)S(1)}, u32[]{:S(2)}, u32[]{:S(2)}) collective-permute-start(bf16[2,384,128]{2,1,0:T(8,128)(2,1)S(1)} %get-tuple-element.17.refs_1_), channel_id=1, source_target_pairs={{0,3},{1,2},{2,1},{3,0},{4,7},{5,6},{6,5},{7,4},{8,11},{9,10},{10,... | collective-permute-start | bytes 589832 | tf_op jit(solution)/shard_map/ppermute | solution.py:311
  30.3 9.1 %all-to-all-start.1 = ((bf16[8,48,128]{2,1,0:T(8,128)(2,1)}), bf16[8,48,128]{2,1,0:T(8,128)(2,1)S(1)}, u32[]{:S(2)}, u32[]{:S(2)}) async-start(bf16[8,48,128]{2,1,0:T(8,128)(2,1)} %col_attention.1), calls=%async_computation.1 | async-start | bytes 196608 | tf_op jit(solution)/shard_map/all_to_all | solution.py:319

commit v3 on v2

--- a/solution.py
+++ b/solution.py
@@ -51,14 +51,19 @@
 def edge_kernel(image, bottom, side):
     rows, cols, _ = image.shape
     bottom[...] = image[rows - 1 :]
-    side[...] = image[:, cols - 2 * SPLIT :].astype(F32)[:, 2 * SPLIT - 1].astype(BF16)
-
-
-def join_kernel(side, upper, joined):
-    size = side.shape[0]
+    side[...] = unless_last(image[:, cols - 2 * SPLIT :].astype(F32)[:, 2 * SPLIT - 1], "col").astype(BF16)
+
+
+def unless_last(value, axis):
+    last = lax.axis_index(axis) == lax.axis_size(axis) - 1
+    return jnp.where(last, jnp.zeros_like(value), value)
+
+
+def join_kernel(bottom, left, joined):
+    size = bottom.shape[1]
     extra = joined.shape[0] - size
-    joined[:size] = side[...]
-    joined[size:] = upper[0, upper.shape[1] - extra :]
+    joined[:size] = unless_last(bottom[0], "row")
+    joined[size:] = unless_last(left[left.shape[0] - extra :], "row")
 
 
 def own_kernel(image, weight, merged, pixels):
@@ -84,10 +89,10 @@
 
 
 def merge_kernel(
-    merged, upper, joined, weight, qkv, bias, gain, shift, gain2, shift2, tokens, normed, chunks, edges
+    merged, left, joined, weight, qkv, bias, gain, shift, gain2, shift2, tokens, normed, chunks, edges
 ):
-    in_cols, channels = upper.shape[1:]
-    in_rows = 2 * merged.shape[0] // (in_cols // 2)
+    in_rows, channels = left.shape
+    in_cols = 4 * merged.shape[0] // in_rows
     rows, cols = in_rows // 2, in_cols // 2
     width = weight.shape[3]
     depth = width // HEADS
@@ -95,10 +100,10 @@
     row = lambda ref: ref[...].reshape(1, width)
     for part, start, size in lane_parts(channels):
         lanes, here = pl.ds(0, size), pl.ds(start, size)
-        beside = joined[:, here].astype(F32)
-        edges[part, 0, pl.ds(first, in_cols), lanes] = upper[0, :, here].astype(F32)
-        edges[part, 0, pl.ds(first - 1, 1), lanes] = beside[beside.shape[0] - 1 :]
-        edges[part, 1, pl.ds(first, in_rows), lanes] = beside[:in_rows]
+        upper = joined[:, here].astype(F32)
+        edges[part, 0, pl.ds(first, in_cols), lanes] = upper[:in_cols]
+        edges[part, 0, pl.ds(first - 1, 1), lanes] = upper[upper.shape[0] - 1 :]
+        edges[part, 1, pl.ds(first, in_rows), lanes] = left[:, here].astype(F32)
         edges[part, 1, pl.ds(first - 1, 1), lanes] = jnp.zeros((1, size), F32)
     above = [every_second(edges, (0,), first - 1 + tap, cols, channels).astype(BF16) for tap in range(3)]
     aside = [every_second(edges, (1,), first - 1 + tap, rows, channels).astype(BF16) for tap in range(3)]
@@ -338,8 +343,8 @@
     depth = width // HEADS
     row_count = lax.axis_size("row")
     col_count = lax.axis_size("col")
-    down = [(k, k + 1) for k in range(row_count - 1)]
-    right = [(k, k + 1) for k in range(col_count - 1)]
+    down = [(k, (k + 1) % row_count) for k in range(row_count)]
+    right = [(k, (k + 1) % col_count) for k in range(col_count)]
     near = 2 * SPLIT
     bottom, side = call(
         edge_kernel,
@@ -348,7 +353,7 @@
         (image,),
         10**10,
     )
-    upper = lax.ppermute(bottom, "row", down)
+    left = lax.ppermute(side, "col", right)
     pixel_parts = -(-channels // LANES)
     merged = call(
         own_kernel,
@@ -359,9 +364,9 @@
         [pltpu.VMEM((pixel_parts, in_rows + 1, in_cols + SPLIT, LANES), F32)],
     )
     joined = call(
-        join_kernel, "join", shape((in_rows + near, channels)), (side, upper), 10**5
-    )
-    joined = lax.ppermute(joined, "col", right)
+        join_kernel, "join", shape((in_cols + near, channels)), (bottom, left), 10**5
+    )
+    joined = lax.ppermute(joined, "row", down)
     stripes, across = rows // SPLIT, cols // SPLIT
     per = across * HALF // row_count
     lanes = rows * SPLIT
@@ -375,7 +380,7 @@
         ),
         (
             merged,
-            upper,
+            left,
             joined,
             conv_weight,
             qkv_weight,

time: 40.7 us -> 38.7 us (0.951)
  the two profiles are of different devices: /device:TPU:6 before, /device:TPU:0 now
where the time goes in v3:
time: 38.7 us; the launch traced here: 38.4 us
  starting transfers between devices  15 us (39%)
  waiting for transfers between devices  12.6 us (33%)
  Pallas kernels  9.49 us (25%)
  local copies, waits for them, and re-layouts  1.2 us (3%)
    all_to_all x2, starting transfers between devices, exchanged(): lax.all_to_all(value, axis, 0, 0, axis_index_groups=[order], tiled=True)  10.2 us
    pallas_call x8, Pallas kernels, call(): pl.pallas_call(kernel, out_shape=out_shape, in_specs=vmem(len(args)), out...  9.49 us
    all_to_all x2, waiting for transfers between devices, exchanged(): lax.all_to_all(value, axis, 0, 0, axis_index_groups=[order], tiled=True)  5.17 us
    ppermute x1, waiting for transfers between devices, on_device(): joined = lax.ppermute(joined, 'row', down)  4.06 us
    ppermute x1, waiting for transfers between devices, on_device(): left = lax.ppermute(side, 'col', right)  3.35 us
    ppermute x1, starting transfers between devices, on_device(): joined = lax.ppermute(joined, 'row', down)  2.38 us
    ppermute x3, starting transfers between devices, gathered(): held.append(lax.ppermute(value, axis, pairs))  1.93 us
    unnamed x20, local copies, waits for them, and re-layouts  1.2 us
  transfers between devices with their start and end apart: 7, of which 4 were waited for; matrix products, arithmetic and copies ran while one was open for 0% of the time, Pallas kernels for 17%

profile of v3, /device:TPU:0, one launch (start us, length us, event | category | flops | bytes accessed | tf_op | source)
XLA Modules:
  0.0 38.4 jit_solution(65985463823651509)
XLA Ops:
  0.0 1.1 %copy-done.8 = bf16[32,32,192]{2,1,0:T(8,128)(2,1)S(1)} copy-done((bf16[32,32,192]{2,1,0:T(8,128)(2,1)S(1)}, bf16[32,32,192]{2,1,0:T(8,128)(2,1)}, u32[]{:S(2)}) %copy-start.8) | copy-done | bytes 393240
  1.1 0.1 edge.1
  1.2 0.5 %collective-permute-start = (bf16[32,192]{1,0:T(8,128)(2,1)S(1)}, bf16[32,192]{1,0:T(8,128)(2,1)S(1)}, u32[]{:S(2)}, u32[]{:S(2)}) collective-permute-start(bf16[32,192]{1,0:T(8,128)(2,1)S(1)} %get-tuple-element.12), channel_id=1, source_target_pairs={{0,1},{1,2},{2,3},{3,0},{4,5},{5,6},{6,7},{7,4},{8,9},{9,10},{10,1... | collective-permute-start | bytes 36872 | tf_op jit(solution)/shard_map/ppermute | solution.py:356
  1.7 3.3 %collective-permute-done.left = bf16[32,192]{1,0:T(8,128)(2,1)S(1)} collective-permute-done((bf16[32,192]{1,0:T(8,128)(2,1)S(1)}, bf16[32,192]{1,0:T(8,128)(2,1)S(1)}, u32[]{:S(2)}, u32[]{:S(2)}) %collective-permute-start) | collective-permute-done | bytes 12320 | tf_op jit(solution)/shard_map/ppermute | solution.py:356
  5.1 0.0 copy-start.4
  5.1 0.0 copy-start.5
  5.1 0.0 copy-start.6
  5.1 0.0 copy-start.7
  5.1 2.4 %collective-permute-start.1 = (bf16[48,192]{1,0:T(8,128)(2,1)S(1)}, bf16[48,192]{1,0:T(8,128)(2,1)S(1)}, u32[]{:S(2)}, u32[]{:S(2)}) collective-permute-start(bf16[48,192]{1,0:T(8,128)(2,1)S(1)} %join.1), channel_id=1, source_target_pairs={{0,4},{4,8},{8,12},{12,16},{16,20},{20,24},{24,28},{28,0},{1,5},{5... | collective-permute-start | bytes 55304 | tf_op jit(solution)/shard_map/ppermute | solution.py:369
  7.5 0.0 copy-done
  7.5 0.8 %own_tile.1.merged = f32[256,384]{1,0:T(8,128)S(1)} custom-call(bf16[32,32,192]{2,1,0:T(8,128)(2,1)S(1)} %copy-done.8, bf16[3,3,192,384]{3,2,1,0:T(8,128)(2,1)S(1)} %copy-done), custom_call_target="tpu_custom_call" | custom-call | flops 1000000000 | bytes 1720320 | tf_op jit(solution)/shard_map/own_tile/pallas_call | solution.py:295
  8.3 4.1 %collective-permute-done.1.joined = bf16[48,192]{1,0:T(8,128)(2,1)S(1)} collective-permute-done((bf16[48,192]{1,0:T(8,128)(2,1)S(1)}, bf16[48,192]{1,0:T(8,128)(2,1)S(1)}, u32[]{:S(2)}, u32[]{:S(2)}) %collective-permute-start.1) | collective-permute-done | bytes 18464 | tf_op jit(solution)/shard_map/ppermute | solution.py:369
  12.4 0.0 copy-done.1
  12.4 0.0 copy-done.3
  12.4 0.0 copy-done.4
  12.4 1.8 %merge.1 = (bf16[256,384]{1,0:T(8,128)(2,1)S(1)}, bf16[256,384]{1,0:T(8,128)(2,1)S(1)}, bf16[8,144,128]{2,1,0:T(8,128)(2,1)}) custom-call(f32[256,384]{1,0:T(8,128)S(1)} %own_tile.1.merged, bf16[32,192]{1,0:T(8,128)(2,1)S(1)} %collective-permute-done.left, bf16[48,192]{1,0:T(8,128)(2,1)S(1)} %collective-permute-done.1.joined, ...), custom_call_target="tpu_custom_call" | custom-call | flops 500000000 | bytes 2643456 | tf_op jit(solution)/shard_map/merge/pallas_call | solution.py:295
  14.2 5.1 %all-to-all-start = ((bf16[8,144,128]{2,1,0:T(8,128)(2,1)}), bf16[8,144,128]{2,1,0:T(8,128)(2,1)S(1)}, u32[]{:S(2)}, u32[]{:S(2)}) async-start(bf16[8,144,128]{2,1,0:T(8,128)(2,1)} %get-tuple-element.14), calls=%async_computation | async-start | bytes 589824 | tf_op jit(solution)/shard_map/all_to_all | solution.py:324
  19.3 0.4 %row_qkv.1 = (bf16[2,192,128]{2,1,0:T(8,128)(2,1)S(1)}, bf16[2,384,128]{2,1,0:T(8,128)(2,1)S(1)}) custom-call(bf16[256,384]{1,0:T(8,128)(2,1)S(1)} %get-tuple-element.15.normed, bf16[384,1152]{1,0:T(8,128)(2,1)S(1)} %copy-done.1), custom_call_target="tpu_custom_call" | custom-call | flops 300000000 | bytes 1081344 | tf_op jit(solution)/shard_map/row_qkv/pallas_call | solution.py:295
  19.8 0.0 copy-start.2
  19.8 0.0 copy-start.9
  19.8 0.1 collective-permute-start.4
  19.9 1.7 %collective-permute-start.3 = (bf16[2,384,128]{2,1,0:T(8,128)(2,1)S(1)}, bf16[2,384,128]{2,1,0:T(8,128)(2,1)S(1)}, u32[]{:S(2)}, u32[]{:S(2)}) collective-permute-start(bf16[2,384,128]{2,1,0:T(8,128)(2,1)S(1)} %get-tuple-element.17.refs_1_), channel_id=1, source_target_pairs={{0,2},{1,3},{2,0},{3,1},{4,6},{5,7},{6,4},{7,5},{8,10},{9,11},{10,... | collective-permute-start | bytes 589832 | tf_op jit(solution)/shard_map/ppermute | solution.py:316
  21.6 0.1 collective-permute-start.2
  21.7 3.5 %all-to-all-done.refs_0_ = bf16[8,144,128]{2,1,0:T(8,128)(2,1)S(1)} async-done(((bf16[8,144,128]{2,1,0:T(8,128)(2,1)}), bf16[8,144,128]{2,1,0:T(8,128)(2,1)S(1)}, u32[]{:S(2)}, u32[]{:S(2)}) %all-to-all-start) | async-done | bytes 294944 | tf_op jit(solution)/shard_map/all_to_all | solution.py:324
  25.2 3.5 %col_attention.1 = bf16[8,48,128]{2,1,0:T(8,128)(2,1)} custom-call(bf16[8,144,128]{2,1,0:T(8,128)(2,1)S(1)} %all-to-all-done.refs_0_), custom_call_target="tpu_custom_call" | custom-call | flops 2000000000 | bytes 294912 | tf_op jit(solution)/shard_map/col_attention/pallas_call | solution.py:295
  28.8 5.1 %all-to-all-start.1 = ((bf16[8,48,128]{2,1,0:T(8,128)(2,1)}), bf16[8,48,128]{2,1,0:T(8,128)(2,1)S(1)}, u32[]{:S(2)}, u32[]{:S(2)}) async-start(bf16[8,48,128]{2,1,0:T(8,128)(2,1)} %col_attention.1), calls=%async_computation.1 | async-start | bytes 196608 | tf_op jit(solution)/shard_map/all_to_all | solution.py:324
  33.9 0.0 collective-permute-done.4.refs_4_
  33.9 0.0 collective-permute-done.3.refs_3_
  33.9 0.0 collective-permute-done.2.refs_2_
  33.9 1.9 %row_attention.1.partial = f32[256,384]{1,0:T(8,128)S(1)} custom-call(bf16[2,192,128]{2,1,0:T(8,128)(2,1)S(1)} %get-tuple-element.16.refs_0_, bf16[2,384,128]{2,1,0:T(8,128)(2,1)S(1)} %get-tuple-element.17.refs_1_, bf16[2,384,128]{2,1,0:T(8,128)(2,1)S(1)} %collective-permute-done.2.refs_2_, bf16[2,384,128]{2,1,0:T(8,128)(2,1)S(1)} %collective-permute-done.3.refs_3_, ...), custom_call_target="tpu_custom_call" | custom-call | flops 2000000000 | bytes 1377792 | tf_op jit(solution)/shard_map/row_attention/pallas_call | solution.py:295
  35.8 1.6 %all-to-all-done.1.arrived = bf16[8,48,128]{2,1,0:T(8,128)(2,1)S(1)} async-done(((bf16[8,48,128]{2,1,0:T(8,128)(2,1)}), bf16[8,48,128]{2,1,0:T(8,128)(2,1)S(1)}, u32[]{:S(2)}, u32[]{:S(2)}) %all-to-all-start.1) | async-done | bytes 98336 | tf_op jit(solution)/shard_map/all_to_all | solution.py:324
  37.5 1.0 %output.1 = bf16[16,16,384]{2,1,0:T(8,128)(2,1)} custom-call(bf16[8,48,128]{2,1,0:T(8,128)(2,1)S(1)} %all-to-all-done.1.arrived, f32[256,384]{1,0:T(8,128)S(1)} %row_attention.1.partial, bf16[384,384]{1,0:T(8,128)(2,1)S(1)} %copy-done.2), custom_call_target="tpu_custom_call" | custom-call | flops 100000000 | bytes 786432 | tf_op jit(solution)/shard_map/output/pallas_call | solution.py:295
  (10 shorter events, 0.0 us)
Async XLA Ops:
  0.0 7.5 %copy-start = (bf16[3,3,192,384]{3,2,1,0:T(8,128)(2,1)S(1)}, bf16[3,3,192,384]{3,2,1,0:T(8,128)(2,1)}, u32[]{:S(2)}) copy-start(bf16[3,3,192,384]{3,2,1,0:T(8,128)(2,1)} %weight.4) | copy-start | bytes 3981316
  0.0 1.1 %copy-start.8 = (bf16[32,32,192]{2,1,0:T(8,128)(2,1)S(1)}, bf16[32,32,192]{2,1,0:T(8,128)(2,1)}, u32[]{:S(2)}) copy-start(bf16[32,32,192]{2,1,0:T(8,128)(2,1)} %image.3) | copy-start | bytes 1179652
  1.2 3.9 %collective-permute-start = (bf16[32,192]{1,0:T(8,128)(2,1)S(1)}, bf16[32,192]{1,0:T(8,128)(2,1)S(1)}, u32[]{:S(2)}, u32[]{:S(2)}) collective-permute-start(bf16[32,192]{1,0:T(8,128)(2,1)S(1)} %get-tuple-element.12), channel_id=1, source_target_pairs={{0,1},{1,2},{2,3},{3,0},{4,5},{5,6},{6,7},{7,4},{8,9},{9,10},{10,1... | collective-permute-start | bytes 36872 | tf_op jit(solution)/shard_map/ppermute | solution.py:356
  5.1 7.3 %copy-start.1 = (bf16[384,1152]{1,0:T(8,128)(2,1)S(1)}, bf16[384,1152]{1,0:T(8,128)(2,1)}, u32[]{:S(2)}) copy-start(bf16[384,1152]{1,0:T(8,128)(2,1)} %qkv.3) | copy-start | bytes 2654212
  5.1 7.3 %copy-start.3 = (f32[384]{0:T(512)S(1)}, f32[384]{0:T(512)}, u32[]{:S(2)}) copy-start(f32[384]{0:T(512)} %bias.1) | copy-start | bytes 4612
  5.1 7.3 %copy-start.4 = (f32[384]{0:T(512)S(1)}, f32[384]{0:T(512)}, u32[]{:S(2)}) copy-start(f32[384]{0:T(512)} %gain.1) | copy-start | bytes 4612
  5.1 7.3 %copy-start.5 = (f32[384]{0:T(512)S(1)}, f32[384]{0:T(512)}, u32[]{:S(2)}) copy-start(f32[384]{0:T(512)} %shift.1) | copy-start | bytes 4612
  5.1 7.3 %copy-start.6 = (f32[384]{0:T(512)S(1)}, f32[384]{0:T(512)}, u32[]{:S(2)}) copy-start(f32[384]{0:T(512)} %gain2.1) | copy-start | bytes 4612
  5.1 7.3 %copy-start.7 = (f32[384]{0:T(512)S(1)}, f32[384]{0:T(512)}, u32[]{:S(2)}) copy-start(f32[384]{0:T(512)} %shift2.1) | copy-start | bytes 4612
  5.1 7.2 %collective-permute-start.1 = (bf16[48,192]{1,0:T(8,128)(2,1)S(1)}, bf16[48,192]{1,0:T(8,128)(2,1)S(1)}, u32[]{:S(2)}, u32[]{:S(2)}) collective-permute-start(bf16[48,192]{1,0:T(8,128)(2,1)S(1)} %join.1), channel_id=1, source_target_pairs={{0,4},{4,8},{8,12},{12,16},{16,20},{20,24},{24,28},{28,0},{1,5},{5... | collective-permute-start | bytes 55304 | tf_op jit(solution)/shard_map/ppermute | solution.py:369
  14.2 11.0 %all-to-all-start = ((bf16[8,144,128]{2,1,0:T(8,128)(2,1)}), bf16[8,144,128]{2,1,0:T(8,128)(2,1)S(1)}, u32[]{:S(2)}, u32[]{:S(2)}) async-start(bf16[8,144,128]{2,1,0:T(8,128)(2,1)} %get-tuple-element.14), calls=%async_computation | async-start | bytes 589824 | tf_op jit(solution)/shard_map/all_to_all | solution.py:324
  19.8 14.1 %copy-start.2 = (bf16[384,384]{1,0:T(8,128)(2,1)S(1)}, bf16[384,384]{1,0:T(8,128)(2,1)}, u32[]{:S(2)}) copy-start(bf16[384,384]{1,0:T(8,128)(2,1)} %weight.5) | copy-start | bytes 884740
  19.8 14.1 %copy-start.9 = (f32[384]{0:T(512)S(1)}, f32[384]{0:T(512)}, u32[]{:S(2)}) copy-start(f32[384]{0:T(512)} %refs_7_.1) | copy-start | bytes 4612
  19.8 14.1 %collective-permute-start.4 = (bf16[2,384,128]{2,1,0:T(8,128)(2,1)S(1)}, bf16[2,384,128]{2,1,0:T(8,128)(2,1)S(1)}, u32[]{:S(2)}, u32[]{:S(2)}) collective-permute-start(bf16[2,384,128]{2,1,0:T(8,128)(2,1)S(1)} %get-tuple-element.17.refs_1_), channel_id=1, source_target_pairs={{0,1},{1,0},{2,3},{3,2},{4,5},{5,4},{6,7},{7,6},{8,9},{9,8},{10,11... | collective-permute-start | bytes 589832 | tf_op jit(solution)/shard_map/ppermute | solution.py:316
  19.9 14.0 %collective-permute-start.3 = (bf16[2,384,128]{2,1,0:T(8,128)(2,1)S(1)}, bf16[2,384,128]{2,1,0:T(8,128)(2,1)S(1)}, u32[]{:S(2)}, u32[]{:S(2)}) collective-permute-start(bf16[2,384,128]{2,1,0:T(8,128)(2,1)S(1)} %get-tuple-element.17.refs_1_), channel_id=1, source_target_pairs={{0,2},{1,3},{2,0},{3,1},{4,6},{5,7},{6,4},{7,5},{8,10},{9,11},{10,... | collective-permute-start | bytes 589832 | tf_op jit(solution)/shard_map/ppermute | solution.py:316
  21.6 12.3 %collective-permute-start.2 = (bf16[2,384,128]{2,1,0:T(8,128)(2,1)S(1)}, bf16[2,384,128]{2,1,0:T(8,128)(2,1)S(1)}, u32[]{:S(2)}, u32[]{:S(2)}) collective-permute-start(bf16[2,384,128]{2,1,0:T(8,128)(2,1)S(1)} %get-tuple-element.17.refs_1_), channel_id=1, source_target_pairs={{0,3},{1,2},{2,1},{3,0},{4,7},{5,6},{6,5},{7,4},{8,11},{9,10},{10,... | collective-permute-start | bytes 589832 | tf_op jit(solution)/shard_map/ppermute | solution.py:316
  28.8 8.7 %all-to-all-start.1 = ((bf16[8,48,128]{2,1,0:T(8,128)(2,1)}), bf16[8,48,128]{2,1,0:T(8,128)(2,1)S(1)}, u32[]{:S(2)}, u32[]{:S(2)}) async-start(bf16[8,48,128]{2,1,0:T(8,128)(2,1)} %col_attention.1), calls=%async_computation.1 | async-start | bytes 196608 | tf_op jit(solution)/shard_map/all_to_all | solution.py:324

commit v4 on v3

--- a/solution.py
+++ b/solution.py
@@ -48,22 +48,20 @@
     )
 
 
-def edge_kernel(image, bottom, side):
-    rows, cols, _ = image.shape
-    bottom[...] = image[rows - 1 :]
-    side[...] = unless_last(image[:, cols - 2 * SPLIT :].astype(F32)[:, 2 * SPLIT - 1], "col").astype(BF16)
-
-
 def unless_last(value, axis):
     last = lax.axis_index(axis) == lax.axis_size(axis) - 1
     return jnp.where(last, jnp.zeros_like(value), value)
 
 
-def join_kernel(bottom, left, joined):
-    size = bottom.shape[1]
-    extra = joined.shape[0] - size
-    joined[:size] = unless_last(bottom[0], "row")
-    joined[size:] = unless_last(left[left.shape[0] - extra :], "row")
+def edge_kernel(image, bottom, side):
+    rows, cols, _ = image.shape
+    near = 2 * SPLIT
+    bottom[...] = unless_last(image[rows - 1], "row")
+    side[...] = unless_last(image[:, cols - near :].astype(F32)[:, near - 1], "col").astype(BF16)
+
+
+def corner_kernel(bottom, corner):
+    corner[...] = unless_last(bottom[bottom.shape[0] - corner.shape[0] :], "col")
 
 
 def own_kernel(image, weight, merged, pixels):
@@ -89,7 +87,7 @@
 
 
 def merge_kernel(
-    merged, left, joined, weight, qkv, bias, gain, shift, gain2, shift2, tokens, normed, chunks, edges
+    merged, upper, left, corner, weight, qkv, bias, gain, shift, gain2, shift2, tokens, normed, chunks, edges, held_chunks, sems
 ):
     in_rows, channels = left.shape
     in_cols = 4 * merged.shape[0] // in_rows
@@ -100,9 +98,8 @@
     row = lambda ref: ref[...].reshape(1, width)
     for part, start, size in lane_parts(channels):
         lanes, here = pl.ds(0, size), pl.ds(start, size)
-        upper = joined[:, here].astype(F32)
-        edges[part, 0, pl.ds(first, in_cols), lanes] = upper[:in_cols]
-        edges[part, 0, pl.ds(first - 1, 1), lanes] = upper[upper.shape[0] - 1 :]
+        edges[part, 0, pl.ds(first, in_cols), lanes] = upper[:, here].astype(F32)
+        edges[part, 0, pl.ds(first - 1, 1), lanes] = corner[:, here].astype(F32)[corner.shape[0] - 1 :]
         edges[part, 1, pl.ds(first, in_rows), lanes] = left[:, here].astype(F32)
         edges[part, 1, pl.ds(first - 1, 1), lanes] = jnp.zeros((1, size), F32)
     above = [every_second(edges, (0,), first - 1 + tap, cols, channels).astype(BF16) for tap in range(3)]
@@ -131,6 +128,7 @@
     count = chunks.shape[0]
     per = across * HALF // count
     square = SPLIT * SPLIT
+    copies = [pltpu.make_async_copy(held_chunks.at[k], chunks.at[k], sems.at[k]) for k in range(count)]
     for b in range(across):
         mine = [
             again[(a * across + b) * square : (a * across + b + 1) * square] for a in range(rows // SPLIT)
@@ -144,9 +142,12 @@
             lines.append(wide.T[begin - base :])
         for item in range(b * HALF, (b + 1) * HALF, per):
             low = (item - b * HALF) * depth
-            chunks[item // per] = jnp.concatenate(
+            held_chunks[item // per] = jnp.concatenate(
                 [kind[low : low + per * depth] for kind in lines], 0
             ).astype(BF16)
+            copies[item // per].start()
+    for copy in copies:
+        copy.wait()
 
 
 def row_qkv_kernel(normed, qkv, queries, pairs):
@@ -199,17 +200,18 @@
     return mixed[:depth] / mixed[depth : depth + 1]
 
 
-def col_attention_kernel(depth, arrived, result):
+def col_attention_kernel(depth, arrived, result, done, sems):
     count, lines, length = arrived.shape
     per = lines // (3 * depth)
     total = per * depth
     lanes = jnp.concatenate([arrived[s].astype(F32) for s in range(count)], 1)
-    key_rows = lanes[total : 2 * total].T.astype(BF16)
+    key_rows = lanes[total : 2 * total].astype(BF16).T
     values = [
         with_sum_row(lanes[2 * total + h * depth : 2 * total + (h + 1) * depth]) for h in range(per)
     ]
-    block = 4 * length
-    done = {}
+    block = 2 * length
+    copies = [pltpu.make_async_copy(done.at[k], result.at[k], sems.at[k]) for k in range(count)]
+    heads = []
 
     def score(item):
         begin, h = item
@@ -218,14 +220,18 @@
         return scores, jnp.max(scores, 0, keepdims=True)
 
     def finish(item, scores, highest):
-        done[item] = attended(dot(values[item[1]], weights_of(scores, highest, depth)), depth)
-
-    starts = range(0, count * length, block)
-    ahead_of([(begin, h) for begin in starts for h in range(per)], score, finish, 1)
-    for begin in starts:
-        heads = jnp.concatenate([done[begin, h] for h in range(per)], 0).astype(BF16)
-        for k in range(block // length):
-            result[begin // length + k] = heads[:, k * length : (k + 1) * length]
+        begin, h = item
+        heads.append(attended(dot(values[h], weights_of(scores, highest, depth)), depth))
+        if h == per - 1:
+            both = jnp.concatenate(heads, 0).astype(BF16)
+            heads.clear()
+            for k in range(begin // length, (begin + block) // length):
+                done[k] = both[:, k * length - begin : (k + 1) * length - begin]
+                copies[k].start()
+
+    ahead_of([(begin, h) for begin in range(0, count * length, block) for h in range(per)], score, finish, 3)
+    for copy in copies:
+        copy.wait()
 
 
 def row_attention_kernel(count, queries, *refs):
@@ -290,13 +296,16 @@
         ).astype(BF16)
 
 
-def call(kernel, name, out_shape, args, flops, scratch=()):
+def call(kernel, name, out_shape, args, flops, scratch=(), loose=()):
+    several = isinstance(out_shape, tuple)
+    spaces = [pl.ANY if k in loose else pltpu.VMEM for k in range(len(out_shape) if several else 1)]
+    specs = tuple(pl.BlockSpec(memory_space=space) for space in spaces)
     moved = sum(x.size * x.dtype.itemsize for x in args)
     return pl.pallas_call(
         kernel,
         out_shape=out_shape,
         in_specs=vmem(len(args)),
-        out_specs=jax.tree.map(lambda _: pl.BlockSpec(memory_space=pltpu.VMEM), out_shape),
+        out_specs=specs if several else specs[0],
         scratch_shapes=scratch,
         compiler_params=params(),
         cost_estimate=pl.CostEstimate(flops=flops, bytes_accessed=moved, transcendentals=0),
@@ -345,15 +354,23 @@
     col_count = lax.axis_size("col")
     down = [(k, (k + 1) % row_count) for k in range(row_count)]
     right = [(k, (k + 1) % col_count) for k in range(col_count)]
+    diagonal = []
+    for r in range(row_count):
+        for c in range(col_count):
+            target = (r, 0) if c == col_count - 1 else ((r + 1) % row_count, c + 1)
+            diagonal.append((r * col_count + c, target[0] * col_count + target[1]))
     near = 2 * SPLIT
     bottom, side = call(
         edge_kernel,
         "edge",
-        (shape((1, in_cols, channels)), shape((in_rows, channels))),
+        (shape((in_cols, channels)), shape((in_rows, channels))),
         (image,),
-        10**10,
-    )
+        10**5,
+    )
+    corner = call(corner_kernel, "corner", shape((near, channels)), (bottom,), 10**10)
+    upper = lax.ppermute(bottom, "row", down)
     left = lax.ppermute(side, "col", right)
+    corner = lax.ppermute(corner, ("row", "col"), diagonal)
     pixel_parts = -(-channels // LANES)
     merged = call(
         own_kernel,
@@ -363,10 +380,6 @@
         10**9,
         [pltpu.VMEM((pixel_parts, in_rows + 1, in_cols + SPLIT, LANES), F32)],
     )
-    joined = call(
-        join_kernel, "join", shape((in_cols + near, channels)), (bottom, left), 10**5
-    )
-    joined = lax.ppermute(joined, "row", down)
     stripes, across = rows // SPLIT, cols // SPLIT
     per = across * HALF // row_count
     lanes = rows * SPLIT
@@ -380,8 +393,9 @@
         ),
         (
             merged,
+            upper,
             left,
-            joined,
+            corner,
             conv_weight,
             qkv_weight,
             conv_bias,
@@ -391,7 +405,12 @@
             norm_shift,
         ),
         5 * 10**8,
-        [pltpu.VMEM((pixel_parts, 2, max(in_rows, in_cols) + SPLIT, LANES), F32)],
+        [
+            pltpu.VMEM((pixel_parts, 2, max(in_rows, in_cols) + SPLIT, LANES), F32),
+            pltpu.VMEM((row_count, 3 * per * depth, lanes), BF16),
+            pltpu.SemaphoreType.DMA((row_count,)),
+        ],
+        (2,),
     )
     arrived = exchanged(chunks, "row")
     queries, pairs = call(
@@ -408,6 +427,8 @@
         shape((row_count, per * depth, lanes)),
         (arrived,),
         2 * 10**9,
+        [pltpu.VMEM((row_count, per * depth, lanes), BF16), pltpu.SemaphoreType.DMA((row_count,))],
+        (0,),
     )
     back = exchanged(result, "row")
     partial = call(

time: 38.7 us -> 38 us (0.982)
  waiting for transfers between devices: 12.6 us -> 7.44 us
  starting transfers between devices: 15 us -> 19.6 us
    ppermute x1 -> x2, waiting for transfers between devices: 4.06 us -> 0.83 us  [the longest x1 0.82 us: on_device(): upper = lax.ppermute(bottom, 'row', down)]
    ppermute x1, waiting for transfers between devices: 3.35 us -> 0.48 us  [on_device(): left = lax.ppermute(side, 'col', right)]
    ppermute x1, starting transfers between devices: 0.5 us -> 1.93 us  [on_device(): left = lax.ppermute(side, 'col', right)]
    ppermute x1 -> x2, starting transfers between devices: 2.38 us -> 3.7 us  [the longest x1 3.02 us: on_device(): upper = lax.ppermute(bottom, 'row', down)]
    all_to_all x2, starting transfers between devices: 10.2 us -> 11.3 us  [exchanged(): lax.all_to_all(value, axis, 0, 0, axis_index_groups=[order], tiled=True)]
    all_to_all x2, waiting for transfers between devices: 5.17 us -> 6.13 us  [exchanged(): lax.all_to_all(value, axis, 0, 0, axis_index_groups=[order], tiled=True)]
    ppermute x3, starting transfers between devices: 1.93 us -> 2.68 us  [gathered(): held.append(lax.ppermute(value, axis, pairs))]
    unnamed x20 -> x22, local copies, waits for them, and re-layouts: 1.2 us -> 1.09 us
  transfers between devices with their start and end apart: 7 -> 8, of which waited for: 4 -> 4; matrix products, arithmetic and copies ran while one was open for 0% -> 0% of each run, Pallas kernels for 17% -> 17%
where the time goes in v4:
time: 38 us; the launch traced here: 37.7 us
  starting transfers between devices  19.6 us (52%)
  Pallas kernels  9.41 us (25%)
  waiting for transfers between devices  7.44 us (20%)
  local copies, waits for them, and re-layouts  1.09 us (3%)
    all_to_all x2, starting transfers between devices, exchanged(): lax.all_to_all(value, axis, 0, 0, axis_index_groups=[order], tiled=True)  11.3 us
    pallas_call x8, Pallas kernels, call(): pl.pallas_call(kernel, out_shape=out_shape, in_specs=vmem(len(args)), out...  9.41 us
    all_to_all x2, waiting for transfers between devices, exchanged(): lax.all_to_all(value, axis, 0, 0, axis_index_groups=[order], tiled=True)  6.13 us
    ppermute x1, starting transfers between devices, on_device(): upper = lax.ppermute(bottom, 'row', down)  3.02 us
    ppermute x3, starting transfers between devices, gathered(): held.append(lax.ppermute(value, axis, pairs))  2.68 us
    ppermute x1, starting transfers between devices, on_device(): left = lax.ppermute(side, 'col', right)  1.93 us
    unnamed x22, local copies, waits for them, and re-layouts  1.09 us
    ppermute x1, waiting for transfers between devices, on_device(): upper = lax.ppermute(bottom, 'row', down)  0.82 us
  transfers between devices with their start and end apart: 8, of which 4 were waited for; matrix products, arithmetic and copies ran while one was open for 0% of the time, Pallas kernels for 17%

profile of v4, /device:TPU:0, one launch (start us, length us, event | category | flops | bytes accessed | tf_op | source)
XLA Modules:
  0.0 37.7 jit_solution(6704767006610774823)
XLA Ops:
  0.0 1.0 %copy-done.2 = bf16[32,32,192]{2,1,0:T(8,128)(2,1)S(1)} copy-done((bf16[32,32,192]{2,1,0:T(8,128)(2,1)S(1)}, bf16[32,32,192]{2,1,0:T(8,128)(2,1)}, u32[]{:S(2)}) %copy-start.2) | copy-done | bytes 393240
  1.0 0.1 edge.1
  1.1 0.0 copy-start
  1.1 0.0 copy-start.3
  1.1 3.0 %collective-permute-start = (bf16[32,192]{1,0:T(8,128)(2,1)S(1)}, bf16[32,192]{1,0:T(8,128)(2,1)S(1)}, u32[]{:S(2)}, u32[]{:S(2)}) collective-permute-start(bf16[32,192]{1,0:T(8,128)(2,1)S(1)} %get-tuple-element.12.bottom), channel_id=1, source_target_pairs={{0,4},{4,8},{8,12},{12,16},{16,20},{20,24},{24,28},{28,0},{1,5},{5... | collective-permute-start | bytes 36872 | tf_op jit(solution)/shard_map/ppermute | solution.py:371
  4.2 0.7 %collective-permute-start.2 = (bf16[16,192]{1,0:T(8,128)(2,1)S(1)}, bf16[16,192]{1,0:T(8,128)(2,1)S(1)}, u32[]{:S(2)}, u32[]{:S(2)}) collective-permute-start(bf16[16,192]{1,0:T(8,128)(2,1)S(1)} %corner.1), channel_id=1, source_target_pairs={{0,5},{1,6},{2,7},{3,0},{4,9},{5,10},{6,11},{7,4},{8,13},{9,14},{1... | collective-permute-start | bytes 18440 | tf_op jit(solution)/shard_map/ppermute | solution.py:373
  4.8 0.0 copy-start.8
  4.9 0.0 copy-start.9
  4.9 1.9 %collective-permute-start.1 = (bf16[32,192]{1,0:T(8,128)(2,1)S(1)}, bf16[32,192]{1,0:T(8,128)(2,1)S(1)}, u32[]{:S(2)}, u32[]{:S(2)}) collective-permute-start(bf16[32,192]{1,0:T(8,128)(2,1)S(1)} %get-tuple-element.13), channel_id=1, source_target_pairs={{0,1},{1,2},{2,3},{3,0},{4,5},{5,6},{6,7},{7,4},{8,9},{9,10},{10,1... | collective-permute-start | bytes 36872 | tf_op jit(solution)/shard_map/ppermute | solution.py:372
  6.8 0.8 %own_tile.1.merged = f32[256,384]{1,0:T(8,128)S(1)} custom-call(bf16[32,32,192]{2,1,0:T(8,128)(2,1)S(1)} %copy-done.3, bf16[3,3,192,384]{3,2,1,0:T(8,128)(2,1)S(1)} %copy-done), custom_call_target="tpu_custom_call" | custom-call | flops 1000000000 | bytes 1720320 | tf_op jit(solution)/shard_map/own_tile/pallas_call | solution.py:304
  7.6 0.0 collective-permute-done.2.corner
  7.6 0.5 %collective-permute-done.1.left = bf16[32,192]{1,0:T(8,128)(2,1)S(1)} collective-permute-done((bf16[32,192]{1,0:T(8,128)(2,1)S(1)}, bf16[32,192]{1,0:T(8,128)(2,1)S(1)}, u32[]{:S(2)}, u32[]{:S(2)}) %collective-permute-start.1) | collective-permute-done | bytes 12320 | tf_op jit(solution)/shard_map/ppermute | solution.py:372
  8.1 0.8 %collective-permute-done.upper = bf16[32,192]{1,0:T(8,128)(2,1)S(1)} collective-permute-done((bf16[32,192]{1,0:T(8,128)(2,1)S(1)}, bf16[32,192]{1,0:T(8,128)(2,1)S(1)}, u32[]{:S(2)}, u32[]{:S(2)}) %collective-permute-start) | collective-permute-done | bytes 12320 | tf_op jit(solution)/shard_map/ppermute | solution.py:371
  8.9 0.0 copy-done.6
  8.9 0.0 copy-done.7
  8.9 1.8 %merge.1 = (bf16[256,384]{1,0:T(8,128)(2,1)S(1)}, bf16[256,384]{1,0:T(8,128)(2,1)S(1)}, bf16[8,144,128]{2,1,0:T(8,128)(2,1)}) custom-call(f32[256,384]{1,0:T(8,128)S(1)} %own_tile.1.merged, bf16[32,192]{1,0:T(8,128)(2,1)S(1)} %collective-permute-done.upper, bf16[32,192]{1,0:T(8,128)(2,1)S(1)} %collective-permute-done.1.left, ...), custom_call_target="tpu_custom_call" | custom-call | flops 500000000 | bytes 2643456 | tf_op jit(solution)/shard_map/merge/pallas_call | solution.py:304
  10.8 6.1 %all-to-all-start = ((bf16[8,144,128]{2,1,0:T(8,128)(2,1)}), bf16[8,144,128]{2,1,0:T(8,128)(2,1)S(1)}, u32[]{:S(2)}, u32[]{:S(2)}) async-start(bf16[8,144,128]{2,1,0:T(8,128)(2,1)} %get-tuple-element.14), calls=%async_computation | async-start | bytes 589824 | tf_op jit(solution)/shard_map/all_to_all | solution.py:333
  16.9 0.4 %row_qkv.1 = (bf16[2,192,128]{2,1,0:T(8,128)(2,1)S(1)}, bf16[2,384,128]{2,1,0:T(8,128)(2,1)S(1)}) custom-call(bf16[256,384]{1,0:T(8,128)(2,1)S(1)} %get-tuple-element.15.normed, bf16[384,1152]{1,0:T(8,128)(2,1)S(1)} %copy-done.1), custom_call_target="tpu_custom_call" | custom-call | flops 300000000 | bytes 1081344 | tf_op jit(solution)/shard_map/row_qkv/pallas_call | solution.py:304
  17.3 0.0 copy-start.4
  17.3 0.0 copy-start.10
  17.3 0.1 collective-permute-start.5
  17.4 2.5 %collective-permute-start.4 = (bf16[2,384,128]{2,1,0:T(8,128)(2,1)S(1)}, bf16[2,384,128]{2,1,0:T(8,128)(2,1)S(1)}, u32[]{:S(2)}, u32[]{:S(2)}) collective-permute-start(bf16[2,384,128]{2,1,0:T(8,128)(2,1)S(1)} %get-tuple-element.17.refs_1_), channel_id=1, source_target_pairs={{0,2},{1,3},{2,0},{3,1},{4,6},{5,7},{6,4},{7,5},{8,10},{9,11},{10,... | collective-permute-start | bytes 589832 | tf_op jit(solution)/shard_map/ppermute | solution.py:325
  19.9 0.1 collective-permute-start.3
  20.0 4.4 %all-to-all-done.refs_0_ = bf16[8,144,128]{2,1,0:T(8,128)(2,1)S(1)} async-done(((bf16[8,144,128]{2,1,0:T(8,128)(2,1)}), bf16[8,144,128]{2,1,0:T(8,128)(2,1)S(1)}, u32[]{:S(2)}, u32[]{:S(2)}) %all-to-all-start) | async-done | bytes 294944 | tf_op jit(solution)/shard_map/all_to_all | solution.py:333
  24.5 3.4 %col_attention.1 = bf16[8,48,128]{2,1,0:T(8,128)(2,1)} custom-call(bf16[8,144,128]{2,1,0:T(8,128)(2,1)S(1)} %all-to-all-done.refs_0_), custom_call_target="tpu_custom_call" | custom-call | flops 2000000000 | bytes 294912 | tf_op jit(solution)/shard_map/col_attention/pallas_call | solution.py:304
  27.9 5.2 %all-to-all-start.1 = ((bf16[8,48,128]{2,1,0:T(8,128)(2,1)}), bf16[8,48,128]{2,1,0:T(8,128)(2,1)S(1)}, u32[]{:S(2)}, u32[]{:S(2)}) async-start(bf16[8,48,128]{2,1,0:T(8,128)(2,1)} %col_attention.1), calls=%async_computation.1 | async-start | bytes 196608 | tf_op jit(solution)/shard_map/all_to_all | solution.py:333
  33.1 0.0 collective-permute-done.5.refs_4_
  33.1 0.0 collective-permute-done.4.refs_3_
  33.1 0.0 collective-permute-done.3.refs_2_
  33.1 1.9 %row_attention.1.partial = f32[256,384]{1,0:T(8,128)S(1)} custom-call(bf16[2,192,128]{2,1,0:T(8,128)(2,1)S(1)} %get-tuple-element.16.refs_0_, bf16[2,384,128]{2,1,0:T(8,128)(2,1)S(1)} %get-tuple-element.17.refs_1_, bf16[2,384,128]{2,1,0:T(8,128)(2,1)S(1)} %collective-permute-done.3.refs_2_, bf16[2,384,128]{2,1,0:T(8,128)(2,1)S(1)} %collective-permute-done.4.refs_3_, ...), custom_call_target="tpu_custom_call" | custom-call | flops 2000000000 | bytes 1377792 | tf_op jit(solution)/shard_map/row_attention/pallas_call | solution.py:304
  35.1 1.7 %all-to-all-done.1.arrived = bf16[8,48,128]{2,1,0:T(8,128)(2,1)S(1)} async-done(((bf16[8,48,128]{2,1,0:T(8,128)(2,1)}), bf16[8,48,128]{2,1,0:T(8,128)(2,1)S(1)}, u32[]{:S(2)}, u32[]{:S(2)}) %all-to-all-start.1) | async-done | bytes 98336 | tf_op jit(solution)/shard_map/all_to_all | solution.py:333
  36.8 1.0 %output.1 = bf16[16,16,384]{2,1,0:T(8,128)(2,1)} custom-call(bf16[8,48,128]{2,1,0:T(8,128)(2,1)S(1)} %all-to-all-done.1.arrived, f32[256,384]{1,0:T(8,128)S(1)} %row_attention.1.partial, bf16[384,384]{1,0:T(8,128)(2,1)S(1)} %copy-done.4), custom_call_target="tpu_custom_call" | custom-call | flops 100000000 | bytes 786432 | tf_op jit(solution)/shard_map/output/pallas_call | solution.py:304
  (14 shorter events, 0.0 us)
Async XLA Ops:
  0.0 1.0 %copy-start.2 = (bf16[32,32,192]{2,1,0:T(8,128)(2,1)S(1)}, bf16[32,32,192]{2,1,0:T(8,128)(2,1)}, u32[]{:S(2)}) copy-start(bf16[32,32,192]{2,1,0:T(8,128)(2,1)} %image.3) | copy-start | bytes 1179652
  1.1 5.7 %copy-start = (bf16[3,3,192,384]{3,2,1,0:T(8,128)(2,1)S(1)}, bf16[3,3,192,384]{3,2,1,0:T(8,128)(2,1)}, u32[]{:S(2)}) copy-start(bf16[3,3,192,384]{3,2,1,0:T(8,128)(2,1)} %weight.4) | copy-start | bytes 3981316
  1.1 5.7 %copy-start.3 = (bf16[32,32,192]{2,1,0:T(8,128)(2,1)S(1)}, bf16[32,32,192]{2,1,0:T(8,128)(2,1)}, u32[]{:S(2)}) copy-start(bf16[32,32,192]{2,1,0:T(8,128)(2,1)} %image.3) | copy-start | bytes 1179652
  1.1 7.8 %collective-permute-start = (bf16[32,192]{1,0:T(8,128)(2,1)S(1)}, bf16[32,192]{1,0:T(8,128)(2,1)S(1)}, u32[]{:S(2)}, u32[]{:S(2)}) collective-permute-start(bf16[32,192]{1,0:T(8,128)(2,1)S(1)} %get-tuple-element.12.bottom), channel_id=1, source_target_pairs={{0,4},{4,8},{8,12},{12,16},{16,20},{20,24},{24,28},{28,0},{1,5},{5... | collective-permute-start | bytes 36872 | tf_op jit(solution)/shard_map/ppermute | solution.py:371
  4.2 3.4 %collective-permute-start.2 = (bf16[16,192]{1,0:T(8,128)(2,1)S(1)}, bf16[16,192]{1,0:T(8,128)(2,1)S(1)}, u32[]{:S(2)}, u32[]{:S(2)}) collective-permute-start(bf16[16,192]{1,0:T(8,128)(2,1)S(1)} %corner.1), channel_id=1, source_target_pairs={{0,5},{1,6},{2,7},{3,0},{4,9},{5,10},{6,11},{7,4},{8,13},{9,14},{1... | collective-permute-start | bytes 18440 | tf_op jit(solution)/shard_map/ppermute | solution.py:373
  4.8 4.1 %copy-start.1 = (bf16[384,1152]{1,0:T(8,128)(2,1)S(1)}, bf16[384,1152]{1,0:T(8,128)(2,1)}, u32[]{:S(2)}) copy-start(bf16[384,1152]{1,0:T(8,128)(2,1)} %qkv.3) | copy-start | bytes 2654212
  4.8 4.1 %copy-start.5 = (f32[384]{0:T(512)S(1)}, f32[384]{0:T(512)}, u32[]{:S(2)}) copy-start(f32[384]{0:T(512)} %bias.1) | copy-start | bytes 4612
  4.8 4.1 %copy-start.6 = (f32[384]{0:T(512)S(1)}, f32[384]{0:T(512)}, u32[]{:S(2)}) copy-start(f32[384]{0:T(512)} %gain.1) | copy-start | bytes 4612
  4.8 4.1 %copy-start.7 = (f32[384]{0:T(512)S(1)}, f32[384]{0:T(512)}, u32[]{:S(2)}) copy-start(f32[384]{0:T(512)} %shift.1) | copy-start | bytes 4612
  4.8 4.1 %copy-start.8 = (f32[384]{0:T(512)S(1)}, f32[384]{0:T(512)}, u32[]{:S(2)}) copy-start(f32[384]{0:T(512)} %gain2.1) | copy-start | bytes 4612
  4.9 4.1 %copy-start.9 = (f32[384]{0:T(512)S(1)}, f32[384]{0:T(512)}, u32[]{:S(2)}) copy-start(f32[384]{0:T(512)} %shift2.1) | copy-start | bytes 4612
  4.9 3.2 %collective-permute-start.1 = (bf16[32,192]{1,0:T(8,128)(2,1)S(1)}, bf16[32,192]{1,0:T(8,128)(2,1)S(1)}, u32[]{:S(2)}, u32[]{:S(2)}) collective-permute-start(bf16[32,192]{1,0:T(8,128)(2,1)S(1)} %get-tuple-element.13), channel_id=1, source_target_pairs={{0,1},{1,2},{2,3},{3,0},{4,5},{5,6},{6,7},{7,4},{8,9},{9,10},{10,1... | collective-permute-start | bytes 36872 | tf_op jit(solution)/shard_map/ppermute | solution.py:372
  10.8 13.7 %all-to-all-start = ((bf16[8,144,128]{2,1,0:T(8,128)(2,1)}), bf16[8,144,128]{2,1,0:T(8,128)(2,1)S(1)}, u32[]{:S(2)}, u32[]{:S(2)}) async-start(bf16[8,144,128]{2,1,0:T(8,128)(2,1)} %get-tuple-element.14), calls=%async_computation | async-start | bytes 589824 | tf_op jit(solution)/shard_map/all_to_all | solution.py:333
  17.3 15.8 %copy-start.4 = (bf16[384,384]{1,0:T(8,128)(2,1)S(1)}, bf16[384,384]{1,0:T(8,128)(2,1)}, u32[]{:S(2)}) copy-start(bf16[384,384]{1,0:T(8,128)(2,1)} %weight.5) | copy-start | bytes 884740
  17.3 15.8 %copy-start.10 = (f32[384]{0:T(512)S(1)}, f32[384]{0:T(512)}, u32[]{:S(2)}) copy-start(f32[384]{0:T(512)} %refs_7_.1) | copy-start | bytes 4612
  17.3 15.8 %collective-permute-start.5 = (bf16[2,384,128]{2,1,0:T(8,128)(2,1)S(1)}, bf16[2,384,128]{2,1,0:T(8,128)(2,1)S(1)}, u32[]{:S(2)}, u32[]{:S(2)}) collective-permute-start(bf16[2,384,128]{2,1,0:T(8,128)(2,1)S(1)} %get-tuple-element.17.refs_1_), channel_id=1, source_target_pairs={{0,1},{1,0},{2,3},{3,2},{4,5},{5,4},{6,7},{7,6},{8,9},{9,8},{10,11... | collective-permute-start | bytes 589832 | tf_op jit(solution)/shard_map/ppermute | solution.py:325
  17.4 15.7 %collective-permute-start.4 = (bf16[2,384,128]{2,1,0:T(8,128)(2,1)S(1)}, bf16[2,384,128]{2,1,0:T(8,128)(2,1)S(1)}, u32[]{:S(2)}, u32[]{:S(2)}) collective-permute-start(bf16[2,384,128]{2,1,0:T(8,128)(2,1)S(1)} %get-tuple-element.17.refs_1_), channel_id=1, source_target_pairs={{0,2},{1,3},{2,0},{3,1},{4,6},{5,7},{6,4},{7,5},{8,10},{9,11},{10,... | collective-permute-start | bytes 589832 | tf_op jit(solution)/shard_map/ppermute | solution.py:325
  19.9 13.2 %collective-permute-start.3 = (bf16[2,384,128]{2,1,0:T(8,128)(2,1)S(1)}, bf16[2,384,128]{2,1,0:T(8,128)(2,1)S(1)}, u32[]{:S(2)}, u32[]{:S(2)}) collective-permute-start(bf16[2,384,128]{2,1,0:T(8,128)(2,1)S(1)} %get-tuple-element.17.refs_1_), channel_id=1, source_target_pairs={{0,3},{1,2},{2,1},{3,0},{4,7},{5,6},{6,5},{7,4},{8,11},{9,10},{10,... | collective-permute-start | bytes 589832 | tf_op jit(solution)/shard_map/ppermute | solution.py:325
  27.9 8.9 %all-to-all-start.1 = ((bf16[8,48,128]{2,1,0:T(8,128)(2,1)}), bf16[8,48,128]{2,1,0:T(8,128)(2,1)S(1)}, u32[]{:S(2)}, u32[]{:S(2)}) async-start(bf16[8,48,128]{2,1,0:T(8,128)(2,1)} %col_attention.1), calls=%async_computation.1 | async-start | bytes 196608 | tf_op jit(solution)/shard_map/all_to_all | solution.py:333

commit v5 on v4

--- a/solution.py
+++ b/solution.py
@@ -48,20 +48,13 @@
     )
 
 
-def unless_last(value, axis):
-    last = lax.axis_index(axis) == lax.axis_size(axis) - 1
-    return jnp.where(last, jnp.zeros_like(value), value)
-
-
-def edge_kernel(image, bottom, side):
-    rows, cols, _ = image.shape
+def edge_kernel(image, side):
     near = 2 * SPLIT
-    bottom[...] = unless_last(image[rows - 1], "row")
-    side[...] = unless_last(image[:, cols - near :].astype(F32)[:, near - 1], "col").astype(BF16)
+    side[...] = image[:, image.shape[1] - near :].astype(F32)[:, near - 1].astype(BF16)
 
 
 def corner_kernel(bottom, corner):
-    corner[...] = unless_last(bottom[bottom.shape[0] - corner.shape[0] :], "col")
+    corner[...] = bottom[bottom.shape[0] - corner.shape[0] :]
 
 
 def own_kernel(image, weight, merged, pixels):
@@ -86,6 +79,10 @@
     merged[...] = total
 
 
+def kept(value, axis):
+    return jnp.where(lax.axis_index(axis) == 0, jnp.zeros(value.shape, F32), value.astype(F32))
+
+
 def merge_kernel(
     merged, upper, left, corner, weight, qkv, bias, gain, shift, gain2, shift2, tokens, normed, chunks, edges, held_chunks, sems
 ):
@@ -98,9 +95,9 @@
     row = lambda ref: ref[...].reshape(1, width)
     for part, start, size in lane_parts(channels):
         lanes, here = pl.ds(0, size), pl.ds(start, size)
-        edges[part, 0, pl.ds(first, in_cols), lanes] = upper[:, here].astype(F32)
-        edges[part, 0, pl.ds(first - 1, 1), lanes] = corner[:, here].astype(F32)[corner.shape[0] - 1 :]
-        edges[part, 1, pl.ds(first, in_rows), lanes] = left[:, here].astype(F32)
+        edges[part, 0, pl.ds(first, in_cols), lanes] = kept(upper[:, here], "row")
+        edges[part, 0, pl.ds(first - 1, 1), lanes] = kept(kept(corner[:, here], "row")[corner.shape[0] - 1 :], "col")
+        edges[part, 1, pl.ds(first, in_rows), lanes] = kept(left[:, here], "col")
         edges[part, 1, pl.ds(first - 1, 1), lanes] = jnp.zeros((1, size), F32)
     above = [every_second(edges, (0,), first - 1 + tap, cols, channels).astype(BF16) for tap in range(3)]
     aside = [every_second(edges, (1,), first - 1 + tap, rows, channels).astype(BF16) for tap in range(3)]
@@ -205,7 +202,12 @@
     per = lines // (3 * depth)
     total = per * depth
     lanes = jnp.concatenate([arrived[s].astype(F32) for s in range(count)], 1)
-    key_rows = lanes[total : 2 * total].astype(BF16).T
+    rest = lanes[total : 2 * total] * (math.log2(math.e) / math.sqrt(depth))
+    key_rows = []
+    for _ in range(3):
+        key_rows.append(rest.astype(BF16).astype(F32))
+        rest = rest - key_rows[-1]
+    key_rows = jnp.concatenate(key_rows, 0).T.astype(BF16)
     values = [
         with_sum_row(lanes[2 * total + h * depth : 2 * total + (h + 1) * depth]) for h in range(per)
     ]
@@ -216,12 +218,13 @@
     def score(item):
         begin, h = item
         queries = padded_rows(lanes[h * depth : (h + 1) * depth, begin : begin + block], h * depth, total)
-        scores = dot(key_rows, queries.astype(BF16))
+        scores = dot(key_rows, jnp.concatenate([queries] * 3, 0).astype(BF16))
         return scores, jnp.max(scores, 0, keepdims=True)
 
     def finish(item, scores, highest):
         begin, h = item
-        heads.append(attended(dot(values[h], weights_of(scores, highest, depth)), depth))
+        probs = jnp.exp2(scores - highest).astype(BF16)
+        heads.append(attended(dot(values[h], probs), depth))
         if h == per - 1:
             both = jnp.concatenate(heads, 0).astype(BF16)
             heads.clear()
@@ -229,7 +232,7 @@
                 done[k] = both[:, k * length - begin : (k + 1) * length - begin]
                 copies[k].start()
 
-    ahead_of([(begin, h) for begin in range(0, count * length, block) for h in range(per)], score, finish, 3)
+    ahead_of([(begin, h) for begin in range(0, count * length, block) for h in range(per)], score, finish, 4)
     for copy in copies:
         copy.wait()
 
@@ -359,18 +362,13 @@
         for c in range(col_count):
             target = (r, 0) if c == col_count - 1 else ((r + 1) % row_count, c + 1)
             diagonal.append((r * col_count + c, target[0] * col_count + target[1]))
+    bottom = image[in_rows - 1]
     near = 2 * SPLIT
-    bottom, side = call(
-        edge_kernel,
-        "edge",
-        (shape((in_cols, channels)), shape((in_rows, channels))),
-        (image,),
-        10**5,
-    )
-    corner = call(corner_kernel, "corner", shape((near, channels)), (bottom,), 10**10)
+    tail = call(corner_kernel, "corner", shape((near, channels)), (bottom,), 10**10)
+    side = call(edge_kernel, "edge", shape((in_rows, channels)), (image,), 10**5)
     upper = lax.ppermute(bottom, "row", down)
     left = lax.ppermute(side, "col", right)
-    corner = lax.ppermute(corner, ("row", "col"), diagonal)
+    corner = lax.ppermute(tail, ("row", "col"), diagonal)
     pixel_parts = -(-channels // LANES)
     merged = call(
         own_kernel,

time: 38 us -> 37.5 us (0.987)
    unnamed x22 -> x20, local copies, waits for them, and re-layouts: 1.09 us -> 0.06 us
    squeeze x0 -> x1, local copies, waits for them, and re-layouts: none -> 0.72 us  [on_device(): bottom = image[in_rows - 1]]
where the time goes in v5:
time: 37.5 us; the launch traced here: 37.1 us
  starting transfers between devices  19.6 us (52%)
  Pallas kernels  9.19 us (25%)
  waiting for transfers between devices  7.44 us (20%)
  local copies, waits for them, and re-layouts  0.78 us (2%)
    all_to_all x2, starting transfers between devices, exchanged(): lax.all_to_all(value, axis, 0, 0, axis_index_groups=[order], tiled=True)  11.4 us
    pallas_call x8, Pallas kernels, call(): pl.pallas_call(kernel, out_shape=out_shape, in_specs=vmem(len(args)), out...  9.19 us
    all_to_all x2, waiting for transfers between devices, exchanged(): lax.all_to_all(value, axis, 0, 0, axis_index_groups=[order], tiled=True)  6.2 us
    ppermute x1, starting transfers between devices, on_device(): upper = lax.ppermute(bottom, 'row', down)  2.97 us
    ppermute x3, starting transfers between devices, gathered(): held.append(lax.ppermute(value, axis, pairs))  2.6 us
    ppermute x1, starting transfers between devices, on_device(): left = lax.ppermute(side, 'col', right)  1.93 us
  transfers between devices with their start and end apart: 8, of which 4 were waited for; matrix products, arithmetic and copies ran while one was open for 0% of the time, Pallas kernels for 17%

profile of v5, /device:TPU:0, one launch (start us, length us, event | category | flops | bytes accessed | tf_op | source)
XLA Modules:
  0.0 37.1 jit_solution(15042054764308641489)
XLA Ops:
  0.0 0.7 %slice_bitcast_fusion.bottom = bf16[32,192]{1,0:T(8,128)(2,1)S(1)} fusion(bf16[32,32,192]{2,1,0:T(8,128)(2,1)} %image.3), kind=kLoop, calls=%fused_computation | loop fusion | bytes 24576 | tf_op jit(solution)/shard_map/squeeze | solution.py:365
  0.7 3.0 %collective-permute-start = (bf16[32,192]{1,0:T(8,128)(2,1)S(1)}, bf16[32,192]{1,0:T(8,128)(2,1)S(1)}, u32[]{:S(2)}, u32[]{:S(2)}) collective-permute-start(bf16[32,192]{1,0:T(8,128)(2,1)S(1)} %slice_bitcast_fusion.bottom), channel_id=1, source_target_pairs={{0,4},{4,8},{8,12},{12,16},{16,20},{20,24},{24,28},{28,0},{1,5},{5... | collective-permute-start | bytes 36872 | tf_op jit(solution)/shard_map/ppermute | solution.py:369
  3.7 0.7 %collective-permute-start.2 = (bf16[16,192]{1,0:T(8,128)(2,1)S(1)}, bf16[16,192]{1,0:T(8,128)(2,1)S(1)}, u32[]{:S(2)}, u32[]{:S(2)}) collective-permute-start(bf16[16,192]{1,0:T(8,128)(2,1)S(1)} %corner.1), channel_id=1, source_target_pairs={{0,5},{1,6},{2,7},{3,0},{4,9},{5,10},{6,11},{7,4},{8,13},{9,14},{1... | collective-permute-start | bytes 18440 | tf_op jit(solution)/shard_map/ppermute | solution.py:371
  4.4 0.0 copy-start.1
  4.4 0.0 copy-start.4
  4.4 0.0 copy-start.5
  4.5 0.0 copy-start.6
  4.5 0.0 copy-start.7
  4.5 0.0 copy-start.8
  4.5 1.9 %collective-permute-start.1 = (bf16[32,192]{1,0:T(8,128)(2,1)S(1)}, bf16[32,192]{1,0:T(8,128)(2,1)S(1)}, u32[]{:S(2)}, u32[]{:S(2)}) collective-permute-start(bf16[32,192]{1,0:T(8,128)(2,1)S(1)} %edge.1), channel_id=1, source_target_pairs={{0,1},{1,2},{2,3},{3,0},{4,5},{5,6},{6,7},{7,4},{8,9},{9,10},{10,1... | collective-permute-start | bytes 36872 | tf_op jit(solution)/shard_map/ppermute | solution.py:370
  6.4 0.8 %own_tile.1.merged = f32[256,384]{1,0:T(8,128)S(1)} custom-call(bf16[32,32,192]{2,1,0:T(8,128)(2,1)S(1)} %copy-done.2, bf16[3,3,192,384]{3,2,1,0:T(8,128)(2,1)S(1)} %copy-done), custom_call_target="tpu_custom_call" | custom-call | flops 1000000000 | bytes 1720320 | tf_op jit(solution)/shard_map/own_tile/pallas_call | solution.py:307
  7.2 0.0 collective-permute-done.2.corner
  7.2 0.5 %collective-permute-done.1.left = bf16[32,192]{1,0:T(8,128)(2,1)S(1)} collective-permute-done((bf16[32,192]{1,0:T(8,128)(2,1)S(1)}, bf16[32,192]{1,0:T(8,128)(2,1)S(1)}, u32[]{:S(2)}, u32[]{:S(2)}) %collective-permute-start.1) | collective-permute-done | bytes 12320 | tf_op jit(solution)/shard_map/ppermute | solution.py:370
  7.7 0.7 %collective-permute-done.upper = bf16[32,192]{1,0:T(8,128)(2,1)S(1)} collective-permute-done((bf16[32,192]{1,0:T(8,128)(2,1)S(1)}, bf16[32,192]{1,0:T(8,128)(2,1)S(1)}, u32[]{:S(2)}, u32[]{:S(2)}) %collective-permute-start) | collective-permute-done | bytes 12320 | tf_op jit(solution)/shard_map/ppermute | solution.py:369
  8.4 0.0 copy-done.1
  8.5 1.8 %merge.1 = (bf16[256,384]{1,0:T(8,128)(2,1)S(1)}, bf16[256,384]{1,0:T(8,128)(2,1)S(1)}, bf16[8,144,128]{2,1,0:T(8,128)(2,1)}) custom-call(f32[256,384]{1,0:T(8,128)S(1)} %own_tile.1.merged, bf16[32,192]{1,0:T(8,128)(2,1)S(1)} %collective-permute-done.upper, bf16[32,192]{1,0:T(8,128)(2,1)S(1)} %collective-permute-done.1.left, ...), custom_call_target="tpu_custom_call" | custom-call | flops 500000000 | bytes 2643456 | tf_op jit(solution)/shard_map/merge/pallas_call | solution.py:307
  10.3 6.2 %all-to-all-start = ((bf16[8,144,128]{2,1,0:T(8,128)(2,1)}), bf16[8,144,128]{2,1,0:T(8,128)(2,1)S(1)}, u32[]{:S(2)}, u32[]{:S(2)}) async-start(bf16[8,144,128]{2,1,0:T(8,128)(2,1)} %get-tuple-element.10), calls=%async_computation | async-start | bytes 589824 | tf_op jit(solution)/shard_map/all_to_all | solution.py:336
  16.5 0.4 %row_qkv.1 = (bf16[2,192,128]{2,1,0:T(8,128)(2,1)S(1)}, bf16[2,384,128]{2,1,0:T(8,128)(2,1)S(1)}) custom-call(bf16[256,384]{1,0:T(8,128)(2,1)S(1)} %get-tuple-element.11.normed, bf16[384,1152]{1,0:T(8,128)(2,1)S(1)} %copy-done.1), custom_call_target="tpu_custom_call" | custom-call | flops 300000000 | bytes 1081344 | tf_op jit(solution)/shard_map/row_qkv/pallas_call | solution.py:307
  16.9 0.0 copy-start.3
  16.9 0.0 copy-start.9
  16.9 0.1 collective-permute-start.5
  17.0 2.5 %collective-permute-start.4 = (bf16[2,384,128]{2,1,0:T(8,128)(2,1)S(1)}, bf16[2,384,128]{2,1,0:T(8,128)(2,1)S(1)}, u32[]{:S(2)}, u32[]{:S(2)}) collective-permute-start(bf16[2,384,128]{2,1,0:T(8,128)(2,1)S(1)} %get-tuple-element.13.refs_1_), channel_id=1, source_target_pairs={{0,2},{1,3},{2,0},{3,1},{4,6},{5,7},{6,4},{7,5},{8,10},{9,11},{10,... | collective-permute-start | bytes 589832 | tf_op jit(solution)/shard_map/ppermute | solution.py:328
  19.5 0.1 collective-permute-start.3
  19.5 4.5 %all-to-all-done.refs_0_ = bf16[8,144,128]{2,1,0:T(8,128)(2,1)S(1)} async-done(((bf16[8,144,128]{2,1,0:T(8,128)(2,1)}), bf16[8,144,128]{2,1,0:T(8,128)(2,1)S(1)}, u32[]{:S(2)}, u32[]{:S(2)}) %all-to-all-start) | async-done | bytes 294944 | tf_op jit(solution)/shard_map/all_to_all | solution.py:336
  24.1 3.2 %col_attention.1 = bf16[8,48,128]{2,1,0:T(8,128)(2,1)} custom-call(bf16[8,144,128]{2,1,0:T(8,128)(2,1)S(1)} %all-to-all-done.refs_0_), custom_call_target="tpu_custom_call" | custom-call | flops 2000000000 | bytes 294912 | tf_op jit(solution)/shard_map/col_attention/pallas_call | solution.py:307
  27.3 5.2 %all-to-all-start.1 = ((bf16[8,48,128]{2,1,0:T(8,128)(2,1)}), bf16[8,48,128]{2,1,0:T(8,128)(2,1)S(1)}, u32[]{:S(2)}, u32[]{:S(2)}) async-start(bf16[8,48,128]{2,1,0:T(8,128)(2,1)} %col_attention.1), calls=%async_computation.1 | async-start | bytes 196608 | tf_op jit(solution)/shard_map/all_to_all | solution.py:336
  32.5 0.0 collective-permute-done.5.refs_4_
  32.5 0.0 collective-permute-done.4.refs_3_
  32.5 0.0 collective-permute-done.3.refs_2_
  32.6 1.9 %row_attention.1.partial = f32[256,384]{1,0:T(8,128)S(1)} custom-call(bf16[2,192,128]{2,1,0:T(8,128)(2,1)S(1)} %get-tuple-element.12.refs_0_, bf16[2,384,128]{2,1,0:T(8,128)(2,1)S(1)} %get-tuple-element.13.refs_1_, bf16[2,384,128]{2,1,0:T(8,128)(2,1)S(1)} %collective-permute-done.3.refs_2_, bf16[2,384,128]{2,1,0:T(8,128)(2,1)S(1)} %collective-permute-done.4.refs_3_, ...), custom_call_target="tpu_custom_call" | custom-call | flops 2000000000 | bytes 1377792 | tf_op jit(solution)/shard_map/row_attention/pallas_call | solution.py:307
  34.5 1.7 %all-to-all-done.1.arrived = bf16[8,48,128]{2,1,0:T(8,128)(2,1)S(1)} async-done(((bf16[8,48,128]{2,1,0:T(8,128)(2,1)}), bf16[8,48,128]{2,1,0:T(8,128)(2,1)S(1)}, u32[]{:S(2)}, u32[]{:S(2)}) %all-to-all-start.1) | async-done | bytes 98336 | tf_op jit(solution)/shard_map/all_to_all | solution.py:336
  36.2 1.0 %output.1 = bf16[16,16,384]{2,1,0:T(8,128)(2,1)} custom-call(bf16[8,48,128]{2,1,0:T(8,128)(2,1)S(1)} %all-to-all-done.1.arrived, f32[256,384]{1,0:T(8,128)S(1)} %row_attention.1.partial, bf16[384,384]{1,0:T(8,128)(2,1)S(1)} %copy-done.3), custom_call_target="tpu_custom_call" | custom-call | flops 100000000 | bytes 786432 | tf_op jit(solution)/shard_map/output/pallas_call | solution.py:307
  (13 shorter events, 0.1 us)
Async XLA Ops:
  0.7 3.7 %copy-start.2 = (bf16[32,32,192]{2,1,0:T(8,128)(2,1)S(1)}, bf16[32,32,192]{2,1,0:T(8,128)(2,1)}, u32[]{:S(2)}) copy-start(bf16[32,32,192]{2,1,0:T(8,128)(2,1)} %image.3) | copy-start | bytes 1179652
  0.7 5.7 %copy-start = (bf16[3,3,192,384]{3,2,1,0:T(8,128)(2,1)S(1)}, bf16[3,3,192,384]{3,2,1,0:T(8,128)(2,1)}, u32[]{:S(2)}) copy-start(bf16[3,3,192,384]{3,2,1,0:T(8,128)(2,1)} %weight.4) | copy-start | bytes 3981316
  0.7 7.7 %collective-permute-start = (bf16[32,192]{1,0:T(8,128)(2,1)S(1)}, bf16[32,192]{1,0:T(8,128)(2,1)S(1)}, u32[]{:S(2)}, u32[]{:S(2)}) collective-permute-start(bf16[32,192]{1,0:T(8,128)(2,1)S(1)} %slice_bitcast_fusion.bottom), channel_id=1, source_target_pairs={{0,4},{4,8},{8,12},{12,16},{16,20},{20,24},{24,28},{28,0},{1,5},{5... | collective-permute-start | bytes 36872 | tf_op jit(solution)/shard_map/ppermute | solution.py:369
  3.7 3.5 %collective-permute-start.2 = (bf16[16,192]{1,0:T(8,128)(2,1)S(1)}, bf16[16,192]{1,0:T(8,128)(2,1)S(1)}, u32[]{:S(2)}, u32[]{:S(2)}) collective-permute-start(bf16[16,192]{1,0:T(8,128)(2,1)S(1)} %corner.1), channel_id=1, source_target_pairs={{0,5},{1,6},{2,7},{3,0},{4,9},{5,10},{6,11},{7,4},{8,13},{9,14},{1... | collective-permute-start | bytes 18440 | tf_op jit(solution)/shard_map/ppermute | solution.py:371
  4.4 4.0 %copy-start.1 = (bf16[384,1152]{1,0:T(8,128)(2,1)S(1)}, bf16[384,1152]{1,0:T(8,128)(2,1)}, u32[]{:S(2)}) copy-start(bf16[384,1152]{1,0:T(8,128)(2,1)} %qkv.3) | copy-start | bytes 2654212
  4.4 4.0 %copy-start.4 = (f32[384]{0:T(512)S(1)}, f32[384]{0:T(512)}, u32[]{:S(2)}) copy-start(f32[384]{0:T(512)} %bias.1) | copy-start | bytes 4612
  4.4 4.0 %copy-start.5 = (f32[384]{0:T(512)S(1)}, f32[384]{0:T(512)}, u32[]{:S(2)}) copy-start(f32[384]{0:T(512)} %gain.1) | copy-start | bytes 4612
  4.5 4.0 %copy-start.6 = (f32[384]{0:T(512)S(1)}, f32[384]{0:T(512)}, u32[]{:S(2)}) copy-start(f32[384]{0:T(512)} %shift.1) | copy-start | bytes 4612
  4.5 4.0 %copy-start.7 = (f32[384]{0:T(512)S(1)}, f32[384]{0:T(512)}, u32[]{:S(2)}) copy-start(f32[384]{0:T(512)} %gain2.1) | copy-start | bytes 4612
  4.5 4.0 %copy-start.8 = (f32[384]{0:T(512)S(1)}, f32[384]{0:T(512)}, u32[]{:S(2)}) copy-start(f32[384]{0:T(512)} %shift2.1) | copy-start | bytes 4612
  4.5 3.2 %collective-permute-start.1 = (bf16[32,192]{1,0:T(8,128)(2,1)S(1)}, bf16[32,192]{1,0:T(8,128)(2,1)S(1)}, u32[]{:S(2)}, u32[]{:S(2)}) collective-permute-start(bf16[32,192]{1,0:T(8,128)(2,1)S(1)} %edge.1), channel_id=1, source_target_pairs={{0,1},{1,2},{2,3},{3,0},{4,5},{5,6},{6,7},{7,4},{8,9},{9,10},{10,1... | collective-permute-start | bytes 36872 | tf_op jit(solution)/shard_map/ppermute | solution.py:370
  10.3 13.7 %all-to-all-start = ((bf16[8,144,128]{2,1,0:T(8,128)(2,1)}), bf16[8,144,128]{2,1,0:T(8,128)(2,1)S(1)}, u32[]{:S(2)}, u32[]{:S(2)}) async-start(bf16[8,144,128]{2,1,0:T(8,128)(2,1)} %get-tuple-element.10), calls=%async_computation | async-start | bytes 589824 | tf_op jit(solution)/shard_map/all_to_all | solution.py:336
  16.9 15.6 %copy-start.3 = (bf16[384,384]{1,0:T(8,128)(2,1)S(1)}, bf16[384,384]{1,0:T(8,128)(2,1)}, u32[]{:S(2)}) copy-start(bf16[384,384]{1,0:T(8,128)(2,1)} %weight.5) | copy-start | bytes 884740
  16.9 15.6 %copy-start.9 = (f32[384]{0:T(512)S(1)}, f32[384]{0:T(512)}, u32[]{:S(2)}) copy-start(f32[384]{0:T(512)} %refs_7_.1) | copy-start | bytes 4612
  16.9 15.6 %collective-permute-start.5 = (bf16[2,384,128]{2,1,0:T(8,128)(2,1)S(1)}, bf16[2,384,128]{2,1,0:T(8,128)(2,1)S(1)}, u32[]{:S(2)}, u32[]{:S(2)}) collective-permute-start(bf16[2,384,128]{2,1,0:T(8,128)(2,1)S(1)} %get-tuple-element.13.refs_1_), channel_id=1, source_target_pairs={{0,1},{1,0},{2,3},{3,2},{4,5},{5,4},{6,7},{7,6},{8,9},{9,8},{10,11... | collective-permute-start | bytes 589832 | tf_op jit(solution)/shard_map/ppermute | solution.py:328
  17.0 15.5 %collective-permute-start.4 = (bf16[2,384,128]{2,1,0:T(8,128)(2,1)S(1)}, bf16[2,384,128]{2,1,0:T(8,128)(2,1)S(1)}, u32[]{:S(2)}, u32[]{:S(2)}) collective-permute-start(bf16[2,384,128]{2,1,0:T(8,128)(2,1)S(1)} %get-tuple-element.13.refs_1_), channel_id=1, source_target_pairs={{0,2},{1,3},{2,0},{3,1},{4,6},{5,7},{6,4},{7,5},{8,10},{9,11},{10,... | collective-permute-start | bytes 589832 | tf_op jit(solution)/shard_map/ppermute | solution.py:328
  19.5 13.1 %collective-permute-start.3 = (bf16[2,384,128]{2,1,0:T(8,128)(2,1)S(1)}, bf16[2,384,128]{2,1,0:T(8,128)(2,1)S(1)}, u32[]{:S(2)}, u32[]{:S(2)}) collective-permute-start(bf16[2,384,128]{2,1,0:T(8,128)(2,1)S(1)} %get-tuple-element.13.refs_1_), channel_id=1, source_target_pairs={{0,3},{1,2},{2,1},{3,0},{4,7},{5,6},{6,5},{7,4},{8,11},{9,10},{10,... | collective-permute-start | bytes 589832 | tf_op jit(solution)/shard_map/ppermute | solution.py:328
  27.3 8.9 %all-to-all-start.1 = ((bf16[8,48,128]{2,1,0:T(8,128)(2,1)}), bf16[8,48,128]{2,1,0:T(8,128)(2,1)S(1)}, u32[]{:S(2)}, u32[]{:S(2)}) async-start(bf16[8,48,128]{2,1,0:T(8,128)(2,1)} %col_attention.1), calls=%async_computation.1 | async-start | bytes 196608 | tf_op jit(solution)/shard_map/all_to_all | solution.py:336

commit v6 on v5

--- a/solution.py
+++ b/solution.py
@@ -331,7 +331,7 @@
 
 def exchanged(value, axis):
     count = lax.axis_size(axis)
-    lead = 5 * count // 8
+    lead = count // 4
     order = [lead] + [k for k in range(count) if k != lead]
     return lax.all_to_all(value, axis, 0, 0, axis_index_groups=[order], tiled=True)
 

time: 37.5 us -> 37.4 us (level)
  starting transfers between devices: 19.6 us -> 16.2 us
  waiting for transfers between devices: 7.44 us -> 10.6 us
    all_to_all x2, starting transfers between devices: 11.4 us -> 7.99 us  [exchanged(): lax.all_to_all(value, axis, 0, 0, axis_index_groups=[order], tiled=True)]
    all_to_all x2, waiting for transfers between devices: 6.2 us -> 9.39 us  [exchanged(): lax.all_to_all(value, axis, 0, 0, axis_index_groups=[order], tiled=True)]
where the time goes in v6:
time: 37.4 us; the launch traced here: 37 us
  starting transfers between devices  16.2 us (43%)
  waiting for transfers between devices  10.6 us (28%)
  Pallas kernels  9.2 us (25%)
  local copies, waits for them, and re-layouts  0.78 us (2%)
    all_to_all x2, waiting for transfers between devices, exchanged(): lax.all_to_all(value, axis, 0, 0, axis_index_groups=[order], tiled=True)  9.39 us
    pallas_call x8, Pallas kernels, call(): pl.pallas_call(kernel, out_shape=out_shape, in_specs=vmem(len(args)), out...  9.2 us
    all_to_all x2, starting transfers between devices, exchanged(): lax.all_to_all(value, axis, 0, 0, axis_index_groups=[order], tiled=True)  7.99 us
    ppermute x1, starting transfers between devices, on_device(): upper = lax.ppermute(bottom, 'row', down)  2.97 us
    ppermute x3, starting transfers between devices, gathered(): held.append(lax.ppermute(value, axis, pairs))  2.63 us
    ppermute x1, starting transfers between devices, on_device(): left = lax.ppermute(side, 'col', right)  1.93 us
  transfers between devices with their start and end apart: 8, of which 4 were waited for; matrix products, arithmetic and copies ran while one was open for 0% of the time, Pallas kernels for 17%

profile of v6, /device:TPU:0, one launch (start us, length us, event | category | flops | bytes accessed | tf_op | source)
XLA Modules:
  0.0 37.0 jit_solution(14654902843062512744)
XLA Ops:
  0.0 0.7 %slice_bitcast_fusion.bottom = bf16[32,192]{1,0:T(8,128)(2,1)S(1)} fusion(bf16[32,32,192]{2,1,0:T(8,128)(2,1)} %image.3), kind=kLoop, calls=%fused_computation | loop fusion | bytes 24576 | tf_op jit(solution)/shard_map/squeeze | solution.py:365
  0.7 3.0 %collective-permute-start = (bf16[32,192]{1,0:T(8,128)(2,1)S(1)}, bf16[32,192]{1,0:T(8,128)(2,1)S(1)}, u32[]{:S(2)}, u32[]{:S(2)}) collective-permute-start(bf16[32,192]{1,0:T(8,128)(2,1)S(1)} %slice_bitcast_fusion.bottom), channel_id=1, source_target_pairs={{0,4},{4,8},{8,12},{12,16},{16,20},{20,24},{24,28},{28,0},{1,5},{5... | collective-permute-start | bytes 36872 | tf_op jit(solution)/shard_map/ppermute | solution.py:369
  3.7 0.7 %collective-permute-start.2 = (bf16[16,192]{1,0:T(8,128)(2,1)S(1)}, bf16[16,192]{1,0:T(8,128)(2,1)S(1)}, u32[]{:S(2)}, u32[]{:S(2)}) collective-permute-start(bf16[16,192]{1,0:T(8,128)(2,1)S(1)} %corner.1), channel_id=1, source_target_pairs={{0,5},{1,6},{2,7},{3,0},{4,9},{5,10},{6,11},{7,4},{8,13},{9,14},{1... | collective-permute-start | bytes 18440 | tf_op jit(solution)/shard_map/ppermute | solution.py:371
  4.4 0.0 copy-start.1
  4.4 0.0 copy-start.4
  4.4 0.0 copy-start.5
  4.5 0.0 copy-start.6
  4.5 0.0 copy-start.7
  4.5 0.0 copy-start.8
  4.5 1.9 %collective-permute-start.1 = (bf16[32,192]{1,0:T(8,128)(2,1)S(1)}, bf16[32,192]{1,0:T(8,128)(2,1)S(1)}, u32[]{:S(2)}, u32[]{:S(2)}) collective-permute-start(bf16[32,192]{1,0:T(8,128)(2,1)S(1)} %edge.1), channel_id=1, source_target_pairs={{0,1},{1,2},{2,3},{3,0},{4,5},{5,6},{6,7},{7,4},{8,9},{9,10},{10,1... | collective-permute-start | bytes 36872 | tf_op jit(solution)/shard_map/ppermute | solution.py:370
  6.4 0.8 %own_tile.1.merged = f32[256,384]{1,0:T(8,128)S(1)} custom-call(bf16[32,32,192]{2,1,0:T(8,128)(2,1)S(1)} %copy-done.2, bf16[3,3,192,384]{3,2,1,0:T(8,128)(2,1)S(1)} %copy-done), custom_call_target="tpu_custom_call" | custom-call | flops 1000000000 | bytes 1720320 | tf_op jit(solution)/shard_map/own_tile/pallas_call | solution.py:307
  7.2 0.0 collective-permute-done.2.corner
  7.2 0.5 %collective-permute-done.1.left = bf16[32,192]{1,0:T(8,128)(2,1)S(1)} collective-permute-done((bf16[32,192]{1,0:T(8,128)(2,1)S(1)}, bf16[32,192]{1,0:T(8,128)(2,1)S(1)}, u32[]{:S(2)}, u32[]{:S(2)}) %collective-permute-start.1) | collective-permute-done | bytes 12320 | tf_op jit(solution)/shard_map/ppermute | solution.py:370
  7.7 0.7 %collective-permute-done.upper = bf16[32,192]{1,0:T(8,128)(2,1)S(1)} collective-permute-done((bf16[32,192]{1,0:T(8,128)(2,1)S(1)}, bf16[32,192]{1,0:T(8,128)(2,1)S(1)}, u32[]{:S(2)}, u32[]{:S(2)}) %collective-permute-start) | collective-permute-done | bytes 12320 | tf_op jit(solution)/shard_map/ppermute | solution.py:369
  8.5 1.8 %merge.1 = (bf16[256,384]{1,0:T(8,128)(2,1)S(1)}, bf16[256,384]{1,0:T(8,128)(2,1)S(1)}, bf16[8,144,128]{2,1,0:T(8,128)(2,1)}) custom-call(f32[256,384]{1,0:T(8,128)S(1)} %own_tile.1.merged, bf16[32,192]{1,0:T(8,128)(2,1)S(1)} %collective-permute-done.upper, bf16[32,192]{1,0:T(8,128)(2,1)S(1)} %collective-permute-done.1.left, ...), custom_call_target="tpu_custom_call" | custom-call | flops 500000000 | bytes 2643456 | tf_op jit(solution)/shard_map/merge/pallas_call | solution.py:307
  10.3 4.7 %all-to-all-start = ((bf16[8,144,128]{2,1,0:T(8,128)(2,1)}), bf16[8,144,128]{2,1,0:T(8,128)(2,1)S(1)}, u32[]{:S(2)}, u32[]{:S(2)}) async-start(bf16[8,144,128]{2,1,0:T(8,128)(2,1)} %get-tuple-element.10), calls=%async_computation | async-start | bytes 589824 | tf_op jit(solution)/shard_map/all_to_all | solution.py:336
  15.0 0.4 %row_qkv.1 = (bf16[2,192,128]{2,1,0:T(8,128)(2,1)S(1)}, bf16[2,384,128]{2,1,0:T(8,128)(2,1)S(1)}) custom-call(bf16[256,384]{1,0:T(8,128)(2,1)S(1)} %get-tuple-element.11.normed, bf16[384,1152]{1,0:T(8,128)(2,1)S(1)} %copy-done.1), custom_call_target="tpu_custom_call" | custom-call | flops 300000000 | bytes 1081344 | tf_op jit(solution)/shard_map/row_qkv/pallas_call | solution.py:307
  15.4 0.0 copy-start.3
  15.4 0.0 copy-start.9
  15.4 0.1 collective-permute-start.5
  15.5 2.5 %collective-permute-start.4 = (bf16[2,384,128]{2,1,0:T(8,128)(2,1)S(1)}, bf16[2,384,128]{2,1,0:T(8,128)(2,1)S(1)}, u32[]{:S(2)}, u32[]{:S(2)}) collective-permute-start(bf16[2,384,128]{2,1,0:T(8,128)(2,1)S(1)} %get-tuple-element.13.refs_1_), channel_id=1, source_target_pairs={{0,2},{1,3},{2,0},{3,1},{4,6},{5,7},{6,4},{7,5},{8,10},{9,11},{10,... | collective-permute-start | bytes 589832 | tf_op jit(solution)/shard_map/ppermute | solution.py:328
  18.0 0.1 collective-permute-start.3
  18.1 6.0 %all-to-all-done.refs_0_ = bf16[8,144,128]{2,1,0:T(8,128)(2,1)S(1)} async-done(((bf16[8,144,128]{2,1,0:T(8,128)(2,1)}), bf16[8,144,128]{2,1,0:T(8,128)(2,1)S(1)}, u32[]{:S(2)}, u32[]{:S(2)}) %all-to-all-start) | async-done | bytes 294944 | tf_op jit(solution)/shard_map/all_to_all | solution.py:336
  24.1 3.2 %col_attention.1 = bf16[8,48,128]{2,1,0:T(8,128)(2,1)} custom-call(bf16[8,144,128]{2,1,0:T(8,128)(2,1)S(1)} %all-to-all-done.refs_0_), custom_call_target="tpu_custom_call" | custom-call | flops 2000000000 | bytes 294912 | tf_op jit(solution)/shard_map/col_attention/pallas_call | solution.py:307
  27.3 3.3 %all-to-all-start.1 = ((bf16[8,48,128]{2,1,0:T(8,128)(2,1)}), bf16[8,48,128]{2,1,0:T(8,128)(2,1)S(1)}, u32[]{:S(2)}, u32[]{:S(2)}) async-start(bf16[8,48,128]{2,1,0:T(8,128)(2,1)} %col_attention.1), calls=%async_computation.1 | async-start | bytes 196608 | tf_op jit(solution)/shard_map/all_to_all | solution.py:336
  30.6 0.0 collective-permute-done.5.refs_4_
  30.7 0.0 collective-permute-done.4.refs_3_
  30.7 0.0 collective-permute-done.3.refs_2_
  30.7 0.0 copy-done.3
  30.7 1.9 %row_attention.1.partial = f32[256,384]{1,0:T(8,128)S(1)} custom-call(bf16[2,192,128]{2,1,0:T(8,128)(2,1)S(1)} %get-tuple-element.12.refs_0_, bf16[2,384,128]{2,1,0:T(8,128)(2,1)S(1)} %get-tuple-element.13.refs_1_, bf16[2,384,128]{2,1,0:T(8,128)(2,1)S(1)} %collective-permute-done.3.refs_2_, bf16[2,384,128]{2,1,0:T(8,128)(2,1)S(1)} %collective-permute-done.4.refs_3_, ...), custom_call_target="tpu_custom_call" | custom-call | flops 2000000000 | bytes 1377792 | tf_op jit(solution)/shard_map/row_attention/pallas_call | solution.py:307
  32.6 3.4 %all-to-all-done.1.arrived = bf16[8,48,128]{2,1,0:T(8,128)(2,1)S(1)} async-done(((bf16[8,48,128]{2,1,0:T(8,128)(2,1)}), bf16[8,48,128]{2,1,0:T(8,128)(2,1)S(1)}, u32[]{:S(2)}, u32[]{:S(2)}) %all-to-all-start.1) | async-done | bytes 98336 | tf_op jit(solution)/shard_map/all_to_all | solution.py:336
  36.0 1.0 %output.1 = bf16[16,16,384]{2,1,0:T(8,128)(2,1)} custom-call(bf16[8,48,128]{2,1,0:T(8,128)(2,1)S(1)} %all-to-all-done.1.arrived, f32[256,384]{1,0:T(8,128)S(1)} %row_attention.1.partial, bf16[384,384]{1,0:T(8,128)(2,1)S(1)} %copy-done.3), custom_call_target="tpu_custom_call" | custom-call | flops 100000000 | bytes 786432 | tf_op jit(solution)/shard_map/output/pallas_call | solution.py:307
  (13 shorter events, 0.1 us)
Async XLA Ops:
  0.7 3.7 %copy-start.2 = (bf16[32,32,192]{2,1,0:T(8,128)(2,1)S(1)}, bf16[32,32,192]{2,1,0:T(8,128)(2,1)}, u32[]{:S(2)}) copy-start(bf16[32,32,192]{2,1,0:T(8,128)(2,1)} %image.3) | copy-start | bytes 1179652
  0.7 5.7 %copy-start = (bf16[3,3,192,384]{3,2,1,0:T(8,128)(2,1)S(1)}, bf16[3,3,192,384]{3,2,1,0:T(8,128)(2,1)}, u32[]{:S(2)}) copy-start(bf16[3,3,192,384]{3,2,1,0:T(8,128)(2,1)} %weight.4) | copy-start | bytes 3981316
  0.7 7.7 %collective-permute-start = (bf16[32,192]{1,0:T(8,128)(2,1)S(1)}, bf16[32,192]{1,0:T(8,128)(2,1)S(1)}, u32[]{:S(2)}, u32[]{:S(2)}) collective-permute-start(bf16[32,192]{1,0:T(8,128)(2,1)S(1)} %slice_bitcast_fusion.bottom), channel_id=1, source_target_pairs={{0,4},{4,8},{8,12},{12,16},{16,20},{20,24},{24,28},{28,0},{1,5},{5... | collective-permute-start | bytes 36872 | tf_op jit(solution)/shard_map/ppermute | solution.py:369
  3.7 3.5 %collective-permute-start.2 = (bf16[16,192]{1,0:T(8,128)(2,1)S(1)}, bf16[16,192]{1,0:T(8,128)(2,1)S(1)}, u32[]{:S(2)}, u32[]{:S(2)}) collective-permute-start(bf16[16,192]{1,0:T(8,128)(2,1)S(1)} %corner.1), channel_id=1, source_target_pairs={{0,5},{1,6},{2,7},{3,0},{4,9},{5,10},{6,11},{7,4},{8,13},{9,14},{1... | collective-permute-start | bytes 18440 | tf_op jit(solution)/shard_map/ppermute | solution.py:371
  4.4 4.0 %copy-start.1 = (bf16[384,1152]{1,0:T(8,128)(2,1)S(1)}, bf16[384,1152]{1,0:T(8,128)(2,1)}, u32[]{:S(2)}) copy-start(bf16[384,1152]{1,0:T(8,128)(2,1)} %qkv.3) | copy-start | bytes 2654212
  4.4 4.0 %copy-start.4 = (f32[384]{0:T(512)S(1)}, f32[384]{0:T(512)}, u32[]{:S(2)}) copy-start(f32[384]{0:T(512)} %bias.1) | copy-start | bytes 4612
  4.4 4.0 %copy-start.5 = (f32[384]{0:T(512)S(1)}, f32[384]{0:T(512)}, u32[]{:S(2)}) copy-start(f32[384]{0:T(512)} %gain.1) | copy-start | bytes 4612
  4.5 4.0 %copy-start.6 = (f32[384]{0:T(512)S(1)}, f32[384]{0:T(512)}, u32[]{:S(2)}) copy-start(f32[384]{0:T(512)} %shift.1) | copy-start | bytes 4612
  4.5 4.0 %copy-start.7 = (f32[384]{0:T(512)S(1)}, f32[384]{0:T(512)}, u32[]{:S(2)}) copy-start(f32[384]{0:T(512)} %gain2.1) | copy-start | bytes 4612
  4.5 4.0 %copy-start.8 = (f32[384]{0:T(512)S(1)}, f32[384]{0:T(512)}, u32[]{:S(2)}) copy-start(f32[384]{0:T(512)} %shift2.1) | copy-start | bytes 4612
  4.5 3.2 %collective-permute-start.1 = (bf16[32,192]{1,0:T(8,128)(2,1)S(1)}, bf16[32,192]{1,0:T(8,128)(2,1)S(1)}, u32[]{:S(2)}, u32[]{:S(2)}) collective-permute-start(bf16[32,192]{1,0:T(8,128)(2,1)S(1)} %edge.1), channel_id=1, source_target_pairs={{0,1},{1,2},{2,3},{3,0},{4,5},{5,6},{6,7},{7,4},{8,9},{9,10},{10,1... | collective-permute-start | bytes 36872 | tf_op jit(solution)/shard_map/ppermute | solution.py:370
  10.3 13.7 %all-to-all-start = ((bf16[8,144,128]{2,1,0:T(8,128)(2,1)}), bf16[8,144,128]{2,1,0:T(8,128)(2,1)S(1)}, u32[]{:S(2)}, u32[]{:S(2)}) async-start(bf16[8,144,128]{2,1,0:T(8,128)(2,1)} %get-tuple-element.10), calls=%async_computation | async-start | bytes 589824 | tf_op jit(solution)/shard_map/all_to_all | solution.py:336
  15.4 15.3 %copy-start.3 = (bf16[384,384]{1,0:T(8,128)(2,1)S(1)}, bf16[384,384]{1,0:T(8,128)(2,1)}, u32[]{:S(2)}) copy-start(bf16[384,384]{1,0:T(8,128)(2,1)} %weight.5) | copy-start | bytes 884740
  15.4 15.3 %copy-start.9 = (f32[384]{0:T(512)S(1)}, f32[384]{0:T(512)}, u32[]{:S(2)}) copy-start(f32[384]{0:T(512)} %refs_7_.1) | copy-start | bytes 4612
  15.4 15.2 %collective-permute-start.5 = (bf16[2,384,128]{2,1,0:T(8,128)(2,1)S(1)}, bf16[2,384,128]{2,1,0:T(8,128)(2,1)S(1)}, u32[]{:S(2)}, u32[]{:S(2)}) collective-permute-start(bf16[2,384,128]{2,1,0:T(8,128)(2,1)S(1)} %get-tuple-element.13.refs_1_), channel_id=1, source_target_pairs={{0,1},{1,0},{2,3},{3,2},{4,5},{5,4},{6,7},{7,6},{8,9},{9,8},{10,11... | collective-permute-start | bytes 589832 | tf_op jit(solution)/shard_map/ppermute | solution.py:328
  15.5 15.1 %collective-permute-start.4 = (bf16[2,384,128]{2,1,0:T(8,128)(2,1)S(1)}, bf16[2,384,128]{2,1,0:T(8,128)(2,1)S(1)}, u32[]{:S(2)}, u32[]{:S(2)}) collective-permute-start(bf16[2,384,128]{2,1,0:T(8,128)(2,1)S(1)} %get-tuple-element.13.refs_1_), channel_id=1, source_target_pairs={{0,2},{1,3},{2,0},{3,1},{4,6},{5,7},{6,4},{7,5},{8,10},{9,11},{10,... | collective-permute-start | bytes 589832 | tf_op jit(solution)/shard_map/ppermute | solution.py:328
  18.0 12.7 %collective-permute-start.3 = (bf16[2,384,128]{2,1,0:T(8,128)(2,1)S(1)}, bf16[2,384,128]{2,1,0:T(8,128)(2,1)S(1)}, u32[]{:S(2)}, u32[]{:S(2)}) collective-permute-start(bf16[2,384,128]{2,1,0:T(8,128)(2,1)S(1)} %get-tuple-element.13.refs_1_), channel_id=1, source_target_pairs={{0,3},{1,2},{2,1},{3,0},{4,7},{5,6},{6,5},{7,4},{8,11},{9,10},{10,... | collective-permute-start | bytes 589832 | tf_op jit(solution)/shard_map/ppermute | solution.py:328
  27.3 8.7 %all-to-all-start.1 = ((bf16[8,48,128]{2,1,0:T(8,128)(2,1)}), bf16[8,48,128]{2,1,0:T(8,128)(2,1)S(1)}, u32[]{:S(2)}, u32[]{:S(2)}) async-start(bf16[8,48,128]{2,1,0:T(8,128)(2,1)} %col_attention.1), calls=%async_computation.1 | async-start | bytes 196608 | tf_op jit(solution)/shard_map/all_to_all | solution.py:336

commit v7 on v6

--- a/solution.py
+++ b/solution.py
@@ -376,7 +376,7 @@
         shape((rows * cols, width), F32),
         (image, conv_weight),
         10**9,
-        [pltpu.VMEM((pixel_parts, in_rows + 1, in_cols + SPLIT, LANES), F32)],
+        [pltpu.VMEM((pixel_parts, in_rows + 1, in_cols + 2 * SPLIT, LANES), F32)],
     )
     stripes, across = rows // SPLIT, cols // SPLIT
     per = across * HALF // row_count
@@ -404,7 +404,7 @@
         ),
         5 * 10**8,
         [
-            pltpu.VMEM((pixel_parts, 2, max(in_rows, in_cols) + SPLIT, LANES), F32),
+            pltpu.VMEM((pixel_parts, 2, max(in_rows, in_cols) + 2 * SPLIT, LANES), F32),
             pltpu.VMEM((row_count, 3 * per * depth, lanes), BF16),
             pltpu.SemaphoreType.DMA((row_count,)),
         ],

time: 37.4 us -> 37.4 us (level)
  no operation moved by 1% of the time
where the time goes in v7:
time: 37.4 us; the launch traced here: 37 us
  starting transfers between devices  16.2 us (43%)
  waiting for transfers between devices  10.6 us (28%)
  Pallas kernels  9.18 us (25%)
  local copies, waits for them, and re-layouts  0.78 us (2%)
    all_to_all x2, waiting for transfers between devices, exchanged(): lax.all_to_all(value, axis, 0, 0, axis_index_groups=[order], tiled=True)  9.39 us
    pallas_call x8, Pallas kernels, call(): pl.pallas_call(kernel, out_shape=out_shape, in_specs=vmem(len(args)), out...  9.18 us
    all_to_all x2, starting transfers between devices, exchanged(): lax.all_to_all(value, axis, 0, 0, axis_index_groups=[order], tiled=True)  7.99 us
    ppermute x1, starting transfers between devices, on_device(): upper = lax.ppermute(bottom, 'row', down)  2.97 us
    ppermute x3, starting transfers between devices, gathered(): held.append(lax.ppermute(value, axis, pairs))  2.63 us
    ppermute x1, starting transfers between devices, on_device(): left = lax.ppermute(side, 'col', right)  1.93 us
  transfers between devices with their start and end apart: 8, of which 4 were waited for; matrix products, arithmetic and copies ran while one was open for 0% of the time, Pallas kernels for 17%

profile of v7, /device:TPU:0, one launch (start us, length us, event | category | flops | bytes accessed | tf_op | source)
XLA Modules:
  0.0 37.0 jit_solution(4376000138610120784)
XLA Ops:
  0.0 0.7 %slice_bitcast_fusion.bottom = bf16[32,192]{1,0:T(8,128)(2,1)S(1)} fusion(bf16[32,32,192]{2,1,0:T(8,128)(2,1)} %image.3), kind=kLoop, calls=%fused_computation | loop fusion | bytes 24576 | tf_op jit(solution)/shard_map/squeeze | solution.py:365
  0.7 3.0 %collective-permute-start = (bf16[32,192]{1,0:T(8,128)(2,1)S(1)}, bf16[32,192]{1,0:T(8,128)(2,1)S(1)}, u32[]{:S(2)}, u32[]{:S(2)}) collective-permute-start(bf16[32,192]{1,0:T(8,128)(2,1)S(1)} %slice_bitcast_fusion.bottom), channel_id=1, source_target_pairs={{0,4},{4,8},{8,12},{12,16},{16,20},{20,24},{24,28},{28,0},{1,5},{5... | collective-permute-start | bytes 36872 | tf_op jit(solution)/shard_map/ppermute | solution.py:369
  3.7 0.7 %collective-permute-start.2 = (bf16[16,192]{1,0:T(8,128)(2,1)S(1)}, bf16[16,192]{1,0:T(8,128)(2,1)S(1)}, u32[]{:S(2)}, u32[]{:S(2)}) collective-permute-start(bf16[16,192]{1,0:T(8,128)(2,1)S(1)} %corner.1), channel_id=1, source_target_pairs={{0,5},{1,6},{2,7},{3,0},{4,9},{5,10},{6,11},{7,4},{8,13},{9,14},{1... | collective-permute-start | bytes 18440 | tf_op jit(solution)/shard_map/ppermute | solution.py:371
  4.4 0.0 copy-done.2
  4.4 0.0 copy-start.1
  4.4 0.0 copy-start.4
  4.4 0.0 copy-start.5
  4.5 0.0 copy-start.6
  4.5 0.0 copy-start.7
  4.5 0.0 copy-start.8
  4.5 1.9 %collective-permute-start.1 = (bf16[32,192]{1,0:T(8,128)(2,1)S(1)}, bf16[32,192]{1,0:T(8,128)(2,1)S(1)}, u32[]{:S(2)}, u32[]{:S(2)}) collective-permute-start(bf16[32,192]{1,0:T(8,128)(2,1)S(1)} %edge.1), channel_id=1, source_target_pairs={{0,1},{1,2},{2,3},{3,0},{4,5},{5,6},{6,7},{7,4},{8,9},{9,10},{10,1... | collective-permute-start | bytes 36872 | tf_op jit(solution)/shard_map/ppermute | solution.py:370
  6.4 0.8 %own_tile.1.merged = f32[256,384]{1,0:T(8,128)S(1)} custom-call(bf16[32,32,192]{2,1,0:T(8,128)(2,1)S(1)} %copy-done.2, bf16[3,3,192,384]{3,2,1,0:T(8,128)(2,1)S(1)} %copy-done), custom_call_target="tpu_custom_call" | custom-call | flops 1000000000 | bytes 1720320 | tf_op jit(solution)/shard_map/own_tile/pallas_call | solution.py:307
  7.2 0.0 collective-permute-done.2.corner
  7.2 0.5 %collective-permute-done.1.left = bf16[32,192]{1,0:T(8,128)(2,1)S(1)} collective-permute-done((bf16[32,192]{1,0:T(8,128)(2,1)S(1)}, bf16[32,192]{1,0:T(8,128)(2,1)S(1)}, u32[]{:S(2)}, u32[]{:S(2)}) %collective-permute-start.1) | collective-permute-done | bytes 12320 | tf_op jit(solution)/shard_map/ppermute | solution.py:370
  7.7 0.7 %collective-permute-done.upper = bf16[32,192]{1,0:T(8,128)(2,1)S(1)} collective-permute-done((bf16[32,192]{1,0:T(8,128)(2,1)S(1)}, bf16[32,192]{1,0:T(8,128)(2,1)S(1)}, u32[]{:S(2)}, u32[]{:S(2)}) %collective-permute-start) | collective-permute-done | bytes 12320 | tf_op jit(solution)/shard_map/ppermute | solution.py:369
  8.5 1.8 %merge.1 = (bf16[256,384]{1,0:T(8,128)(2,1)S(1)}, bf16[256,384]{1,0:T(8,128)(2,1)S(1)}, bf16[8,144,128]{2,1,0:T(8,128)(2,1)}) custom-call(f32[256,384]{1,0:T(8,128)S(1)} %own_tile.1.merged, bf16[32,192]{1,0:T(8,128)(2,1)S(1)} %collective-permute-done.upper, bf16[32,192]{1,0:T(8,128)(2,1)S(1)} %collective-permute-done.1.left, ...), custom_call_target="tpu_custom_call" | custom-call | flops 500000000 | bytes 2643456 | tf_op jit(solution)/shard_map/merge/pallas_call | solution.py:307
  10.3 4.7 %all-to-all-start = ((bf16[8,144,128]{2,1,0:T(8,128)(2,1)}), bf16[8,144,128]{2,1,0:T(8,128)(2,1)S(1)}, u32[]{:S(2)}, u32[]{:S(2)}) async-start(bf16[8,144,128]{2,1,0:T(8,128)(2,1)} %get-tuple-element.10), calls=%async_computation | async-start | bytes 589824 | tf_op jit(solution)/shard_map/all_to_all | solution.py:336
  15.0 0.4 %row_qkv.1 = (bf16[2,192,128]{2,1,0:T(8,128)(2,1)S(1)}, bf16[2,384,128]{2,1,0:T(8,128)(2,1)S(1)}) custom-call(bf16[256,384]{1,0:T(8,128)(2,1)S(1)} %get-tuple-element.11.normed, bf16[384,1152]{1,0:T(8,128)(2,1)S(1)} %copy-done.1), custom_call_target="tpu_custom_call" | custom-call | flops 300000000 | bytes 1081344 | tf_op jit(solution)/shard_map/row_qkv/pallas_call | solution.py:307
  15.4 0.0 copy-start.3
  15.4 0.0 copy-start.9
  15.4 0.1 collective-permute-start.5
  15.5 2.5 %collective-permute-start.4 = (bf16[2,384,128]{2,1,0:T(8,128)(2,1)S(1)}, bf16[2,384,128]{2,1,0:T(8,128)(2,1)S(1)}, u32[]{:S(2)}, u32[]{:S(2)}) collective-permute-start(bf16[2,384,128]{2,1,0:T(8,128)(2,1)S(1)} %get-tuple-element.13.refs_1_), channel_id=1, source_target_pairs={{0,2},{1,3},{2,0},{3,1},{4,6},{5,7},{6,4},{7,5},{8,10},{9,11},{10,... | collective-permute-start | bytes 589832 | tf_op jit(solution)/shard_map/ppermute | solution.py:328
  18.0 0.1 collective-permute-start.3
  18.1 6.0 %all-to-all-done.refs_0_ = bf16[8,144,128]{2,1,0:T(8,128)(2,1)S(1)} async-done(((bf16[8,144,128]{2,1,0:T(8,128)(2,1)}), bf16[8,144,128]{2,1,0:T(8,128)(2,1)S(1)}, u32[]{:S(2)}, u32[]{:S(2)}) %all-to-all-start) | async-done | bytes 294944 | tf_op jit(solution)/shard_map/all_to_all | solution.py:336
  24.1 3.2 %col_attention.1 = bf16[8,48,128]{2,1,0:T(8,128)(2,1)} custom-call(bf16[8,144,128]{2,1,0:T(8,128)(2,1)S(1)} %all-to-all-done.refs_0_), custom_call_target="tpu_custom_call" | custom-call | flops 2000000000 | bytes 294912 | tf_op jit(solution)/shard_map/col_attention/pallas_call | solution.py:307
  27.3 3.3 %all-to-all-start.1 = ((bf16[8,48,128]{2,1,0:T(8,128)(2,1)}), bf16[8,48,128]{2,1,0:T(8,128)(2,1)S(1)}, u32[]{:S(2)}, u32[]{:S(2)}) async-start(bf16[8,48,128]{2,1,0:T(8,128)(2,1)} %col_attention.1), calls=%async_computation.1 | async-start | bytes 196608 | tf_op jit(solution)/shard_map/all_to_all | solution.py:336
  30.6 0.0 collective-permute-done.5.refs_4_
  30.7 0.0 collective-permute-done.4.refs_3_
  30.7 0.0 collective-permute-done.3.refs_2_
  30.7 1.9 %row_attention.1.partial = f32[256,384]{1,0:T(8,128)S(1)} custom-call(bf16[2,192,128]{2,1,0:T(8,128)(2,1)S(1)} %get-tuple-element.12.refs_0_, bf16[2,384,128]{2,1,0:T(8,128)(2,1)S(1)} %get-tuple-element.13.refs_1_, bf16[2,384,128]{2,1,0:T(8,128)(2,1)S(1)} %collective-permute-done.3.refs_2_, bf16[2,384,128]{2,1,0:T(8,128)(2,1)S(1)} %collective-permute-done.4.refs_3_, ...), custom_call_target="tpu_custom_call" | custom-call | flops 2000000000 | bytes 1377792 | tf_op jit(solution)/shard_map/row_attention/pallas_call | solution.py:307
  32.6 3.4 %all-to-all-done.1.arrived = bf16[8,48,128]{2,1,0:T(8,128)(2,1)S(1)} async-done(((bf16[8,48,128]{2,1,0:T(8,128)(2,1)}), bf16[8,48,128]{2,1,0:T(8,128)(2,1)S(1)}, u32[]{:S(2)}, u32[]{:S(2)}) %all-to-all-start.1) | async-done | bytes 98336 | tf_op jit(solution)/shard_map/all_to_all | solution.py:336
  36.0 1.0 %output.1 = bf16[16,16,384]{2,1,0:T(8,128)(2,1)} custom-call(bf16[8,48,128]{2,1,0:T(8,128)(2,1)S(1)} %all-to-all-done.1.arrived, f32[256,384]{1,0:T(8,128)S(1)} %row_attention.1.partial, bf16[384,384]{1,0:T(8,128)(2,1)S(1)} %copy-done.3), custom_call_target="tpu_custom_call" | custom-call | flops 100000000 | bytes 786432 | tf_op jit(solution)/shard_map/output/pallas_call | solution.py:307
  (13 shorter events, 0.1 us)
Async XLA Ops:
  0.7 3.7 %copy-start.2 = (bf16[32,32,192]{2,1,0:T(8,128)(2,1)S(1)}, bf16[32,32,192]{2,1,0:T(8,128)(2,1)}, u32[]{:S(2)}) copy-start(bf16[32,32,192]{2,1,0:T(8,128)(2,1)} %image.3) | copy-start | bytes 1179652
  0.7 5.7 %copy-start = (bf16[3,3,192,384]{3,2,1,0:T(8,128)(2,1)S(1)}, bf16[3,3,192,384]{3,2,1,0:T(8,128)(2,1)}, u32[]{:S(2)}) copy-start(bf16[3,3,192,384]{3,2,1,0:T(8,128)(2,1)} %weight.4) | copy-start | bytes 3981316
  0.7 7.7 %collective-permute-start = (bf16[32,192]{1,0:T(8,128)(2,1)S(1)}, bf16[32,192]{1,0:T(8,128)(2,1)S(1)}, u32[]{:S(2)}, u32[]{:S(2)}) collective-permute-start(bf16[32,192]{1,0:T(8,128)(2,1)S(1)} %slice_bitcast_fusion.bottom), channel_id=1, source_target_pairs={{0,4},{4,8},{8,12},{12,16},{16,20},{20,24},{24,28},{28,0},{1,5},{5... | collective-permute-start | bytes 36872 | tf_op jit(solution)/shard_map/ppermute | solution.py:369
  3.7 3.5 %collective-permute-start.2 = (bf16[16,192]{1,0:T(8,128)(2,1)S(1)}, bf16[16,192]{1,0:T(8,128)(2,1)S(1)}, u32[]{:S(2)}, u32[]{:S(2)}) collective-permute-start(bf16[16,192]{1,0:T(8,128)(2,1)S(1)} %corner.1), channel_id=1, source_target_pairs={{0,5},{1,6},{2,7},{3,0},{4,9},{5,10},{6,11},{7,4},{8,13},{9,14},{1... | collective-permute-start | bytes 18440 | tf_op jit(solution)/shard_map/ppermute | solution.py:371
  4.4 4.0 %copy-start.1 = (bf16[384,1152]{1,0:T(8,128)(2,1)S(1)}, bf16[384,1152]{1,0:T(8,128)(2,1)}, u32[]{:S(2)}) copy-start(bf16[384,1152]{1,0:T(8,128)(2,1)} %qkv.3) | copy-start | bytes 2654212
  4.4 4.0 %copy-start.4 = (f32[384]{0:T(512)S(1)}, f32[384]{0:T(512)}, u32[]{:S(2)}) copy-start(f32[384]{0:T(512)} %bias.1) | copy-start | bytes 4612
  4.4 4.0 %copy-start.5 = (f32[384]{0:T(512)S(1)}, f32[384]{0:T(512)}, u32[]{:S(2)}) copy-start(f32[384]{0:T(512)} %gain.1) | copy-start | bytes 4612
  4.5 4.0 %copy-start.6 = (f32[384]{0:T(512)S(1)}, f32[384]{0:T(512)}, u32[]{:S(2)}) copy-start(f32[384]{0:T(512)} %shift.1) | copy-start | bytes 4612
  4.5 4.0 %copy-start.7 = (f32[384]{0:T(512)S(1)}, f32[384]{0:T(512)}, u32[]{:S(2)}) copy-start(f32[384]{0:T(512)} %gain2.1) | copy-start | bytes 4612
  4.5 4.0 %copy-start.8 = (f32[384]{0:T(512)S(1)}, f32[384]{0:T(512)}, u32[]{:S(2)}) copy-start(f32[384]{0:T(512)} %shift2.1) | copy-start | bytes 4612
  4.5 3.2 %collective-permute-start.1 = (bf16[32,192]{1,0:T(8,128)(2,1)S(1)}, bf16[32,192]{1,0:T(8,128)(2,1)S(1)}, u32[]{:S(2)}, u32[]{:S(2)}) collective-permute-start(bf16[32,192]{1,0:T(8,128)(2,1)S(1)} %edge.1), channel_id=1, source_target_pairs={{0,1},{1,2},{2,3},{3,0},{4,5},{5,6},{6,7},{7,4},{8,9},{9,10},{10,1... | collective-permute-start | bytes 36872 | tf_op jit(solution)/shard_map/ppermute | solution.py:370
  10.3 13.7 %all-to-all-start = ((bf16[8,144,128]{2,1,0:T(8,128)(2,1)}), bf16[8,144,128]{2,1,0:T(8,128)(2,1)S(1)}, u32[]{:S(2)}, u32[]{:S(2)}) async-start(bf16[8,144,128]{2,1,0:T(8,128)(2,1)} %get-tuple-element.10), calls=%async_computation | async-start | bytes 589824 | tf_op jit(solution)/shard_map/all_to_all | solution.py:336
  15.4 15.3 %copy-start.3 = (bf16[384,384]{1,0:T(8,128)(2,1)S(1)}, bf16[384,384]{1,0:T(8,128)(2,1)}, u32[]{:S(2)}) copy-start(bf16[384,384]{1,0:T(8,128)(2,1)} %weight.5) | copy-start | bytes 884740
  15.4 15.3 %copy-start.9 = (f32[384]{0:T(512)S(1)}, f32[384]{0:T(512)}, u32[]{:S(2)}) copy-start(f32[384]{0:T(512)} %refs_7_.1) | copy-start | bytes 4612
  15.4 15.2 %collective-permute-start.5 = (bf16[2,384,128]{2,1,0:T(8,128)(2,1)S(1)}, bf16[2,384,128]{2,1,0:T(8,128)(2,1)S(1)}, u32[]{:S(2)}, u32[]{:S(2)}) collective-permute-start(bf16[2,384,128]{2,1,0:T(8,128)(2,1)S(1)} %get-tuple-element.13.refs_1_), channel_id=1, source_target_pairs={{0,1},{1,0},{2,3},{3,2},{4,5},{5,4},{6,7},{7,6},{8,9},{9,8},{10,11... | collective-permute-start | bytes 589832 | tf_op jit(solution)/shard_map/ppermute | solution.py:328
  15.5 15.1 %collective-permute-start.4 = (bf16[2,384,128]{2,1,0:T(8,128)(2,1)S(1)}, bf16[2,384,128]{2,1,0:T(8,128)(2,1)S(1)}, u32[]{:S(2)}, u32[]{:S(2)}) collective-permute-start(bf16[2,384,128]{2,1,0:T(8,128)(2,1)S(1)} %get-tuple-element.13.refs_1_), channel_id=1, source_target_pairs={{0,2},{1,3},{2,0},{3,1},{4,6},{5,7},{6,4},{7,5},{8,10},{9,11},{10,... | collective-permute-start | bytes 589832 | tf_op jit(solution)/shard_map/ppermute | solution.py:328
  18.0 12.7 %collective-permute-start.3 = (bf16[2,384,128]{2,1,0:T(8,128)(2,1)S(1)}, bf16[2,384,128]{2,1,0:T(8,128)(2,1)S(1)}, u32[]{:S(2)}, u32[]{:S(2)}) collective-permute-start(bf16[2,384,128]{2,1,0:T(8,128)(2,1)S(1)} %get-tuple-element.13.refs_1_), channel_id=1, source_target_pairs={{0,3},{1,2},{2,1},{3,0},{4,7},{5,6},{6,5},{7,4},{8,11},{9,10},{10,... | collective-permute-start | bytes 589832 | tf_op jit(solution)/shard_map/ppermute | solution.py:328
  27.3 8.7 %all-to-all-start.1 = ((bf16[8,48,128]{2,1,0:T(8,128)(2,1)}), bf16[8,48,128]{2,1,0:T(8,128)(2,1)S(1)}, u32[]{:S(2)}, u32[]{:S(2)}) async-start(bf16[8,48,128]{2,1,0:T(8,128)(2,1)} %col_attention.1), calls=%async_computation.1 | async-start | bytes 196608 | tf_op jit(solution)/shard_map/all_to_all | solution.py:336

commit v8 on v7

--- a/solution.py
+++ b/solution.py
@@ -57,7 +57,9 @@
     corner[...] = bottom[bottom.shape[0] - corner.shape[0] :]
 
 
-def own_kernel(image, weight, merged, pixels):
+def own_kernel(
+    image, weight, bias, gain, shift, gain2, shift2, near, top, tokens, normed, pixels
+):
     in_rows, in_cols, channels = image.shape
     rows, cols = in_rows // 2, in_cols // 2
     first = SPLIT
@@ -67,7 +69,8 @@
         pixels[part, pl.ds(1, in_rows), pl.ds(first, in_cols), pl.ds(0, size)] = image[
             :, :, pl.ds(start, size)
         ].astype(F32)
-    total = jnp.zeros((rows * cols, merged.shape[1]), F32)
+    width = weight.shape[3]
+    total = jnp.zeros((rows * cols, width), F32)
     for tap in range(3):
         lines = [
             every_second(pixels, (i,), first - 1 + tap, cols, channels).astype(BF16)
@@ -76,7 +79,21 @@
         for tap_row in range(3):
             window = jnp.concatenate(lines[tap_row : tap_row + 2 * rows - 1 : 2], 0)
             total = total + dot(window, weight[tap_row, tap])
-    merged[...] = total
+    row = lambda ref: ref[...].reshape(1, width)
+    total = (total + row(bias)).reshape(rows, cols, width)
+    near[...] = total[:, :SPLIT]
+    top[...] = total[0, SPLIT:]
+    total = jnp.concatenate(
+        [
+            total[a * SPLIT : (a + 1) * SPLIT, b * SPLIT : (b + 1) * SPLIT].reshape(SPLIT * SPLIT, width)
+            for a, b in quadrants(rows, cols)
+            if b
+        ],
+        0,
+    )
+    held = layer_norm(total, row(gain), row(shift)).astype(BF16)
+    tokens[...] = held
+    normed[...] = layer_norm(held.astype(F32), row(gain2), row(shift2)).astype(BF16)
 
 
 def kept(value, axis):
@@ -84,10 +101,10 @@
 
 
 def merge_kernel(
-    merged, upper, left, corner, weight, qkv, bias, gain, shift, gain2, shift2, tokens, normed, chunks, edges, held_chunks, sems
+    near_grid, own_top, own_tokens, own_normed, upper, left, corner, weight, qkv, gain, shift, gain2, shift2, tokens, normed, chunks, edges, held_chunks, sems
 ):
     in_rows, channels = left.shape
-    in_cols = 4 * merged.shape[0] // in_rows
+    in_cols = upper.shape[0]
     rows, cols = in_rows // 2, in_cols // 2
     width = weight.shape[3]
     depth = width // HEADS
@@ -104,22 +121,31 @@
     corner = dot(jnp.concatenate([above[0], aside[0]], 0), weight[0, 0])
     top = corner[:cols] + dot(above[1], weight[0, 1]) + dot(above[2], weight[0, 2])
     near = corner[cols:] + dot(aside[1], weight[1, 0]) + dot(aside[2], weight[2, 0])
-    grid = merged[...].reshape(rows, cols, width)
-    grid = jnp.concatenate([grid[:1] + top.reshape(1, cols, width), grid[1:]], 0)
+    grid = near_grid[...]
+    grid = jnp.concatenate([grid[:1] + top[:SPLIT].reshape(1, SPLIT, width), grid[1:]], 0)
     begin = lax.broadcasted_iota(jnp.int32, (rows, SPLIT, width), 1) == 0
-    grid = jnp.concatenate(
-        [grid[:, :SPLIT] + jnp.where(begin, near.reshape(rows, 1, width), 0.0), grid[:, SPLIT:]], 1
-    )
-    grid = jnp.concatenate(
-        [
-            grid[a * SPLIT : (a + 1) * SPLIT, b * SPLIT : (b + 1) * SPLIT].reshape(SPLIT * SPLIT, width)
-            for a, b in quadrants(rows, cols)
-        ],
-        0,
-    )
-    held = layer_norm(grid + row(bias), row(gain), row(shift)).astype(BF16)
-    tokens[...] = held
-    again = layer_norm(held.astype(F32), row(gain2), row(shift2)).astype(BF16)
+    grid = (grid + jnp.where(begin, near.reshape(rows, 1, width), 0.0)).reshape(rows * SPLIT, width)
+    grid = jnp.concatenate([grid, own_top[...] + top[SPLIT:]], 0)
+    square = SPLIT * SPLIT
+    others = cols // SPLIT - 1
+
+    def joined(mine, rest):
+        pieces = []
+        for a, b in quadrants(rows, cols):
+            if b == 0:
+                pieces.append(mine[a * square : (a + 1) * square])
+                continue
+            begin = (a * others + b - 1) * square
+            piece = rest[begin : begin + square]
+            if a == 0:
+                first_row = rows * SPLIT + (b - 1) * SPLIT
+                piece = jnp.concatenate([mine[first_row : first_row + SPLIT], piece[SPLIT:]], 0)
+            pieces.append(piece)
+        return jnp.concatenate(pieces, 0).astype(BF16)
+
+    held = layer_norm(grid, row(gain), row(shift)).astype(BF16).astype(F32)
+    tokens[...] = joined(held, own_tokens[...].astype(F32))
+    again = joined(layer_norm(held, row(gain2), row(shift2)), own_normed[...].astype(F32))
     normed[...] = again
     across = cols // SPLIT
     count = chunks.shape[0]
@@ -370,11 +396,18 @@
     left = lax.ppermute(side, "col", right)
     corner = lax.ppermute(tail, ("row", "col"), diagonal)
     pixel_parts = -(-channels // LANES)
-    merged = call(
+    norms = (merge_gain, merge_shift, norm_gain, norm_shift)
+    apart = rows * (cols - SPLIT)
+    own = call(
         own_kernel,
         "own_tile",
-        shape((rows * cols, width), F32),
-        (image, conv_weight),
+        (
+            shape((rows, SPLIT, width), F32),
+            shape((cols - SPLIT, width), F32),
+            shape((apart, width)),
+            shape((apart, width)),
+        ),
+        (image, conv_weight, conv_bias, *norms),
         10**9,
         [pltpu.VMEM((pixel_parts, in_rows + 1, in_cols + 2 * SPLIT, LANES), F32)],
     )
@@ -390,17 +423,13 @@
             shape((row_count, 3 * per * depth, lanes)),
         ),
         (
-            merged,
+            *own,
             upper,
             left,
             corner,
             conv_weight,
             qkv_weight,
-            conv_bias,
-            merge_gain,
-            merge_shift,
-            norm_gain,
-            norm_shift,
+            *norms,
         ),
         5 * 10**8,
         [

time: 37.4 us -> 37.4 us (level)
    ppermute x1, waiting for transfers between devices: 0.49 us -> 0.1 us  [on_device(): left = lax.ppermute(side, 'col', right)]
  transfers between devices with their start and end apart: 8 -> 8, of which waited for: 4 -> 4; matrix products, arithmetic and copies ran while one was open for 0% -> 0% of each run, Pallas kernels for 17% -> 18%
where the time goes in v8:
time: 37.4 us; the launch traced here: 37 us
  starting transfers between devices  16.2 us (43%)
  waiting for transfers between devices  10.3 us (28%)
  Pallas kernels  9.53 us (25%)
  local copies, waits for them, and re-layouts  0.77 us (2%)
    pallas_call x8, Pallas kernels, call(): pl.pallas_call(kernel, out_shape=out_shape, in_specs=vmem(len(args)), out...  9.53 us
    all_to_all x2, waiting for transfers between devices, exchanged(): lax.all_to_all(value, axis, 0, 0, axis_index_groups=[order], tiled=True)  9.4 us
    all_to_all x2, starting transfers between devices, exchanged(): lax.all_to_all(value, axis, 0, 0, axis_index_groups=[order], tiled=True)  7.92 us
    ppermute x1, starting transfers between devices, on_device(): upper = lax.ppermute(bottom, 'row', down)  3.02 us
    ppermute x3, starting transfers between devices, gathered(): held.append(lax.ppermute(value, axis, pairs))  2.68 us
    ppermute x1, starting transfers between devices, on_device(): left = lax.ppermute(side, 'col', right)  1.93 us
    ppermute x1, waiting for transfers between devices, on_device(): upper = lax.ppermute(bottom, 'row', down)  0.8 us
  transfers between devices with their start and end apart: 8, of which 4 were waited for; matrix products, arithmetic and copies ran while one was open for 0% of the time, Pallas kernels for 18%

profile of v8, /device:TPU:0, one launch (start us, length us, event | category | flops | bytes accessed | tf_op | source)
XLA Modules:
  0.0 37.0 jit_solution(3168755524354975339)
XLA Ops:
  0.0 0.7 %slice_bitcast_fusion.bottom = bf16[32,192]{1,0:T(8,128)(2,1)S(1)} fusion(bf16[32,32,192]{2,1,0:T(8,128)(2,1)} %image.3), kind=kLoop, calls=%fused_computation | loop fusion | bytes 24576 | tf_op jit(solution)/shard_map/squeeze | solution.py:391
  0.7 0.0 copy-start.6
  0.7 0.0 copy-start.7
  0.8 0.0 copy-start.8
  0.8 3.0 %collective-permute-start = (bf16[32,192]{1,0:T(8,128)(2,1)S(1)}, bf16[32,192]{1,0:T(8,128)(2,1)S(1)}, u32[]{:S(2)}, u32[]{:S(2)}) collective-permute-start(bf16[32,192]{1,0:T(8,128)(2,1)S(1)} %slice_bitcast_fusion.bottom), channel_id=1, source_target_pairs={{0,4},{4,8},{8,12},{12,16},{16,20},{20,24},{24,28},{28,0},{1,5},{5... | collective-permute-start | bytes 36872 | tf_op jit(solution)/shard_map/ppermute | solution.py:395
  3.8 0.7 %collective-permute-start.2 = (bf16[16,192]{1,0:T(8,128)(2,1)S(1)}, bf16[16,192]{1,0:T(8,128)(2,1)S(1)}, u32[]{:S(2)}, u32[]{:S(2)}) collective-permute-start(bf16[16,192]{1,0:T(8,128)(2,1)S(1)} %corner.1), channel_id=1, source_target_pairs={{0,5},{1,6},{2,7},{3,0},{4,9},{5,10},{6,11},{7,4},{8,13},{9,14},{1... | collective-permute-start | bytes 18440 | tf_op jit(solution)/shard_map/ppermute | solution.py:397
  4.5 0.0 copy-done.2
  4.5 0.0 copy-start.1
  4.5 1.9 %collective-permute-start.1 = (bf16[32,192]{1,0:T(8,128)(2,1)S(1)}, bf16[32,192]{1,0:T(8,128)(2,1)S(1)}, u32[]{:S(2)}, u32[]{:S(2)}) collective-permute-start(bf16[32,192]{1,0:T(8,128)(2,1)S(1)} %edge.1), channel_id=1, source_target_pairs={{0,1},{1,2},{2,3},{3,0},{4,5},{5,6},{6,7},{7,4},{8,9},{9,10},{10,1... | collective-permute-start | bytes 36872 | tf_op jit(solution)/shard_map/ppermute | solution.py:396
  6.5 0.0 copy-done
  6.5 0.0 copy-done.4
  6.5 1.1 %own_tile.1 = (f32[16,8,384]{2,1,0:T(8,128)S(1)}, f32[8,384]{1,0:T(8,128)S(1)}, bf16[128,384]{1,0:T(8,128)(2,1)S(1)}, bf16[128,384]{1,0:T(8,128)(2,1)S(1)}) custom-call(bf16[32,32,192]{2,1,0:T(8,128)(2,1)S(1)} %copy-done.2, bf16[3,3,192,384]{3,2,1,0:T(8,128)(2,1)S(1)} %copy-done, f32[384]{0:T(512)S(1)} %copy-done.8, f32[384]{0:T(512)S(1)} %copy-done.4, ...), custom_call_target="tpu_custom_call" | custom-call | flops 1000000000 | bytes 1728000 | tf_op jit(solution)/shard_map/own_tile/pallas_call | solution.py:333
  7.6 0.0 collective-permute-done.2.corner
  7.6 0.1 collective-permute-done.1.left
  7.7 0.8 %collective-permute-done.upper = bf16[32,192]{1,0:T(8,128)(2,1)S(1)} collective-permute-done((bf16[32,192]{1,0:T(8,128)(2,1)S(1)}, bf16[32,192]{1,0:T(8,128)(2,1)S(1)}, u32[]{:S(2)}, u32[]{:S(2)}) %collective-permute-start) | collective-permute-done | bytes 12320 | tf_op jit(solution)/shard_map/ppermute | solution.py:395
  8.5 1.8 %merge.1 = (bf16[256,384]{1,0:T(8,128)(2,1)S(1)}, bf16[256,384]{1,0:T(8,128)(2,1)S(1)}, bf16[8,144,128]{2,1,0:T(8,128)(2,1)}) custom-call(f32[16,8,384]{2,1,0:T(8,128)S(1)} %get-tuple-element.14.near_grid, f32[8,384]{1,0:T(8,128)S(1)} %get-tuple-element.15.own_top, bf16[128,384]{1,0:T(8,128)(2,1)S(1)} %get-tuple-element.16.own_tokens, ...), custom_call_target="tpu_custom_call" | custom-call | flops 500000000 | bytes 2654208 | tf_op jit(solution)/shard_map/merge/pallas_call | solution.py:333
  10.4 4.6 %all-to-all-start = ((bf16[8,144,128]{2,1,0:T(8,128)(2,1)}), bf16[8,144,128]{2,1,0:T(8,128)(2,1)S(1)}, u32[]{:S(2)}, u32[]{:S(2)}) async-start(bf16[8,144,128]{2,1,0:T(8,128)(2,1)} %get-tuple-element.18), calls=%async_computation | async-start | bytes 589824 | tf_op jit(solution)/shard_map/all_to_all | solution.py:362
  15.0 0.4 %row_qkv.1 = (bf16[2,192,128]{2,1,0:T(8,128)(2,1)S(1)}, bf16[2,384,128]{2,1,0:T(8,128)(2,1)S(1)}) custom-call(bf16[256,384]{1,0:T(8,128)(2,1)S(1)} %get-tuple-element.19.normed, bf16[384,1152]{1,0:T(8,128)(2,1)S(1)} %copy-done.1), custom_call_target="tpu_custom_call" | custom-call | flops 300000000 | bytes 1081344 | tf_op jit(solution)/shard_map/row_qkv/pallas_call | solution.py:333
  15.4 0.0 copy-start.3
  15.4 0.0 copy-start.9
  15.4 0.1 collective-permute-start.5
  15.5 2.5 %collective-permute-start.4 = (bf16[2,384,128]{2,1,0:T(8,128)(2,1)S(1)}, bf16[2,384,128]{2,1,0:T(8,128)(2,1)S(1)}, u32[]{:S(2)}, u32[]{:S(2)}) collective-permute-start(bf16[2,384,128]{2,1,0:T(8,128)(2,1)S(1)} %get-tuple-element.21.refs_1_), channel_id=1, source_target_pairs={{0,2},{1,3},{2,0},{3,1},{4,6},{5,7},{6,4},{7,5},{8,10},{9,11},{10,... | collective-permute-start | bytes 589832 | tf_op jit(solution)/shard_map/ppermute | solution.py:354
  18.0 0.1 collective-permute-start.3
  18.1 6.0 %all-to-all-done.refs_0_ = bf16[8,144,128]{2,1,0:T(8,128)(2,1)S(1)} async-done(((bf16[8,144,128]{2,1,0:T(8,128)(2,1)}), bf16[8,144,128]{2,1,0:T(8,128)(2,1)S(1)}, u32[]{:S(2)}, u32[]{:S(2)}) %all-to-all-start) | async-done | bytes 294944 | tf_op jit(solution)/shard_map/all_to_all | solution.py:362
  24.1 3.2 %col_attention.1 = bf16[8,48,128]{2,1,0:T(8,128)(2,1)} custom-call(bf16[8,144,128]{2,1,0:T(8,128)(2,1)S(1)} %all-to-all-done.refs_0_), custom_call_target="tpu_custom_call" | custom-call | flops 2000000000 | bytes 294912 | tf_op jit(solution)/shard_map/col_attention/pallas_call | solution.py:333
  27.4 3.3 %all-to-all-start.1 = ((bf16[8,48,128]{2,1,0:T(8,128)(2,1)}), bf16[8,48,128]{2,1,0:T(8,128)(2,1)S(1)}, u32[]{:S(2)}, u32[]{:S(2)}) async-start(bf16[8,48,128]{2,1,0:T(8,128)(2,1)} %col_attention.1), calls=%async_computation.1 | async-start | bytes 196608 | tf_op jit(solution)/shard_map/all_to_all | solution.py:362
  30.7 0.0 collective-permute-done.5.refs_4_
  30.7 0.0 collective-permute-done.4.refs_3_
  30.7 0.0 collective-permute-done.3.refs_2_
  30.7 1.9 %row_attention.1.partial = f32[256,384]{1,0:T(8,128)S(1)} custom-call(bf16[2,192,128]{2,1,0:T(8,128)(2,1)S(1)} %get-tuple-element.20.refs_0_, bf16[2,384,128]{2,1,0:T(8,128)(2,1)S(1)} %get-tuple-element.21.refs_1_, bf16[2,384,128]{2,1,0:T(8,128)(2,1)S(1)} %collective-permute-done.3.refs_2_, bf16[2,384,128]{2,1,0:T(8,128)(2,1)S(1)} %collective-permute-done.4.refs_3_, ...), custom_call_target="tpu_custom_call" | custom-call | flops 2000000000 | bytes 1377792 | tf_op jit(solution)/shard_map/row_attention/pallas_call | solution.py:333
  32.7 3.4 %all-to-all-done.1.arrived = bf16[8,48,128]{2,1,0:T(8,128)(2,1)S(1)} async-done(((bf16[8,48,128]{2,1,0:T(8,128)(2,1)}), bf16[8,48,128]{2,1,0:T(8,128)(2,1)S(1)}, u32[]{:S(2)}, u32[]{:S(2)}) %all-to-all-start.1) | async-done | bytes 98336 | tf_op jit(solution)/shard_map/all_to_all | solution.py:362
  36.1 1.0 %output.1 = bf16[16,16,384]{2,1,0:T(8,128)(2,1)} custom-call(bf16[8,48,128]{2,1,0:T(8,128)(2,1)S(1)} %all-to-all-done.1.arrived, f32[256,384]{1,0:T(8,128)S(1)} %row_attention.1.partial, bf16[384,384]{1,0:T(8,128)(2,1)S(1)} %copy-done.3), custom_call_target="tpu_custom_call" | custom-call | flops 100000000 | bytes 786432 | tf_op jit(solution)/shard_map/output/pallas_call | solution.py:333
  (13 shorter events, 0.1 us)
Async XLA Ops:
  0.7 3.8 %copy-start.2 = (bf16[32,32,192]{2,1,0:T(8,128)(2,1)S(1)}, bf16[32,32,192]{2,1,0:T(8,128)(2,1)}, u32[]{:S(2)}) copy-start(bf16[32,32,192]{2,1,0:T(8,128)(2,1)} %image.3) | copy-start | bytes 1179652
  0.7 5.7 %copy-start = (bf16[3,3,192,384]{3,2,1,0:T(8,128)(2,1)S(1)}, bf16[3,3,192,384]{3,2,1,0:T(8,128)(2,1)}, u32[]{:S(2)}) copy-start(bf16[3,3,192,384]{3,2,1,0:T(8,128)(2,1)} %weight.4) | copy-start | bytes 3981316
  0.7 5.7 %copy-start.4 = (f32[384]{0:T(512)S(1)}, f32[384]{0:T(512)}, u32[]{:S(2)}) copy-start(f32[384]{0:T(512)} %gain.3) | copy-start | bytes 4612
  0.7 5.7 %copy-start.5 = (f32[384]{0:T(512)S(1)}, f32[384]{0:T(512)}, u32[]{:S(2)}) copy-start(f32[384]{0:T(512)} %shift.3) | copy-start | bytes 4612
  0.7 5.7 %copy-start.6 = (f32[384]{0:T(512)S(1)}, f32[384]{0:T(512)}, u32[]{:S(2)}) copy-start(f32[384]{0:T(512)} %gain2.3) | copy-start | bytes 4612
  0.7 5.7 %copy-start.7 = (f32[384]{0:T(512)S(1)}, f32[384]{0:T(512)}, u32[]{:S(2)}) copy-start(f32[384]{0:T(512)} %shift2.3) | copy-start | bytes 4612
  0.8 5.7 %copy-start.8 = (f32[384]{0:T(512)S(1)}, f32[384]{0:T(512)}, u32[]{:S(2)}) copy-start(f32[384]{0:T(512)} %bias.1) | copy-start | bytes 4612
  0.8 7.8 %collective-permute-start = (bf16[32,192]{1,0:T(8,128)(2,1)S(1)}, bf16[32,192]{1,0:T(8,128)(2,1)S(1)}, u32[]{:S(2)}, u32[]{:S(2)}) collective-permute-start(bf16[32,192]{1,0:T(8,128)(2,1)S(1)} %slice_bitcast_fusion.bottom), channel_id=1, source_target_pairs={{0,4},{4,8},{8,12},{12,16},{16,20},{20,24},{24,28},{28,0},{1,5},{5... | collective-permute-start | bytes 36872 | tf_op jit(solution)/shard_map/ppermute | solution.py:395
  3.8 3.8 %collective-permute-start.2 = (bf16[16,192]{1,0:T(8,128)(2,1)S(1)}, bf16[16,192]{1,0:T(8,128)(2,1)S(1)}, u32[]{:S(2)}, u32[]{:S(2)}) collective-permute-start(bf16[16,192]{1,0:T(8,128)(2,1)S(1)} %corner.1), channel_id=1, source_target_pairs={{0,5},{1,6},{2,7},{3,0},{4,9},{5,10},{6,11},{7,4},{8,13},{9,14},{1... | collective-permute-start | bytes 18440 | tf_op jit(solution)/shard_map/ppermute | solution.py:397
  4.5 4.0 %copy-start.1 = (bf16[384,1152]{1,0:T(8,128)(2,1)S(1)}, bf16[384,1152]{1,0:T(8,128)(2,1)}, u32[]{:S(2)}) copy-start(bf16[384,1152]{1,0:T(8,128)(2,1)} %qkv.3) | copy-start | bytes 2654212
  4.5 3.2 %collective-permute-start.1 = (bf16[32,192]{1,0:T(8,128)(2,1)S(1)}, bf16[32,192]{1,0:T(8,128)(2,1)S(1)}, u32[]{:S(2)}, u32[]{:S(2)}) collective-permute-start(bf16[32,192]{1,0:T(8,128)(2,1)S(1)} %edge.1), channel_id=1, source_target_pairs={{0,1},{1,2},{2,3},{3,0},{4,5},{5,6},{6,7},{7,4},{8,9},{9,10},{10,1... | collective-permute-start | bytes 36872 | tf_op jit(solution)/shard_map/ppermute | solution.py:396
  10.4 13.7 %all-to-all-start = ((bf16[8,144,128]{2,1,0:T(8,128)(2,1)}), bf16[8,144,128]{2,1,0:T(8,128)(2,1)S(1)}, u32[]{:S(2)}, u32[]{:S(2)}) async-start(bf16[8,144,128]{2,1,0:T(8,128)(2,1)} %get-tuple-element.18), calls=%async_computation | async-start | bytes 589824 | tf_op jit(solution)/shard_map/all_to_all | solution.py:362
  15.4 15.3 %copy-start.3 = (bf16[384,384]{1,0:T(8,128)(2,1)S(1)}, bf16[384,384]{1,0:T(8,128)(2,1)}, u32[]{:S(2)}) copy-start(bf16[384,384]{1,0:T(8,128)(2,1)} %weight.5) | copy-start | bytes 884740
  15.4 15.3 %copy-start.9 = (f32[384]{0:T(512)S(1)}, f32[384]{0:T(512)}, u32[]{:S(2)}) copy-start(f32[384]{0:T(512)} %refs_7_.1) | copy-start | bytes 4612
  15.4 15.3 %collective-permute-start.5 = (bf16[2,384,128]{2,1,0:T(8,128)(2,1)S(1)}, bf16[2,384,128]{2,1,0:T(8,128)(2,1)S(1)}, u32[]{:S(2)}, u32[]{:S(2)}) collective-permute-start(bf16[2,384,128]{2,1,0:T(8,128)(2,1)S(1)} %get-tuple-element.21.refs_1_), channel_id=1, source_target_pairs={{0,1},{1,0},{2,3},{3,2},{4,5},{5,4},{6,7},{7,6},{8,9},{9,8},{10,11... | collective-permute-start | bytes 589832 | tf_op jit(solution)/shard_map/ppermute | solution.py:354
  15.5 15.2 %collective-permute-start.4 = (bf16[2,384,128]{2,1,0:T(8,128)(2,1)S(1)}, bf16[2,384,128]{2,1,0:T(8,128)(2,1)S(1)}, u32[]{:S(2)}, u32[]{:S(2)}) collective-permute-start(bf16[2,384,128]{2,1,0:T(8,128)(2,1)S(1)} %get-tuple-element.21.refs_1_), channel_id=1, source_target_pairs={{0,2},{1,3},{2,0},{3,1},{4,6},{5,7},{6,4},{7,5},{8,10},{9,11},{10,... | collective-permute-start | bytes 589832 | tf_op jit(solution)/shard_map/ppermute | solution.py:354
  18.0 12.7 %collective-permute-start.3 = (bf16[2,384,128]{2,1,0:T(8,128)(2,1)S(1)}, bf16[2,384,128]{2,1,0:T(8,128)(2,1)S(1)}, u32[]{:S(2)}, u32[]{:S(2)}) collective-permute-start(bf16[2,384,128]{2,1,0:T(8,128)(2,1)S(1)} %get-tuple-element.21.refs_1_), channel_id=1, source_target_pairs={{0,3},{1,2},{2,1},{3,0},{4,7},{5,6},{6,5},{7,4},{8,11},{9,10},{10,... | collective-permute-start | bytes 589832 | tf_op jit(solution)/shard_map/ppermute | solution.py:354
  27.4 8.7 %all-to-all-start.1 = ((bf16[8,48,128]{2,1,0:T(8,128)(2,1)}), bf16[8,48,128]{2,1,0:T(8,128)(2,1)S(1)}, u32[]{:S(2)}, u32[]{:S(2)}) async-start(bf16[8,48,128]{2,1,0:T(8,128)(2,1)} %col_attention.1), calls=%async_computation.1 | async-start | bytes 196608 | tf_op jit(solution)/shard_map/all_to_all | solution.py:362

commit v9 on v7

--- a/solution.py
+++ b/solution.py
@@ -126,17 +126,23 @@
     per = across * HALF // count
     square = SPLIT * SPLIT
     copies = [pltpu.make_async_copy(held_chunks.at[k], chunks.at[k], sems.at[k]) for k in range(count)]
+    mine = jnp.concatenate(
+        [
+            again[(a * across + b) * square : (a * across + b + 1) * square]
+            for b in range(across)
+            for a in range(rows // SPLIT)
+        ],
+        0,
+    )
+    turned = []
+    for kind in range(3):
+        begin = kind * width + width // 2
+        base = begin // LANES * LANES
+        wide = dot(mine, qkv[:, base : (kind + 1) * width])
+        turned.append(wide.T[begin - base :])
+    length = rows * SPLIT
     for b in range(across):
-        mine = [
-            again[(a * across + b) * square : (a * across + b + 1) * square] for a in range(rows // SPLIT)
-        ]
-        mine = jnp.concatenate(mine, 0)
-        lines = []
-        for kind in range(3):
-            begin = kind * width + width // 2
-            base = begin // LANES * LANES
-            wide = dot(mine, qkv[:, base : (kind + 1) * width])
-            lines.append(wide.T[begin - base :])
+        lines = [kind[:, b * length : (b + 1) * length] for kind in turned]
         for item in range(b * HALF, (b + 1) * HALF, per):
             low = (item - b * HALF) * depth
             held_chunks[item // per] = jnp.concatenate(
@@ -232,7 +238,7 @@
                 done[k] = both[:, k * length - begin : (k + 1) * length - begin]
                 copies[k].start()
 
-    ahead_of([(begin, h) for begin in range(0, count * length, block) for h in range(per)], score, finish, 4)
+    ahead_of([(begin, h) for begin in range(0, count * length, block) for h in range(per)], score, finish, 6)
     for copy in copies:
         copy.wait()
 
@@ -285,14 +291,15 @@
     square = SPLIT * SPLIT
     each = count // across
     blocks = {}
+    lines = [
+        jnp.concatenate([arrived[b * each + k].astype(F32) for k in range(each)], 0) for b in range(across)
+    ]
+    mixed = dot(jnp.concatenate(lines, 1).T.astype(BF16), weight[half:])
     for b in range(across):
-        lines = jnp.concatenate([arrived[b * each + k].astype(F32) for k in range(each)], 0)
-        mixed = dot(lines.T.astype(BF16), weight[half:])
         for a in range(down):
             here = pl.ds((a * across + b) * square, square)
-            blocks[a, b] = (partial[here] + mixed[a * square : (a + 1) * square]).reshape(
-                SPLIT, SPLIT, width
-            )
+            begin = (b * down + a) * square
+            blocks[a, b] = (partial[here] + mixed[begin : begin + square]).reshape(SPLIT, SPLIT, width)
     for a in range(down):
         output[a * SPLIT : (a + 1) * SPLIT] = jnp.concatenate(
             [blocks[a, b] for b in range(across)], 1

time: 37.4 us -> 37.4 us (level)
  no operation moved by 1% of the time
where the time goes in v9:
time: 37.4 us; the launch traced here: 37 us
  starting transfers between devices  16.2 us (43%)
  waiting for transfers between devices  10.6 us (28%)
  Pallas kernels  9.24 us (25%)
  local copies, waits for them, and re-layouts  0.78 us (2%)
    all_to_all x2, waiting for transfers between devices, exchanged(): lax.all_to_all(value, axis, 0, 0, axis_index_groups=[order], tiled=True)  9.39 us
    pallas_call x8, Pallas kernels, call(): pl.pallas_call(kernel, out_shape=out_shape, in_specs=vmem(len(args)), out...  9.24 us
    all_to_all x2, starting transfers between devices, exchanged(): lax.all_to_all(value, axis, 0, 0, axis_index_groups=[order], tiled=True)  7.99 us
    ppermute x1, starting transfers between devices, on_device(): upper = lax.ppermute(bottom, 'row', down)  2.97 us
    ppermute x3, starting transfers between devices, gathered(): held.append(lax.ppermute(value, axis, pairs))  2.63 us
    ppermute x1, starting transfers between devices, on_device(): left = lax.ppermute(side, 'col', right)  1.93 us
  transfers between devices with their start and end apart: 8, of which 4 were waited for; matrix products, arithmetic and copies ran while one was open for 0% of the time, Pallas kernels for 17%

profile of v9, /device:TPU:0, one launch (start us, length us, event | category | flops | bytes accessed | tf_op | source)
XLA Modules:
  0.0 37.0 jit_solution(16346387154051903904)
XLA Ops:
  0.0 0.7 %slice_bitcast_fusion.bottom = bf16[32,192]{1,0:T(8,128)(2,1)S(1)} fusion(bf16[32,32,192]{2,1,0:T(8,128)(2,1)} %image.3), kind=kLoop, calls=%fused_computation | loop fusion | bytes 24576 | tf_op jit(solution)/shard_map/squeeze | solution.py:372
  0.7 3.0 %collective-permute-start = (bf16[32,192]{1,0:T(8,128)(2,1)S(1)}, bf16[32,192]{1,0:T(8,128)(2,1)S(1)}, u32[]{:S(2)}, u32[]{:S(2)}) collective-permute-start(bf16[32,192]{1,0:T(8,128)(2,1)S(1)} %slice_bitcast_fusion.bottom), channel_id=1, source_target_pairs={{0,4},{4,8},{8,12},{12,16},{16,20},{20,24},{24,28},{28,0},{1,5},{5... | collective-permute-start | bytes 36872 | tf_op jit(solution)/shard_map/ppermute | solution.py:376
  3.7 0.7 %collective-permute-start.2 = (bf16[16,192]{1,0:T(8,128)(2,1)S(1)}, bf16[16,192]{1,0:T(8,128)(2,1)S(1)}, u32[]{:S(2)}, u32[]{:S(2)}) collective-permute-start(bf16[16,192]{1,0:T(8,128)(2,1)S(1)} %corner.1), channel_id=1, source_target_pairs={{0,5},{1,6},{2,7},{3,0},{4,9},{5,10},{6,11},{7,4},{8,13},{9,14},{1... | collective-permute-start | bytes 18440 | tf_op jit(solution)/shard_map/ppermute | solution.py:378
  4.4 0.0 copy-start.1
  4.4 0.0 copy-start.4
  4.4 0.0 copy-start.5
  4.5 0.0 copy-start.6
  4.5 0.0 copy-start.7
  4.5 0.0 copy-start.8
  4.5 1.9 %collective-permute-start.1 = (bf16[32,192]{1,0:T(8,128)(2,1)S(1)}, bf16[32,192]{1,0:T(8,128)(2,1)S(1)}, u32[]{:S(2)}, u32[]{:S(2)}) collective-permute-start(bf16[32,192]{1,0:T(8,128)(2,1)S(1)} %edge.1), channel_id=1, source_target_pairs={{0,1},{1,2},{2,3},{3,0},{4,5},{5,6},{6,7},{7,4},{8,9},{9,10},{10,1... | collective-permute-start | bytes 36872 | tf_op jit(solution)/shard_map/ppermute | solution.py:377
  6.4 0.8 %own_tile.1.merged = f32[256,384]{1,0:T(8,128)S(1)} custom-call(bf16[32,32,192]{2,1,0:T(8,128)(2,1)S(1)} %copy-done.2, bf16[3,3,192,384]{3,2,1,0:T(8,128)(2,1)S(1)} %copy-done), custom_call_target="tpu_custom_call" | custom-call | flops 1000000000 | bytes 1720320 | tf_op jit(solution)/shard_map/own_tile/pallas_call | solution.py:314
  7.2 0.0 collective-permute-done.2.corner
  7.2 0.5 %collective-permute-done.1.left = bf16[32,192]{1,0:T(8,128)(2,1)S(1)} collective-permute-done((bf16[32,192]{1,0:T(8,128)(2,1)S(1)}, bf16[32,192]{1,0:T(8,128)(2,1)S(1)}, u32[]{:S(2)}, u32[]{:S(2)}) %collective-permute-start.1) | collective-permute-done | bytes 12320 | tf_op jit(solution)/shard_map/ppermute | solution.py:377
  7.7 0.7 %collective-permute-done.upper = bf16[32,192]{1,0:T(8,128)(2,1)S(1)} collective-permute-done((bf16[32,192]{1,0:T(8,128)(2,1)S(1)}, bf16[32,192]{1,0:T(8,128)(2,1)S(1)}, u32[]{:S(2)}, u32[]{:S(2)}) %collective-permute-start) | collective-permute-done | bytes 12320 | tf_op jit(solution)/shard_map/ppermute | solution.py:376
  8.5 1.8 %merge.1 = (bf16[256,384]{1,0:T(8,128)(2,1)S(1)}, bf16[256,384]{1,0:T(8,128)(2,1)S(1)}, bf16[8,144,128]{2,1,0:T(8,128)(2,1)}) custom-call(f32[256,384]{1,0:T(8,128)S(1)} %own_tile.1.merged, bf16[32,192]{1,0:T(8,128)(2,1)S(1)} %collective-permute-done.upper, bf16[32,192]{1,0:T(8,128)(2,1)S(1)} %collective-permute-done.1.left, ...), custom_call_target="tpu_custom_call" | custom-call | flops 500000000 | bytes 2643456 | tf_op jit(solution)/shard_map/merge/pallas_call | solution.py:314
  10.3 4.7 %all-to-all-start = ((bf16[8,144,128]{2,1,0:T(8,128)(2,1)}), bf16[8,144,128]{2,1,0:T(8,128)(2,1)S(1)}, u32[]{:S(2)}, u32[]{:S(2)}) async-start(bf16[8,144,128]{2,1,0:T(8,128)(2,1)} %get-tuple-element.10), calls=%async_computation | async-start | bytes 589824 | tf_op jit(solution)/shard_map/all_to_all | solution.py:343
  15.0 0.4 %row_qkv.1 = (bf16[2,192,128]{2,1,0:T(8,128)(2,1)S(1)}, bf16[2,384,128]{2,1,0:T(8,128)(2,1)S(1)}) custom-call(bf16[256,384]{1,0:T(8,128)(2,1)S(1)} %get-tuple-element.11.normed, bf16[384,1152]{1,0:T(8,128)(2,1)S(1)} %copy-done.1), custom_call_target="tpu_custom_call" | custom-call | flops 300000000 | bytes 1081344 | tf_op jit(solution)/shard_map/row_qkv/pallas_call | solution.py:314
  15.4 0.0 copy-start.3
  15.5 0.0 copy-start.9
  15.5 0.1 collective-permute-start.5
  15.6 2.5 %collective-permute-start.4 = (bf16[2,384,128]{2,1,0:T(8,128)(2,1)S(1)}, bf16[2,384,128]{2,1,0:T(8,128)(2,1)S(1)}, u32[]{:S(2)}, u32[]{:S(2)}) collective-permute-start(bf16[2,384,128]{2,1,0:T(8,128)(2,1)S(1)} %get-tuple-element.13.refs_1_), channel_id=1, source_target_pairs={{0,2},{1,3},{2,0},{3,1},{4,6},{5,7},{6,4},{7,5},{8,10},{9,11},{10,... | collective-permute-start | bytes 589832 | tf_op jit(solution)/shard_map/ppermute | solution.py:335
  18.0 0.1 collective-permute-start.3
  18.1 6.0 %all-to-all-done.refs_0_ = bf16[8,144,128]{2,1,0:T(8,128)(2,1)S(1)} async-done(((bf16[8,144,128]{2,1,0:T(8,128)(2,1)}), bf16[8,144,128]{2,1,0:T(8,128)(2,1)S(1)}, u32[]{:S(2)}, u32[]{:S(2)}) %all-to-all-start) | async-done | bytes 294944 | tf_op jit(solution)/shard_map/all_to_all | solution.py:343
  24.1 3.3 %col_attention.1 = bf16[8,48,128]{2,1,0:T(8,128)(2,1)} custom-call(bf16[8,144,128]{2,1,0:T(8,128)(2,1)S(1)} %all-to-all-done.refs_0_), custom_call_target="tpu_custom_call" | custom-call | flops 2000000000 | bytes 294912 | tf_op jit(solution)/shard_map/col_attention/pallas_call | solution.py:314
  27.4 3.3 %all-to-all-start.1 = ((bf16[8,48,128]{2,1,0:T(8,128)(2,1)}), bf16[8,48,128]{2,1,0:T(8,128)(2,1)S(1)}, u32[]{:S(2)}, u32[]{:S(2)}) async-start(bf16[8,48,128]{2,1,0:T(8,128)(2,1)} %col_attention.1), calls=%async_computation.1 | async-start | bytes 196608 | tf_op jit(solution)/shard_map/all_to_all | solution.py:343
  30.7 0.0 collective-permute-done.5.refs_4_
  30.7 0.0 collective-permute-done.4.refs_3_
  30.7 0.0 collective-permute-done.3.refs_2_
  30.7 0.0 copy-done.3
  30.8 1.9 %row_attention.1.partial = f32[256,384]{1,0:T(8,128)S(1)} custom-call(bf16[2,192,128]{2,1,0:T(8,128)(2,1)S(1)} %get-tuple-element.12.refs_0_, bf16[2,384,128]{2,1,0:T(8,128)(2,1)S(1)} %get-tuple-element.13.refs_1_, bf16[2,384,128]{2,1,0:T(8,128)(2,1)S(1)} %collective-permute-done.3.refs_2_, bf16[2,384,128]{2,1,0:T(8,128)(2,1)S(1)} %collective-permute-done.4.refs_3_, ...), custom_call_target="tpu_custom_call" | custom-call | flops 2000000000 | bytes 1377792 | tf_op jit(solution)/shard_map/row_attention/pallas_call | solution.py:314
  32.7 3.4 %all-to-all-done.1.arrived = bf16[8,48,128]{2,1,0:T(8,128)(2,1)S(1)} async-done(((bf16[8,48,128]{2,1,0:T(8,128)(2,1)}), bf16[8,48,128]{2,1,0:T(8,128)(2,1)S(1)}, u32[]{:S(2)}, u32[]{:S(2)}) %all-to-all-start.1) | async-done | bytes 98336 | tf_op jit(solution)/shard_map/all_to_all | solution.py:343
  36.1 1.0 %output.1 = bf16[16,16,384]{2,1,0:T(8,128)(2,1)} custom-call(bf16[8,48,128]{2,1,0:T(8,128)(2,1)S(1)} %all-to-all-done.1.arrived, f32[256,384]{1,0:T(8,128)S(1)} %row_attention.1.partial, bf16[384,384]{1,0:T(8,128)(2,1)S(1)} %copy-done.3), custom_call_target="tpu_custom_call" | custom-call | flops 100000000 | bytes 786432 | tf_op jit(solution)/shard_map/output/pallas_call | solution.py:314
  (13 shorter events, 0.1 us)
Async XLA Ops:
  0.7 3.7 %copy-start.2 = (bf16[32,32,192]{2,1,0:T(8,128)(2,1)S(1)}, bf16[32,32,192]{2,1,0:T(8,128)(2,1)}, u32[]{:S(2)}) copy-start(bf16[32,32,192]{2,1,0:T(8,128)(2,1)} %image.3) | copy-start | bytes 1179652
  0.7 5.7 %copy-start = (bf16[3,3,192,384]{3,2,1,0:T(8,128)(2,1)S(1)}, bf16[3,3,192,384]{3,2,1,0:T(8,128)(2,1)}, u32[]{:S(2)}) copy-start(bf16[3,3,192,384]{3,2,1,0:T(8,128)(2,1)} %weight.4) | copy-start | bytes 3981316
  0.7 7.7 %collective-permute-start = (bf16[32,192]{1,0:T(8,128)(2,1)S(1)}, bf16[32,192]{1,0:T(8,128)(2,1)S(1)}, u32[]{:S(2)}, u32[]{:S(2)}) collective-permute-start(bf16[32,192]{1,0:T(8,128)(2,1)S(1)} %slice_bitcast_fusion.bottom), channel_id=1, source_target_pairs={{0,4},{4,8},{8,12},{12,16},{16,20},{20,24},{24,28},{28,0},{1,5},{5... | collective-permute-start | bytes 36872 | tf_op jit(solution)/shard_map/ppermute | solution.py:376
  3.7 3.5 %collective-permute-start.2 = (bf16[16,192]{1,0:T(8,128)(2,1)S(1)}, bf16[16,192]{1,0:T(8,128)(2,1)S(1)}, u32[]{:S(2)}, u32[]{:S(2)}) collective-permute-start(bf16[16,192]{1,0:T(8,128)(2,1)S(1)} %corner.1), channel_id=1, source_target_pairs={{0,5},{1,6},{2,7},{3,0},{4,9},{5,10},{6,11},{7,4},{8,13},{9,14},{1... | collective-permute-start | bytes 18440 | tf_op jit(solution)/shard_map/ppermute | solution.py:378
  4.4 4.0 %copy-start.1 = (bf16[384,1152]{1,0:T(8,128)(2,1)S(1)}, bf16[384,1152]{1,0:T(8,128)(2,1)}, u32[]{:S(2)}) copy-start(bf16[384,1152]{1,0:T(8,128)(2,1)} %qkv.3) | copy-start | bytes 2654212
  4.4 4.0 %copy-start.4 = (f32[384]{0:T(512)S(1)}, f32[384]{0:T(512)}, u32[]{:S(2)}) copy-start(f32[384]{0:T(512)} %bias.1) | copy-start | bytes 4612
  4.4 4.0 %copy-start.5 = (f32[384]{0:T(512)S(1)}, f32[384]{0:T(512)}, u32[]{:S(2)}) copy-start(f32[384]{0:T(512)} %gain.1) | copy-start | bytes 4612
  4.5 4.0 %copy-start.6 = (f32[384]{0:T(512)S(1)}, f32[384]{0:T(512)}, u32[]{:S(2)}) copy-start(f32[384]{0:T(512)} %shift.1) | copy-start | bytes 4612
  4.5 4.0 %copy-start.7 = (f32[384]{0:T(512)S(1)}, f32[384]{0:T(512)}, u32[]{:S(2)}) copy-start(f32[384]{0:T(512)} %gain2.1) | copy-start | bytes 4612
  4.5 4.0 %copy-start.8 = (f32[384]{0:T(512)S(1)}, f32[384]{0:T(512)}, u32[]{:S(2)}) copy-start(f32[384]{0:T(512)} %shift2.1) | copy-start | bytes 4612
  4.5 3.2 %collective-permute-start.1 = (bf16[32,192]{1,0:T(8,128)(2,1)S(1)}, bf16[32,192]{1,0:T(8,128)(2,1)S(1)}, u32[]{:S(2)}, u32[]{:S(2)}) collective-permute-start(bf16[32,192]{1,0:T(8,128)(2,1)S(1)} %edge.1), channel_id=1, source_target_pairs={{0,1},{1,2},{2,3},{3,0},{4,5},{5,6},{6,7},{7,4},{8,9},{9,10},{10,1... | collective-permute-start | bytes 36872 | tf_op jit(solution)/shard_map/ppermute | solution.py:377
  10.3 13.7 %all-to-all-start = ((bf16[8,144,128]{2,1,0:T(8,128)(2,1)}), bf16[8,144,128]{2,1,0:T(8,128)(2,1)S(1)}, u32[]{:S(2)}, u32[]{:S(2)}) async-start(bf16[8,144,128]{2,1,0:T(8,128)(2,1)} %get-tuple-element.10), calls=%async_computation | async-start | bytes 589824 | tf_op jit(solution)/shard_map/all_to_all | solution.py:343
  15.4 15.3 %copy-start.3 = (bf16[384,384]{1,0:T(8,128)(2,1)S(1)}, bf16[384,384]{1,0:T(8,128)(2,1)}, u32[]{:S(2)}) copy-start(bf16[384,384]{1,0:T(8,128)(2,1)} %weight.5) | copy-start | bytes 884740
  15.5 15.3 %copy-start.9 = (f32[384]{0:T(512)S(1)}, f32[384]{0:T(512)}, u32[]{:S(2)}) copy-start(f32[384]{0:T(512)} %refs_7_.1) | copy-start | bytes 4612
  15.5 15.2 %collective-permute-start.5 = (bf16[2,384,128]{2,1,0:T(8,128)(2,1)S(1)}, bf16[2,384,128]{2,1,0:T(8,128)(2,1)S(1)}, u32[]{:S(2)}, u32[]{:S(2)}) collective-permute-start(bf16[2,384,128]{2,1,0:T(8,128)(2,1)S(1)} %get-tuple-element.13.refs_1_), channel_id=1, source_target_pairs={{0,1},{1,0},{2,3},{3,2},{4,5},{5,4},{6,7},{7,6},{8,9},{9,8},{10,11... | collective-permute-start | bytes 589832 | tf_op jit(solution)/shard_map/ppermute | solution.py:335
  15.6 15.2 %collective-permute-start.4 = (bf16[2,384,128]{2,1,0:T(8,128)(2,1)S(1)}, bf16[2,384,128]{2,1,0:T(8,128)(2,1)S(1)}, u32[]{:S(2)}, u32[]{:S(2)}) collective-permute-start(bf16[2,384,128]{2,1,0:T(8,128)(2,1)S(1)} %get-tuple-element.13.refs_1_), channel_id=1, source_target_pairs={{0,2},{1,3},{2,0},{3,1},{4,6},{5,7},{6,4},{7,5},{8,10},{9,11},{10,... | collective-permute-start | bytes 589832 | tf_op jit(solution)/shard_map/ppermute | solution.py:335
  18.0 12.7 %collective-permute-start.3 = (bf16[2,384,128]{2,1,0:T(8,128)(2,1)S(1)}, bf16[2,384,128]{2,1,0:T(8,128)(2,1)S(1)}, u32[]{:S(2)}, u32[]{:S(2)}) collective-permute-start(bf16[2,384,128]{2,1,0:T(8,128)(2,1)S(1)} %get-tuple-element.13.refs_1_), channel_id=1, source_target_pairs={{0,3},{1,2},{2,1},{3,0},{4,7},{5,6},{6,5},{7,4},{8,11},{9,10},{10,... | collective-permute-start | bytes 589832 | tf_op jit(solution)/shard_map/ppermute | solution.py:335
  27.4 8.7 %all-to-all-start.1 = ((bf16[8,48,128]{2,1,0:T(8,128)(2,1)}), bf16[8,48,128]{2,1,0:T(8,128)(2,1)S(1)}, u32[]{:S(2)}, u32[]{:S(2)}) async-start(bf16[8,48,128]{2,1,0:T(8,128)(2,1)} %col_attention.1), calls=%async_computation.1 | async-start | bytes 196608 | tf_op jit(solution)/shard_map/all_to_all | solution.py:343

commit v10 on v7

--- a/solution.py
+++ b/solution.py
@@ -232,7 +232,7 @@
                 done[k] = both[:, k * length - begin : (k + 1) * length - begin]
                 copies[k].start()
 
-    ahead_of([(begin, h) for begin in range(0, count * length, block) for h in range(per)], score, finish, 4)
+    ahead_of([(begin, h) for begin in range(0, count * length, block) for h in range(per)], score, finish, 6)
     for copy in copies:
         copy.wait()
 

time: 37.4 us -> 37.4 us (level)
  no operation moved by 1% of the time
where the time goes in v10:
time: 37.4 us; the launch traced here: 37 us
  starting transfers between devices  16.2 us (43%)
  waiting for transfers between devices  10.6 us (28%)
  Pallas kernels  9.22 us (25%)
  local copies, waits for them, and re-layouts  0.78 us (2%)
    all_to_all x2, waiting for transfers between devices, exchanged(): lax.all_to_all(value, axis, 0, 0, axis_index_groups=[order], tiled=True)  9.39 us
    pallas_call x8, Pallas kernels, call(): pl.pallas_call(kernel, out_shape=out_shape, in_specs=vmem(len(args)), out...  9.22 us
    all_to_all x2, starting transfers between devices, exchanged(): lax.all_to_all(value, axis, 0, 0, axis_index_groups=[order], tiled=True)  7.99 us
    ppermute x1, starting transfers between devices, on_device(): upper = lax.ppermute(bottom, 'row', down)  2.97 us
    ppermute x3, starting transfers between devices, gathered(): held.append(lax.ppermute(value, axis, pairs))  2.63 us
    ppermute x1, starting transfers between devices, on_device(): left = lax.ppermute(side, 'col', right)  1.93 us
  transfers between devices with their start and end apart: 8, of which 4 were waited for; matrix products, arithmetic and copies ran while one was open for 0% of the time, Pallas kernels for 17%

profile of v10, /device:TPU:0, one launch (start us, length us, event | category | flops | bytes accessed | tf_op | source)
XLA Modules:
  0.0 37.0 jit_solution(3913413905771164704)
XLA Ops:
  0.0 0.7 %slice_bitcast_fusion.bottom = bf16[32,192]{1,0:T(8,128)(2,1)S(1)} fusion(bf16[32,32,192]{2,1,0:T(8,128)(2,1)} %image.3), kind=kLoop, calls=%fused_computation | loop fusion | bytes 24576 | tf_op jit(solution)/shard_map/squeeze | solution.py:365
  0.7 3.0 %collective-permute-start = (bf16[32,192]{1,0:T(8,128)(2,1)S(1)}, bf16[32,192]{1,0:T(8,128)(2,1)S(1)}, u32[]{:S(2)}, u32[]{:S(2)}) collective-permute-start(bf16[32,192]{1,0:T(8,128)(2,1)S(1)} %slice_bitcast_fusion.bottom), channel_id=1, source_target_pairs={{0,4},{4,8},{8,12},{12,16},{16,20},{20,24},{24,28},{28,0},{1,5},{5... | collective-permute-start | bytes 36872 | tf_op jit(solution)/shard_map/ppermute | solution.py:369
  3.7 0.7 %collective-permute-start.2 = (bf16[16,192]{1,0:T(8,128)(2,1)S(1)}, bf16[16,192]{1,0:T(8,128)(2,1)S(1)}, u32[]{:S(2)}, u32[]{:S(2)}) collective-permute-start(bf16[16,192]{1,0:T(8,128)(2,1)S(1)} %corner.1), channel_id=1, source_target_pairs={{0,5},{1,6},{2,7},{3,0},{4,9},{5,10},{6,11},{7,4},{8,13},{9,14},{1... | collective-permute-start | bytes 18440 | tf_op jit(solution)/shard_map/ppermute | solution.py:371
  4.4 0.0 copy-done.2
  4.4 0.0 copy-start.1
  4.4 0.0 copy-start.4
  4.4 0.0 copy-start.5
  4.5 0.0 copy-start.6
  4.5 0.0 copy-start.7
  4.5 0.0 copy-start.8
  4.5 1.9 %collective-permute-start.1 = (bf16[32,192]{1,0:T(8,128)(2,1)S(1)}, bf16[32,192]{1,0:T(8,128)(2,1)S(1)}, u32[]{:S(2)}, u32[]{:S(2)}) collective-permute-start(bf16[32,192]{1,0:T(8,128)(2,1)S(1)} %edge.1), channel_id=1, source_target_pairs={{0,1},{1,2},{2,3},{3,0},{4,5},{5,6},{6,7},{7,4},{8,9},{9,10},{10,1... | collective-permute-start | bytes 36872 | tf_op jit(solution)/shard_map/ppermute | solution.py:370
  6.4 0.8 %own_tile.1.merged = f32[256,384]{1,0:T(8,128)S(1)} custom-call(bf16[32,32,192]{2,1,0:T(8,128)(2,1)S(1)} %copy-done.2, bf16[3,3,192,384]{3,2,1,0:T(8,128)(2,1)S(1)} %copy-done), custom_call_target="tpu_custom_call" | custom-call | flops 1000000000 | bytes 1720320 | tf_op jit(solution)/shard_map/own_tile/pallas_call | solution.py:307
  7.2 0.0 collective-permute-done.2.corner
  7.2 0.5 %collective-permute-done.1.left = bf16[32,192]{1,0:T(8,128)(2,1)S(1)} collective-permute-done((bf16[32,192]{1,0:T(8,128)(2,1)S(1)}, bf16[32,192]{1,0:T(8,128)(2,1)S(1)}, u32[]{:S(2)}, u32[]{:S(2)}) %collective-permute-start.1) | collective-permute-done | bytes 12320 | tf_op jit(solution)/shard_map/ppermute | solution.py:370
  7.7 0.7 %collective-permute-done.upper = bf16[32,192]{1,0:T(8,128)(2,1)S(1)} collective-permute-done((bf16[32,192]{1,0:T(8,128)(2,1)S(1)}, bf16[32,192]{1,0:T(8,128)(2,1)S(1)}, u32[]{:S(2)}, u32[]{:S(2)}) %collective-permute-start) | collective-permute-done | bytes 12320 | tf_op jit(solution)/shard_map/ppermute | solution.py:369
  8.5 1.8 %merge.1 = (bf16[256,384]{1,0:T(8,128)(2,1)S(1)}, bf16[256,384]{1,0:T(8,128)(2,1)S(1)}, bf16[8,144,128]{2,1,0:T(8,128)(2,1)}) custom-call(f32[256,384]{1,0:T(8,128)S(1)} %own_tile.1.merged, bf16[32,192]{1,0:T(8,128)(2,1)S(1)} %collective-permute-done.upper, bf16[32,192]{1,0:T(8,128)(2,1)S(1)} %collective-permute-done.1.left, ...), custom_call_target="tpu_custom_call" | custom-call | flops 500000000 | bytes 2643456 | tf_op jit(solution)/shard_map/merge/pallas_call | solution.py:307
  10.3 4.7 %all-to-all-start = ((bf16[8,144,128]{2,1,0:T(8,128)(2,1)}), bf16[8,144,128]{2,1,0:T(8,128)(2,1)S(1)}, u32[]{:S(2)}, u32[]{:S(2)}) async-start(bf16[8,144,128]{2,1,0:T(8,128)(2,1)} %get-tuple-element.10), calls=%async_computation | async-start | bytes 589824 | tf_op jit(solution)/shard_map/all_to_all | solution.py:336
  15.0 0.4 %row_qkv.1 = (bf16[2,192,128]{2,1,0:T(8,128)(2,1)S(1)}, bf16[2,384,128]{2,1,0:T(8,128)(2,1)S(1)}) custom-call(bf16[256,384]{1,0:T(8,128)(2,1)S(1)} %get-tuple-element.11.normed, bf16[384,1152]{1,0:T(8,128)(2,1)S(1)} %copy-done.1), custom_call_target="tpu_custom_call" | custom-call | flops 300000000 | bytes 1081344 | tf_op jit(solution)/shard_map/row_qkv/pallas_call | solution.py:307
  15.4 0.0 copy-start.3
  15.4 0.0 copy-start.9
  15.4 0.1 collective-permute-start.5
  15.5 2.5 %collective-permute-start.4 = (bf16[2,384,128]{2,1,0:T(8,128)(2,1)S(1)}, bf16[2,384,128]{2,1,0:T(8,128)(2,1)S(1)}, u32[]{:S(2)}, u32[]{:S(2)}) collective-permute-start(bf16[2,384,128]{2,1,0:T(8,128)(2,1)S(1)} %get-tuple-element.13.refs_1_), channel_id=1, source_target_pairs={{0,2},{1,3},{2,0},{3,1},{4,6},{5,7},{6,4},{7,5},{8,10},{9,11},{10,... | collective-permute-start | bytes 589832 | tf_op jit(solution)/shard_map/ppermute | solution.py:328
  18.0 0.1 collective-permute-start.3
  18.1 6.0 %all-to-all-done.refs_0_ = bf16[8,144,128]{2,1,0:T(8,128)(2,1)S(1)} async-done(((bf16[8,144,128]{2,1,0:T(8,128)(2,1)}), bf16[8,144,128]{2,1,0:T(8,128)(2,1)S(1)}, u32[]{:S(2)}, u32[]{:S(2)}) %all-to-all-start) | async-done | bytes 294944 | tf_op jit(solution)/shard_map/all_to_all | solution.py:336
  24.1 3.3 %col_attention.1 = bf16[8,48,128]{2,1,0:T(8,128)(2,1)} custom-call(bf16[8,144,128]{2,1,0:T(8,128)(2,1)S(1)} %all-to-all-done.refs_0_), custom_call_target="tpu_custom_call" | custom-call | flops 2000000000 | bytes 294912 | tf_op jit(solution)/shard_map/col_attention/pallas_call | solution.py:307
  27.3 3.3 %all-to-all-start.1 = ((bf16[8,48,128]{2,1,0:T(8,128)(2,1)}), bf16[8,48,128]{2,1,0:T(8,128)(2,1)S(1)}, u32[]{:S(2)}, u32[]{:S(2)}) async-start(bf16[8,48,128]{2,1,0:T(8,128)(2,1)} %col_attention.1), calls=%async_computation.1 | async-start | bytes 196608 | tf_op jit(solution)/shard_map/all_to_all | solution.py:336
  30.7 0.0 collective-permute-done.5.refs_4_
  30.7 0.0 collective-permute-done.4.refs_3_
  30.7 0.0 collective-permute-done.3.refs_2_
  30.7 1.9 %row_attention.1.partial = f32[256,384]{1,0:T(8,128)S(1)} custom-call(bf16[2,192,128]{2,1,0:T(8,128)(2,1)S(1)} %get-tuple-element.12.refs_0_, bf16[2,384,128]{2,1,0:T(8,128)(2,1)S(1)} %get-tuple-element.13.refs_1_, bf16[2,384,128]{2,1,0:T(8,128)(2,1)S(1)} %collective-permute-done.3.refs_2_, bf16[2,384,128]{2,1,0:T(8,128)(2,1)S(1)} %collective-permute-done.4.refs_3_, ...), custom_call_target="tpu_custom_call" | custom-call | flops 2000000000 | bytes 1377792 | tf_op jit(solution)/shard_map/row_attention/pallas_call | solution.py:307
  32.6 3.4 %all-to-all-done.1.arrived = bf16[8,48,128]{2,1,0:T(8,128)(2,1)S(1)} async-done(((bf16[8,48,128]{2,1,0:T(8,128)(2,1)}), bf16[8,48,128]{2,1,0:T(8,128)(2,1)S(1)}, u32[]{:S(2)}, u32[]{:S(2)}) %all-to-all-start.1) | async-done | bytes 98336 | tf_op jit(solution)/shard_map/all_to_all | solution.py:336
  36.1 1.0 %output.1 = bf16[16,16,384]{2,1,0:T(8,128)(2,1)} custom-call(bf16[8,48,128]{2,1,0:T(8,128)(2,1)S(1)} %all-to-all-done.1.arrived, f32[256,384]{1,0:T(8,128)S(1)} %row_attention.1.partial, bf16[384,384]{1,0:T(8,128)(2,1)S(1)} %copy-done.3), custom_call_target="tpu_custom_call" | custom-call | flops 100000000 | bytes 786432 | tf_op jit(solution)/shard_map/output/pallas_call | solution.py:307
  (13 shorter events, 0.1 us)
Async XLA Ops:
  0.7 3.7 %copy-start.2 = (bf16[32,32,192]{2,1,0:T(8,128)(2,1)S(1)}, bf16[32,32,192]{2,1,0:T(8,128)(2,1)}, u32[]{:S(2)}) copy-start(bf16[32,32,192]{2,1,0:T(8,128)(2,1)} %image.3) | copy-start | bytes 1179652
  0.7 5.7 %copy-start = (bf16[3,3,192,384]{3,2,1,0:T(8,128)(2,1)S(1)}, bf16[3,3,192,384]{3,2,1,0:T(8,128)(2,1)}, u32[]{:S(2)}) copy-start(bf16[3,3,192,384]{3,2,1,0:T(8,128)(2,1)} %weight.4) | copy-start | bytes 3981316
  0.7 7.7 %collective-permute-start = (bf16[32,192]{1,0:T(8,128)(2,1)S(1)}, bf16[32,192]{1,0:T(8,128)(2,1)S(1)}, u32[]{:S(2)}, u32[]{:S(2)}) collective-permute-start(bf16[32,192]{1,0:T(8,128)(2,1)S(1)} %slice_bitcast_fusion.bottom), channel_id=1, source_target_pairs={{0,4},{4,8},{8,12},{12,16},{16,20},{20,24},{24,28},{28,0},{1,5},{5... | collective-permute-start | bytes 36872 | tf_op jit(solution)/shard_map/ppermute | solution.py:369
  3.7 3.5 %collective-permute-start.2 = (bf16[16,192]{1,0:T(8,128)(2,1)S(1)}, bf16[16,192]{1,0:T(8,128)(2,1)S(1)}, u32[]{:S(2)}, u32[]{:S(2)}) collective-permute-start(bf16[16,192]{1,0:T(8,128)(2,1)S(1)} %corner.1), channel_id=1, source_target_pairs={{0,5},{1,6},{2,7},{3,0},{4,9},{5,10},{6,11},{7,4},{8,13},{9,14},{1... | collective-permute-start | bytes 18440 | tf_op jit(solution)/shard_map/ppermute | solution.py:371
  4.4 4.0 %copy-start.1 = (bf16[384,1152]{1,0:T(8,128)(2,1)S(1)}, bf16[384,1152]{1,0:T(8,128)(2,1)}, u32[]{:S(2)}) copy-start(bf16[384,1152]{1,0:T(8,128)(2,1)} %qkv.3) | copy-start | bytes 2654212
  4.4 4.0 %copy-start.4 = (f32[384]{0:T(512)S(1)}, f32[384]{0:T(512)}, u32[]{:S(2)}) copy-start(f32[384]{0:T(512)} %bias.1) | copy-start | bytes 4612
  4.4 4.0 %copy-start.5 = (f32[384]{0:T(512)S(1)}, f32[384]{0:T(512)}, u32[]{:S(2)}) copy-start(f32[384]{0:T(512)} %gain.1) | copy-start | bytes 4612
  4.5 4.0 %copy-start.6 = (f32[384]{0:T(512)S(1)}, f32[384]{0:T(512)}, u32[]{:S(2)}) copy-start(f32[384]{0:T(512)} %shift.1) | copy-start | bytes 4612
  4.5 4.0 %copy-start.7 = (f32[384]{0:T(512)S(1)}, f32[384]{0:T(512)}, u32[]{:S(2)}) copy-start(f32[384]{0:T(512)} %gain2.1) | copy-start | bytes 4612
  4.5 4.0 %copy-start.8 = (f32[384]{0:T(512)S(1)}, f32[384]{0:T(512)}, u32[]{:S(2)}) copy-start(f32[384]{0:T(512)} %shift2.1) | copy-start | bytes 4612
  4.5 3.2 %collective-permute-start.1 = (bf16[32,192]{1,0:T(8,128)(2,1)S(1)}, bf16[32,192]{1,0:T(8,128)(2,1)S(1)}, u32[]{:S(2)}, u32[]{:S(2)}) collective-permute-start(bf16[32,192]{1,0:T(8,128)(2,1)S(1)} %edge.1), channel_id=1, source_target_pairs={{0,1},{1,2},{2,3},{3,0},{4,5},{5,6},{6,7},{7,4},{8,9},{9,10},{10,1... | collective-permute-start | bytes 36872 | tf_op jit(solution)/shard_map/ppermute | solution.py:370
  10.3 13.7 %all-to-all-start = ((bf16[8,144,128]{2,1,0:T(8,128)(2,1)}), bf16[8,144,128]{2,1,0:T(8,128)(2,1)S(1)}, u32[]{:S(2)}, u32[]{:S(2)}) async-start(bf16[8,144,128]{2,1,0:T(8,128)(2,1)} %get-tuple-element.10), calls=%async_computation | async-start | bytes 589824 | tf_op jit(solution)/shard_map/all_to_all | solution.py:336
  15.4 15.3 %copy-start.3 = (bf16[384,384]{1,0:T(8,128)(2,1)S(1)}, bf16[384,384]{1,0:T(8,128)(2,1)}, u32[]{:S(2)}) copy-start(bf16[384,384]{1,0:T(8,128)(2,1)} %weight.5) | copy-start | bytes 884740
  15.4 15.3 %copy-start.9 = (f32[384]{0:T(512)S(1)}, f32[384]{0:T(512)}, u32[]{:S(2)}) copy-start(f32[384]{0:T(512)} %refs_7_.1) | copy-start | bytes 4612
  15.4 15.2 %collective-permute-start.5 = (bf16[2,384,128]{2,1,0:T(8,128)(2,1)S(1)}, bf16[2,384,128]{2,1,0:T(8,128)(2,1)S(1)}, u32[]{:S(2)}, u32[]{:S(2)}) collective-permute-start(bf16[2,384,128]{2,1,0:T(8,128)(2,1)S(1)} %get-tuple-element.13.refs_1_), channel_id=1, source_target_pairs={{0,1},{1,0},{2,3},{3,2},{4,5},{5,4},{6,7},{7,6},{8,9},{9,8},{10,11... | collective-permute-start | bytes 589832 | tf_op jit(solution)/shard_map/ppermute | solution.py:328
  15.5 15.2 %collective-permute-start.4 = (bf16[2,384,128]{2,1,0:T(8,128)(2,1)S(1)}, bf16[2,384,128]{2,1,0:T(8,128)(2,1)S(1)}, u32[]{:S(2)}, u32[]{:S(2)}) collective-permute-start(bf16[2,384,128]{2,1,0:T(8,128)(2,1)S(1)} %get-tuple-element.13.refs_1_), channel_id=1, source_target_pairs={{0,2},{1,3},{2,0},{3,1},{4,6},{5,7},{6,4},{7,5},{8,10},{9,11},{10,... | collective-permute-start | bytes 589832 | tf_op jit(solution)/shard_map/ppermute | solution.py:328
  18.0 12.7 %collective-permute-start.3 = (bf16[2,384,128]{2,1,0:T(8,128)(2,1)S(1)}, bf16[2,384,128]{2,1,0:T(8,128)(2,1)S(1)}, u32[]{:S(2)}, u32[]{:S(2)}) collective-permute-start(bf16[2,384,128]{2,1,0:T(8,128)(2,1)S(1)} %get-tuple-element.13.refs_1_), channel_id=1, source_target_pairs={{0,3},{1,2},{2,1},{3,0},{4,7},{5,6},{6,5},{7,4},{8,11},{9,10},{10,... | collective-permute-start | bytes 589832 | tf_op jit(solution)/shard_map/ppermute | solution.py:328
  27.3 8.7 %all-to-all-start.1 = ((bf16[8,48,128]{2,1,0:T(8,128)(2,1)}), bf16[8,48,128]{2,1,0:T(8,128)(2,1)S(1)}, u32[]{:S(2)}, u32[]{:S(2)}) async-start(bf16[8,48,128]{2,1,0:T(8,128)(2,1)} %col_attention.1), calls=%async_computation.1 | async-start | bytes 196608 | tf_op jit(solution)/shard_map/all_to_all | solution.py:336
